TPU v7x, 32 devices: a whole 2x2x4 slice. The times are simulated.
32 devices in a mesh: groups: 2 (over y), nodes: 4 (over z), cols: 4 (over x, core).
Axes of the slice: x: 2, y: 2, z: 4, core: 2. Of those that a mesh axis runs over, the one named last changes fastest.
Arguments:
- forces: float32 [256, 16384], P('cols', ('groups', 'nodes')), parts along dimension 1, may hold values from -150 to 150
- couplings: float32 [3, 16384], P(None, ('groups', 'nodes')), parts along dimension 1, may hold values from 0.1 to 1
- ground: float32 [16384], P(('groups', 'nodes')), parts along dimension 0, may hold values from 0.3 to 3
- precond: float32 [128, 128, 128], P(('groups', 'nodes')), parts along dimension 0, may hold values from -3 to 3, as said below
Outputs:
- modes: float32 [256, 16384], P('cols', ('groups', 'nodes')), parts along dimension 1
- tile: float32 [512, 256], P(('groups', 'cols'), 'nodes'), parts along dimension 0
There are 2 independent parts, one for each index of `groups`. A program takes and returns all parts, laid end to end along the dimension named above; each array names one. Nothing has to cross between parts.
Inputs may be any that keep to these rules, and one draw needn't show every extreme that they name: `precond`: each matrix is symmetric positive definite.
All inputs are finite; a program needn't handle non-finite values.
Results may differ from a plain program's by a relative error of at most 0.0003.
Values sent between devices are 32-bit elements; how exact they have to be, the bound alone decides.
No kernel may reach another device: no remote copies, remote signals or barrier semaphores. Data moves between devices by JAX's collectives and lax.ppermute only.
A program may use at most 64 MiB of HBM per device.

v0:
```python
import jax
import jax.numpy as jnp
from jax import lax
from jax.sharding import PartitionSpec as P

GRID_X = 32
GRID_Y = 32
ITERS = 2


def padded_2(block, sides, width):
    for axis, dim in sides:
        count = lax.axis_size(axis)
        forward = [(i, i + 1) for i in range(count - 1)]
        backward = [(target, source) for source, target in forward]
        low = lax.ppermute(
            lax.slice_in_dim(block, block.shape[dim] - width, None, axis=dim), axis, forward
        )
        high = lax.ppermute(lax.slice_in_dim(block, 0, width, axis=dim), axis, backward)
        block = jnp.concatenate([low, block, high], axis=dim)
    return block


def passed_along(block, axis, distance):
    devices = range(lax.axis_size(axis))
    route = [(i - distance, i) for i in devices if i - distance in devices]
    return lax.ppermute(block, axis, route)


def precondition(resid, precond):
    count = resid.shape[0]
    blocks = resid.reshape(count, precond.shape[0], precond.shape[1])
    out = jnp.einsum("cbj,bij->cbi", blocks, precond, precision=lax.Precision.HIGHEST)
    return out.reshape(count, -1)


def edge_masks(total):
    index = jnp.arange(total, dtype=jnp.int32)
    mask_x = (index % GRID_X < GRID_X - 1).astype(jnp.float32)
    mask_y = (index // GRID_X % GRID_Y < GRID_Y - 1).astype(jnp.float32)
    return (mask_x, mask_y)


def stiffness(field, springs, downs, diag, offsets):
    plane = offsets[2]
    length = field.shape[1]
    padded = padded_2(field, (("nodes", 1),), plane)
    result = diag * field
    for spring, down, step in zip(springs, downs, offsets):
        later = padded[:, plane + step : plane + step + length]
        earlier = padded[:, plane - step : plane - step + length]
        result = result - spring * later - down * earlier
    return result


def on_device(forces, couplings, ground, precond):
    plane = GRID_X * GRID_Y
    offsets = [1, GRID_X, plane]
    length = couplings.shape[1]
    left_part = passed_along(couplings[:, length - plane :], "nodes", 1)
    extended = jnp.concatenate([left_part, couplings], axis=1)
    ext_x, ext_y = edge_masks(length + plane)
    extended = jnp.stack([extended[0] * ext_x, extended[1] * ext_y, extended[2]])
    springs = []
    downs = []
    diag = ground
    for row in range(3):
        step = offsets[row]
        spring = extended[row, plane:]
        down = extended[row, plane - step : plane - step + length]
        diag = diag + (spring + down)
        springs.append(spring)
        downs.append(down)

    def apply_stiff(field):
        return stiffness(field, springs, downs, diag, offsets)

    modes = jnp.zeros_like(forces)
    resid = forces

    def resid_dot(left, right):
        return lax.psum(jnp.sum(left * right, axis=1), "nodes")

    zvals = precondition(resid, precond)
    direction = zvals
    rz_now = resid_dot(resid, zvals)
    for step in range(ITERS):
        image = apply_stiff(direction)
        curve = lax.psum(jnp.sum(direction * image, axis=1), "nodes")
        alpha = rz_now / curve
        modes = modes + alpha[:, None] * direction
        resid = resid - alpha[:, None] * image
        if step + 1 < ITERS:
            zvals = precondition(resid, precond)
            rz_new = resid_dot(resid, zvals)
            direction = zvals + (rz_new / rz_now)[:, None] * direction
            rz_now = rz_new
    images = apply_stiff(modes)
    scale = 1.0 / (length * lax.axis_size("nodes"))
    partial_tile = (
        jnp.dot(
            modes,
            lax.all_gather(images, "cols", axis=0, tiled=True).T,
            precision=lax.Precision.HIGHEST,
        )
        * scale
    )
    tile = lax.psum_scatter(partial_tile, "nodes", scatter_dimension=1, tiled=True)
    return (modes, tile)


def solution(mesh):
    in_specs = (
        P("cols", ("groups", "nodes")),
        P(None, ("groups", "nodes")),
        P(("groups", "nodes")),
        P(("groups", "nodes"), None, None),
    )
    out_specs = (P("cols", ("groups", "nodes")), P(("groups", "cols"), "nodes"))
    return jax.shard_map(
        on_device, mesh=mesh, in_specs=in_specs, out_specs=out_specs, check_vma=False
    )
```

profile of v0, /device:TPU:0, one launch (start us, length us, event | category | flops | bytes accessed | tf_op | source)
XLA Modules:
  0.0 139.4 jit_solution(247614671201840220)
XLA Ops:
  7.2 0.8 slice.121
  8.0 5.0 %collective-permute-start = (f32[3,1024]{1,0:T(4,128)S(1)}, f32[3,1024]{1,0:T(4,128)S(1)}, u32[]{:S(2)}, u32[]{:S(2)}) collective-permute-start(f32[3,1024]{1,0:T(4,128)S(1)} %slice.121), channel_id=1, source_target_pairs={{0,4},{4,8},{8,12},{1,5},{5,9},{9,13},{2,6},{6,10},{10,14},{3,7},{... | collective-permute-start | bytes 36872 | tf_op jit(solution)/shard_map/ppermute | solution.py:27
  13.1 3.2 %convolution_bitcast_fusion.1 = f32[16,8,8,128]{3,2,1,0:T(8,128)S(1)} fusion(f32[16,128,128]{2,1,0:T(8,128)S(1)} %copy-done, f32[64,2048]{1,0:T(8,128)} %param.4), kind=kOutput, calls=%fused_computation.1 | convolution fusion | flops 201326592 | bytes 2097152 | tf_op jit(solution)/shard_map/cbj,bij->cbi/dot_general | solution.py:33
  16.4 3.6 %collective-permute-start.2 = (f32[64,1024]{1,0:T(8,128)S(1)}, f32[64,1024]{1,0:T(8,128)S(1)}, u32[]{:S(2)}, u32[]{:S(2)}) collective-permute-start(f32[64,1024]{1,0:T(8,128)S(1)} %get-tuple-element.12), channel_id=1, source_target_pairs={{0,4},{4,8},{8,12},{1,5},{5,9},{9,13},{2,6},{6,10},{10,14},{3,7},{... | collective-permute-start | bytes 786440 | tf_op jit(solution)/shard_map/ppermute | solution.py:16
  20.0 1.3 collective-permute-start.1
  21.4 0.1 fusion.51
  21.6 3.7 %collective-permute-done.2 = f32[64,1024]{1,0:T(8,128)S(1)} collective-permute-done((f32[64,1024]{1,0:T(8,128)S(1)}, f32[64,1024]{1,0:T(8,128)S(1)}, u32[]{:S(2)}, u32[]{:S(2)}) %collective-permute-start.2) | collective-permute-done | bytes 262176 | tf_op jit(solution)/shard_map/ppermute | solution.py:16
  25.3 0.1 constant_dynamic-update-slice_fusion.3
  25.4 4.0 %collective-permute-done.1 = f32[64,1024]{1,0:T(8,128)S(1)} collective-permute-done((f32[64,1024]{1,0:T(8,128)S(1)}, f32[64,1024]{1,0:T(8,128)S(1)}, u32[]{:S(2)}, u32[]{:S(2)}) %collective-permute-start.1) | collective-permute-done | bytes 262176 | tf_op jit(solution)/shard_map/ppermute | solution.py:19
  29.4 0.7 multiply_reduce_fusion
  30.2 9.9 %all-reduce = (f32[64]{0:T(128)S(1)}, f32[64]{0:T(128)S(1)}) all-reduce(f32[64]{0:T(128)S(1)} %get-tuple-element.3, f32[64]{0:T(128)S(1)} %get-tuple-element.2), channel_id=1, replica_groups=mesh['groups'=2,'nodes'=4,'cols'=4] {'nodes'}, use_global_device_ids=true, to_apply=%region_1.2 | all-reduce | flops 128 | bytes 1024 | tf_op jit(solution)/shard_map/psum | solution.py:82
  40.1 2.2 %convolution_bitcast_fusion = f32[16,8,8,128]{3,2,1,0:T(8,128)S(1)} fusion(f32[16,128,128]{2,1,0:T(8,128)S(1)} %copy-done, f32[64,2048]{1,0:T(8,128)S(1)} %copy-done.2, f32[64,2048]{1,0:T(8,128)S(1)} %get-tuple-element.6, f32[64]{0:T(128)S(1)} %div.19), kind=kOutput, calls=%fused_computation | convolution fusion | flops 201588736 | bytes 2621696 | tf_op jit(solution)/shard_map/cbj,bij->cbi/dot_general | solution.py:33
  42.3 0.2 fusion.29
  42.6 8.8 %psum.30 = f32[64]{0:T(128)S(1)} all-reduce(f32[64]{0:T(128)S(1)} %fusion.29), channel_id=1, replica_groups=mesh['groups'=2,'nodes'=4,'cols'=4] {'nodes'}, use_global_device_ids=true, to_apply=%region_5.6 | all-reduce | flops 64 | bytes 512 | tf_op jit(solution)/shard_map/psum | solution.py:82
  51.4 0.1 bitcast_add_fusion
  51.6 3.5 %collective-permute-start.4 = (f32[64,1024]{1,0:T(8,128)S(1)}, f32[64,1024]{1,0:T(8,128)S(1)}, u32[]{:S(2)}, u32[]{:S(2)}) collective-permute-start(f32[64,1024]{1,0:T(8,128)S(1)} %get-tuple-element.10), channel_id=1, source_target_pairs={{0,4},{4,8},{8,12},{1,5},{5,9},{9,13},{2,6},{6,10},{10,14},{3,7},{... | collective-permute-start | bytes 786440 | tf_op jit(solution)/shard_map/ppermute | solution.py:16
  55.1 1.3 collective-permute-start.3
  56.4 2.6 %collective-permute-done.4 = f32[64,1024]{1,0:T(8,128)S(1)} collective-permute-done((f32[64,1024]{1,0:T(8,128)S(1)}, f32[64,1024]{1,0:T(8,128)S(1)}, u32[]{:S(2)}, u32[]{:S(2)}) %collective-permute-start.4) | collective-permute-done | bytes 262176 | tf_op jit(solution)/shard_map/ppermute | solution.py:16
  59.0 4.4 %collective-permute-done.3 = f32[64,1024]{1,0:T(8,128)S(1)} collective-permute-done((f32[64,1024]{1,0:T(8,128)S(1)}, f32[64,1024]{1,0:T(8,128)S(1)}, u32[]{:S(2)}, u32[]{:S(2)}) %collective-permute-start.3) | collective-permute-done | bytes 262176 | tf_op jit(solution)/shard_map/ppermute | solution.py:19
  63.4 0.8 fusion.44
  64.2 8.6 %psum.31 = f32[64]{0:T(128)S(1)} all-reduce(f32[64]{0:T(128)S(1)} %fusion.44), channel_id=1, replica_groups=mesh['groups'=2,'nodes'=4,'cols'=4] {'nodes'}, use_global_device_ids=true, to_apply=%region_7.8 | all-reduce | flops 64 | bytes 512 | tf_op jit(solution)/shard_map/psum | solution.py:89
  72.8 0.1 multiply_add_fusion
  73.0 3.7 %collective-permute-start.6 = (f32[64,1024]{1,0:T(8,128)S(1)}, f32[64,1024]{1,0:T(8,128)S(1)}, u32[]{:S(2)}, u32[]{:S(2)}) collective-permute-start(f32[64,1024]{1,0:T(8,128)S(1)} %get-tuple-element.8), channel_id=1, source_target_pairs={{0,4},{4,8},{8,12},{1,5},{5,9},{9,13},{2,6},{6,10},{10,14},{3,7},{... | collective-permute-start | bytes 786440 | tf_op jit(solution)/shard_map/ppermute | solution.py:16
  76.7 1.3 collective-permute-start.5
  78.0 2.6 %collective-permute-done.6 = f32[64,1024]{1,0:T(8,128)S(1)} collective-permute-done((f32[64,1024]{1,0:T(8,128)S(1)}, f32[64,1024]{1,0:T(8,128)S(1)}, u32[]{:S(2)}, u32[]{:S(2)}) %collective-permute-start.6) | collective-permute-done | bytes 262176 | tf_op jit(solution)/shard_map/ppermute | solution.py:16
  80.5 4.4 %collective-permute-done.5 = f32[64,1024]{1,0:T(8,128)S(1)} collective-permute-done((f32[64,1024]{1,0:T(8,128)S(1)}, f32[64,1024]{1,0:T(8,128)S(1)}, u32[]{:S(2)}, u32[]{:S(2)}) %collective-permute-start.5) | collective-permute-done | bytes 262176 | tf_op jit(solution)/shard_map/ppermute | solution.py:19
  84.9 1.4 %fusion.4 = f32[64,2048]{1,0:T(8,128)} fusion(f32[64,2048]{1,0:T(8,128)S(1)} %multiply_add_fusion, f32[64,1024]{1,0:T(8,128)S(1)} %collective-permute-done.6, f32[64,1024]{1,0:T(8,128)S(1)} %collective-permute-done.5, f32[2048]{0:T(1024)S(1)} %bitcast.64, f32[2048]{0:T(1024)S(1)} %bitcast.60, f32[2048]{0:T(1024)S(1)} %bitcast.76, f32[2048]{0:T(1024)S(1)} %bitcast.80, ...), kind=kLoop, calls=%fused_computation.23 | loop fusion | flops 2490368 | bytes 1630208 | tf_op jit(solution)/shard_map/sub | solution.py:52
  86.4 20.9 %all-gather.2.cloned.1.call-done = f32[256,2048]{1,0:T(8,128)} async-done(((f32[64,2048]{1,0:T(8,128)}), f32[256,2048]{1,0:T(8,128)}) %all-gather.2.cloned.1.call-update) | async-done | bytes 2097168 | tf_op jit(solution)/shard_map/all_gather | solution.py:103
  107.4 3.6 %convolution_multiply_fusion = f32[64,256]{1,0:T(8,128)S(1)} fusion(f32[64,2048]{1,0:T(8,128)S(1)} %multiply_add_fusion, f32[256,2048]{1,0:T(8,128)} %all-gather.2.cloned.1.call-done), kind=kOutput, calls=%fused_computation.2 | convolution fusion | flops 402669568 | bytes 2686976 | tf_op jit(solution)/shard_map/dot_general | solution.py:101
  111.0 0.7 copy.16
  111.8 19.3 %reduce-scatter.4.cloned.1.call-done = f32[64,64]{1,0:T(8,128)} async-done(((f32[256,64]{1,0:T(8,128)}), f32[64,64]{1,0:T(8,128)}) %reduce-scatter.4.cloned.1.call-update) | async-done | bytes 16400
  131.1 1.5 %copy.17 = f32[64,64]{1,0:T(8,128)} copy(f32[64,64]{0,1:T(8,128)} %bitcast.81) | data formatting | bytes 32768
  (30 shorter events, 0.5 us)
Async XLA Ops:
  7.2 5.9 %copy-start = (f32[16,128,128]{2,1,0:T(8,128)S(1)}, f32[16,128,128]{2,1,0:T(8,128)}, u32[]{:S(2)}) copy-start(f32[16,128,128]{2,1,0:T(8,128)} %param.7) | copy-start | bytes 3145732
  7.2 100.2 %all-gather.2.cloned.1.call-start = ((), (), s32[]{:S(2)}) async-start(), calls=%async_computation.1 | async-start | bytes 2621440 | tf_op jit(solution)/shard_map/all_gather | solution.py:103
  8.0 13.3 %copy-start.3 = (f32[3,2048]{1,0:T(4,128)S(1)}, f32[3,2048]{1,0:T(4,128)}, u32[]{:S(2)}) copy-start(f32[3,2048]{1,0:T(4,128)} %param.5) | copy-start | bytes 73732
  8.0 13.5 %copy-start.4 = (f32[2048]{0:T(1024)S(1)}, f32[2048]{0:T(1024)}, u32[]{:S(2)}) copy-start(f32[2048]{0:T(1024)} %param.6) | copy-start | bytes 24580
  8.0 13.3 %collective-permute-start = (f32[3,1024]{1,0:T(4,128)S(1)}, f32[3,1024]{1,0:T(4,128)S(1)}, u32[]{:S(2)}, u32[]{:S(2)}) collective-permute-start(f32[3,1024]{1,0:T(4,128)S(1)} %slice.121), channel_id=1, source_target_pairs={{0,4},{4,8},{8,12},{1,5},{5,9},{9,13},{2,6},{6,10},{10,14},{3,7},{... | collective-permute-start | bytes 36872 | tf_op jit(solution)/shard_map/ppermute | solution.py:27
  16.3 13.1 %copy-start.2 = (f32[64,2048]{1,0:T(8,128)S(1)}, f32[64,2048]{1,0:T(8,128)}, u32[]{:S(2)}) copy-start(f32[64,2048]{1,0:T(8,128)} %param.4) | copy-start | bytes 1572868
  16.4 8.9 %collective-permute-start.2 = (f32[64,1024]{1,0:T(8,128)S(1)}, f32[64,1024]{1,0:T(8,128)S(1)}, u32[]{:S(2)}, u32[]{:S(2)}) collective-permute-start(f32[64,1024]{1,0:T(8,128)S(1)} %get-tuple-element.12), channel_id=1, source_target_pairs={{0,4},{4,8},{8,12},{1,5},{5,9},{9,13},{2,6},{6,10},{10,14},{3,7},{... | collective-permute-start | bytes 786440 | tf_op jit(solution)/shard_map/ppermute | solution.py:16
  20.0 9.4 %collective-permute-start.1 = (f32[64,1024]{1,0:T(8,128)S(1)}, f32[64,1024]{1,0:T(8,128)S(1)}, u32[]{:S(2)}, u32[]{:S(2)}) collective-permute-start(f32[64,1024]{1,0:T(8,128)S(1)} %get-tuple-element.11), channel_id=1, source_target_pairs={{4,0},{8,4},{12,8},{5,1},{9,5},{13,9},{6,2},{10,6},{14,10},{7,3},{... | collective-permute-start | bytes 786440 | tf_op jit(solution)/shard_map/ppermute | solution.py:19
  51.6 7.4 %collective-permute-start.4 = (f32[64,1024]{1,0:T(8,128)S(1)}, f32[64,1024]{1,0:T(8,128)S(1)}, u32[]{:S(2)}, u32[]{:S(2)}) collective-permute-start(f32[64,1024]{1,0:T(8,128)S(1)} %get-tuple-element.10), channel_id=1, source_target_pairs={{0,4},{4,8},{8,12},{1,5},{5,9},{9,13},{2,6},{6,10},{10,14},{3,7},{... | collective-permute-start | bytes 786440 | tf_op jit(solution)/shard_map/ppermute | solution.py:16
  55.1 8.4 %collective-permute-start.3 = (f32[64,1024]{1,0:T(8,128)S(1)}, f32[64,1024]{1,0:T(8,128)S(1)}, u32[]{:S(2)}, u32[]{:S(2)}) collective-permute-start(f32[64,1024]{1,0:T(8,128)S(1)} %get-tuple-element.9), channel_id=1, source_target_pairs={{4,0},{8,4},{12,8},{5,1},{9,5},{13,9},{6,2},{10,6},{14,10},{7,3},{... | collective-permute-start | bytes 786440 | tf_op jit(solution)/shard_map/ppermute | solution.py:19
  72.9 38.1 %copy-start.1 = (f32[64,2048]{1,0:T(8,128)}, f32[64,2048]{1,0:T(8,128)S(1)}, u32[]{:S(2)}) copy-start(f32[64,2048]{1,0:T(8,128)S(1)} %multiply_add_fusion) | copy-start | bytes 1572868
  73.0 7.5 %collective-permute-start.6 = (f32[64,1024]{1,0:T(8,128)S(1)}, f32[64,1024]{1,0:T(8,128)S(1)}, u32[]{:S(2)}, u32[]{:S(2)}) collective-permute-start(f32[64,1024]{1,0:T(8,128)S(1)} %get-tuple-element.8), channel_id=1, source_target_pairs={{0,4},{4,8},{8,12},{1,5},{5,9},{9,13},{2,6},{6,10},{10,14},{3,7},{... | collective-permute-start | bytes 786440 | tf_op jit(solution)/shard_map/ppermute | solution.py:16
  76.7 8.3 %collective-permute-start.5 = (f32[64,1024]{1,0:T(8,128)S(1)}, f32[64,1024]{1,0:T(8,128)S(1)}, u32[]{:S(2)}, u32[]{:S(2)}) collective-permute-start(f32[64,1024]{1,0:T(8,128)S(1)} %get-tuple-element.7), channel_id=1, source_target_pairs={{4,0},{8,4},{12,8},{5,1},{9,5},{13,9},{6,2},{10,6},{14,10},{7,3},{... | collective-permute-start | bytes 786440 | tf_op jit(solution)/shard_map/ppermute | solution.py:19
  86.4 44.7 %reduce-scatter.4.cloned.1.call-start = ((), (), s32[]{:S(2)}) async-start(), calls=%async_computation.2 | async-start | bytes 163840
Sparse Core Ops, SparseCore 0:
  86.5 20.8 all-gather.1
  111.9 19.1 reduce-scatter.3
where the time goes:
time: 140 us; the launch traced here: 139 us
  waiting for transfers between devices  62 us (44%)
  blocking collectives  27.3 us (20%)
  starting transfers between devices  19.8 us (14%)
  between operations  14.3 us (10%)
  matrix products  9 us (6%)
  other arithmetic  3.52 us (3%)
  local copies, waits for them, and re-layouts  3.46 us (2%)
    all_gather x1, waiting for transfers between devices, on_device(): lax.all_gather(images, 'cols', axis=0, tiled=True)  20.9 us
    unnamed x3, waiting for transfers between devices  19.4 us
    psum x2, blocking collectives, resid_dot(): return lax.psum(jnp.sum(left * right, axis=1), 'nodes')  18.7 us
    ppermute x3, waiting for transfers between devices, padded_2(): lax.ppermute(lax.slice_in_dim(block, 0, width, axis=dim), axis, backward)  12.8 us
    ppermute x3, starting transfers between devices, padded_2(): lax.ppermute(lax.slice_in_dim(block, block.shape[dim] - width, None, axis...  10.8 us
    ppermute x3, waiting for transfers between devices, padded_2(): lax.ppermute(lax.slice_in_dim(block, block.shape[dim] - width, None, axis...  8.9 us
    psum x1, blocking collectives, on_device(): curve = lax.psum(jnp.sum(direction * image, axis=1), 'nodes')  8.59 us
    dot_general x2, matrix products, precondition(): jnp.einsum('cbj,bij->cbi', blocks, precond, precision=lax.Precision.HIGHEST)  5.37 us
  transfers between devices with their start and end apart: 9, of which 8 were waited for; matrix products, arithmetic and copies ran while one was open for 3% of the time, Pallas kernels for 0%

commit v1 on v0

v1 whole, which is shorter than its diff:
```python
import functools

import jax
import jax.numpy as jnp
from jax import lax
from jax.experimental import pallas as pl
from jax.experimental.pallas import tpu as pltpu
from jax.sharding import PartitionSpec as P

GRID_X = 32
GRID_Y = 32
PLANE = GRID_X * GRID_Y
LANES = 128
CHUNKS = PLANE // LANES
F32 = jnp.float32


def slot_planes():
    odd = lax.rem(lax.axis_index("nodes"), 2)
    return 1 - odd, odd


def split(x):
    high = x.astype(jnp.bfloat16)
    return high, (x - high.astype(F32)).astype(jnp.bfloat16)


def product(left, right, dims):
    left_high, left_low = left
    right_high, right_low = right
    dot = functools.partial(
        lax.dot_general, dimension_numbers=(dims, ((), ())), preferred_element_type=F32
    )
    return dot(left_high, right_high) + (
        dot(left_low, right_high) + dot(left_high, right_low)
    )


def block_product(x, matrix):
    return product(split(x), split(matrix), ((1,), (0,)))


def chunk(k):
    return slice(k * LANES, (k + 1) * LANES)


def plane_chunk(plane, k):
    return pl.ds(pl.multiple_of(plane * PLANE + k * LANES, LANES), LANES)


def lane_index(rows=8):
    return lax.broadcasted_iota(jnp.int32, (rows, LANES), 1)


def ahead_row(here, after):
    lane = lax.broadcasted_iota(jnp.int32, here.shape, here.ndim - 1)
    mixed = here if after is None else jnp.where(lane < GRID_X, after, here)
    return pltpu.roll(mixed, LANES - GRID_X, mixed.ndim - 1)


def behind_row(before, here):
    lane = lax.broadcasted_iota(jnp.int32, here.shape, here.ndim - 1)
    mixed = here if before is None else jnp.where(lane >= LANES - GRID_X, before, here)
    return pltpu.roll(mixed, GRID_X, mixed.ndim - 1)


def plane_springs(couplings, ground, plane, middle, crossing):
    lane = lane_index()
    inside_x = lane % GRID_X < GRID_X - 1

    def row(ref, index, k):
        return jnp.broadcast_to(ref[index : index + 1, plane_chunk(plane, k)], (8, LANES))

    along_y = []
    for k in range(CHUNKS):
        spring = row(couplings, 1, k)
        if k == CHUNKS - 1:
            spring = jnp.where(lane < LANES - GRID_X, spring, 0.0)
        along_y.append(spring)
    result = []
    for k in range(CHUNKS):
        right = jnp.where(inside_x, row(couplings, 0, k), 0.0)
        left = pltpu.roll(right, 1, 1)
        up = along_y[k]
        before = along_y[k - 1] if k else jnp.zeros_like(up)
        down = behind_row(before, up)
        diag = row(ground, 0, k) + (right + left) + (up + down) + (middle[k] + crossing[k])
        result.append((diag, right, left, up, down, middle[k], crossing[k]))
    return result


def all_springs(couplings, ground, got, rows):
    odd = lax.rem(lax.axis_index("nodes"), 2)
    own, mid = [], []
    for k in range(CHUNKS):
        own.append(jnp.broadcast_to(couplings[2:3, PLANE + k * LANES : PLANE + (k + 1) * LANES], (8, LANES)))
        mid.append(jnp.broadcast_to(couplings[2:3, chunk(k)], (8, LANES)))
    result = []
    for slot, plane in enumerate(slot_planes()):
        theirs = odd == (1 - slot)
        crossing = [
            jnp.where(theirs, got[slot][rows : rows + 8, chunk(k)], own[k])
            for k in range(CHUNKS)
        ]
        result.append(plane_springs(couplings, ground, plane, mid, crossing))
    return result


def stiff_chunk(springs, k, field, other, halo, rows):
    def load(ref, index):
        return ref[0:rows, chunk(index)].reshape(rows // 8, 8, LANES)

    diag, right, left, up, down, middle, crossing = springs[k]
    here = load(field, k)
    before = load(field, k - 1) if k else None
    after = load(field, k + 1) if k < CHUNKS - 1 else None
    result = diag * here
    result = result - right * pltpu.roll(here, LANES - 1, 2)
    result = result - left * pltpu.roll(here, 1, 2)
    result = result - up * ahead_row(here, after)
    result = result - down * behind_row(before, here)
    result = result - middle * load(other, k)
    result = result - crossing * load(halo, k)
    return result.reshape(rows, LANES)


def first_kernel(forces, couplings, precond, out_a, out_b):
    rows = forces.shape[0]
    for out, plane in zip((out_a, out_b), slot_planes()):
        for k in range(CHUNKS):
            out[0:rows, chunk(k)] = block_product(
                forces[:, plane_chunk(plane, k)], precond[plane * CHUNKS + k]
            )
            out[rows : rows + 8, chunk(k)] = jnp.broadcast_to(
                couplings[2:3, PLANE + k * LANES : PLANE + (k + 1) * LANES], (8, LANES)
            )


def other_kernel(forces, precond, out):
    for slot, plane in enumerate(slot_planes()):
        for k in range(CHUNKS):
            out[slot, :, chunk(k)] = block_product(
                forces[:, plane_chunk(plane, k)], precond[plane * CHUNKS + k]
            )


def second_kernel(couplings, ground, precond, d_a, d_b, got_a, got_b, q, w_a, w_b):
    rows = w_a.shape[0]
    springs = all_springs(couplings, ground, (got_a, got_b), rows)
    fields = (d_a, d_b)
    for slot, plane in enumerate(slot_planes()):
        for k in range(CHUNKS):
            image = stiff_chunk(
                springs[slot], k, fields[slot], fields[1 - slot], (got_a, got_b)[slot], rows
            )
            q[slot, :, chunk(k)] = image
            (w_a, w_b)[slot][:, chunk(k)] = block_product(
                image, precond[plane * CHUNKS + k]
            )


def third_kernel(forces, couplings, ground, d_a, d_b, got_a, got_b, q, w_a, w_b, next_a, next_b, v, dots):
    rows = w_a.shape[0]
    springs = all_springs(couplings, ground, (got_a, got_b), rows)
    fields = (w_a, w_b)
    sums = [jnp.zeros((rows, LANES), F32) for _ in range(4)]
    for slot, plane in enumerate(slot_planes()):
        for k in range(CHUNKS):
            image = stiff_chunk(
                springs[slot], k, fields[slot], fields[1 - slot], (next_a, next_b)[slot], rows
            )
            v[slot, :, chunk(k)] = image
            force = forces[:, plane_chunk(plane, k)]
            d_here = (d_a, d_b)[slot][0:rows, chunk(k)]
            q_here = q[slot, :, chunk(k)]
            w_here = fields[slot][:, chunk(k)]
            sums[0] += force * d_here
            sums[1] += d_here * q_here
            sums[2] += q_here * w_here
            sums[3] += w_here * image
    lane = lane_index(rows)
    packed = jnp.zeros((rows, LANES), F32)
    for index, value in enumerate(sums):
        packed = jnp.where(lane == index, jnp.sum(value, axis=1, keepdims=True), packed)
    if rows < LANES:
        packed = jnp.concatenate([packed, jnp.zeros((LANES - rows, LANES), F32)], axis=0)
    dots[...] = packed.T[0:8, :]


def fourth_kernel(n_dots, n_cols, exchange, *refs):
    dots, refs = refs[:n_dots], refs[n_dots:]
    d_a, d_b, q, v, refs = *refs[:4], refs[4:]
    d_all, refs = [(d_a, d_b)] + [tuple(refs[2 * i : 2 * i + 2]) for i in range(n_cols - 1)], refs[2 * n_cols - 2 :]
    w_all, refs = [tuple(refs[2 * i : 2 * i + 2]) for i in range(n_cols)], refs[2 * n_cols :]
    modes, coeffs, outs, gram = refs[0], refs[1], refs[2:-1], refs[-1]
    rows = modes.shape[0]
    total = dots[0][...]
    for piece in dots[1:]:
        total = total + piece[...]
    rz0, dq, qw, wv = (total[i : i + 1, :] for i in range(4))
    alpha0 = rz0 / dq
    rz1 = alpha0 * alpha0 * qw - rz0
    grow = 1.0 + rz1 / rz0
    curve1 = grow * grow * dq - 2.0 * alpha0 * grow * qw + alpha0 * alpha0 * wv
    alpha1 = rz1 / curve1
    used = lane_index(1) < rows
    on_d = jnp.where(used, alpha0 + alpha1 * grow, 0.0)
    on_w = jnp.where(used, -alpha0 * alpha1, 0.0)
    both = jnp.concatenate([on_d, on_w, jnp.zeros((LANES - 2, LANES), F32)], axis=0)
    coeffs[...] = both[0:8, :]
    turned = both.T
    p = jnp.broadcast_to(turned[0:rows, 0:1], (rows, LANES))
    s = jnp.broadcast_to(turned[0:rows, 1:2], (rows, LANES))
    sums = [None] * n_cols
    for slot, plane in enumerate(slot_planes()):
        high, low = [], []
        for k in range(CHUNKS):
            d_here = (d_a, d_b)[slot][0:rows, chunk(k)]
            w_here = w_all[0][slot][:, chunk(k)]
            modes[:, plane_chunk(plane, k)] = p * d_here + s * w_here
            image = p * q[slot, :, chunk(k)] + s * v[slot, :, chunk(k)]
            image_high, image_low = split(image)
            high.append(image_high)
            low.append(image_low)
        image = (jnp.concatenate(high, axis=1), jnp.concatenate(low, axis=1))
        for i in range(n_cols):
            columns = jnp.concatenate(
                [d_all[i][slot][0:rows, :], w_all[i][slot][0:rows, :]], axis=0
            )
            term = product(image, split(columns), ((1,), (1,)))
            sums[i] = term if sums[i] is None else sums[i] + term
    if exchange:
        for i in range(n_cols):
            gram[i] = sums[i]
        mine = lax.axis_index("nodes") ^ lax.axis_index("cols")
        for i in range(n_cols):
            outs[i][...] = gram[mine ^ i]
    else:
        for i in range(n_cols):
            outs[0][i] = sums[i]


def fifth_kernel(scale, n_sums, *refs):
    sums, coeffs, tile = refs[:n_sums], refs[n_sums], refs[n_sums + 1]
    rows = tile.shape[0]
    total = sums[0][...]
    for piece in sums[1:]:
        total = total + piece[...]
    tile[...] = (
        coeffs[0:1, 0:rows] * total[:, 0:rows] + coeffs[1:2, 0:rows] * total[:, rows : 2 * rows]
    ) * scale


def call(kernel, name, args, shapes, scratch=()):
    return pl.pallas_call(
        kernel,
        out_shape=[jax.ShapeDtypeStruct(shape, F32) for shape in shapes],
        in_specs=[pl.BlockSpec(memory_space=pltpu.VMEM)] * len(args),
        out_specs=[pl.BlockSpec(memory_space=pltpu.VMEM)] * len(shapes),
        scratch_shapes=scratch,
        name=name,
    )(*args)


def pairs(count, first):
    result = []
    for low in range(first, count - 1, 2):
        result += [(low, low + 1), (low + 1, low)]
    return result


def swapped(block, axis, bit):
    return lax.ppermute(block, axis, [(i, i ^ bit) for i in range(lax.axis_size(axis))])


def on_device(forces, couplings, ground, precond):
    rows, length = forces.shape
    nodes, cols = lax.axis_size("nodes"), lax.axis_size("cols")
    ground = ground.reshape(1, length)
    bits = []
    while 2 ** len(bits) < cols:
        bits.insert(0, 2 ** len(bits))

    def gathered(block, first=None):
        held = {0: block}
        for bit in bits:
            for key in list(held):
                held[key ^ bit] = swapped(held[key], "cols", bit)
        return held

    field = (rows, PLANE)
    d_a, d_b = call(
        first_kernel, "first", (forces, couplings, precond), [(rows + 8, PLANE)] * 2
    )
    got_a = lax.ppermute(d_a, "nodes", pairs(nodes, 0))
    got_b = lax.ppermute(d_b, "nodes", pairs(nodes, 1))
    d_held = {0: (d_a, d_b)}
    if bits:
        forces_far = swapped(forces, "cols", bits[0])
        (d_far,) = call(other_kernel, "other", (forces_far, precond), [(2, rows, PLANE)])
        d_held[bits[0]] = (d_far[0], d_far[1])
        for bit in bits[1:]:
            for key in list(d_held):
                d_held[key ^ bit] = tuple(swapped(x, "cols", bit) for x in d_held[key])
    q, w_a, w_b = call(
        second_kernel,
        "second",
        (couplings, ground, precond, d_a, d_b, got_a, got_b),
        [(2,) + field, field, field],
    )
    next_a = lax.ppermute(w_a, "nodes", pairs(nodes, 0))
    next_b = lax.ppermute(w_b, "nodes", pairs(nodes, 1))
    w_held_a, w_held_b = gathered(w_a), gathered(w_b)
    v, dots = call(
        third_kernel,
        "third",
        (forces, couplings, ground, d_a, d_b, got_a, got_b, q, w_a, w_b, next_a, next_b),
        [(2,) + field, (8, LANES)],
    )
    exchange = nodes == cols
    if exchange:
        dots = [dots] + [swapped(dots, "nodes", i) for i in range(1, nodes)]
    else:
        dots = [lax.psum(dots, "nodes")]
    operands = dots + [d_a, d_b, q, v]
    for i in range(1, cols):
        operands += d_held[i]
    for i in range(cols):
        operands += [w_held_a[i], w_held_b[i]]
    sums = [(rows, LANES)] * cols if exchange else [(cols, rows, LANES)]
    modes, coeffs, *grams = call(
        functools.partial(fourth_kernel, len(dots), cols, exchange),
        "fourth",
        operands,
        [(rows, length), (8, LANES)] + sums,
        [pltpu.VMEM((cols, rows, LANES), F32)],
    )
    scale = 1.0 / (length * nodes)
    if exchange:
        turn = [(n * cols + c, c * cols + n) for n in range(nodes) for c in range(cols)]
        theirs = lax.ppermute(coeffs, ("nodes", "cols"), turn)
        sums = [grams[0]] + [swapped(grams[i], "nodes", i) for i in range(1, nodes)]
        (tile,) = call(
            functools.partial(fifth_kernel, scale, nodes),
            "fifth",
            (*sums, theirs),
            [(rows, rows)],
        )
    else:
        gram = grams[0]
        every = lax.all_gather(coeffs, "cols")
        mine = lax.axis_index("cols")
        parts = []
        for i in range(cols):
            block = lax.dynamic_index_in_dim(gram, mine ^ i, 0, keepdims=False)
            parts.append(
                every[i, 0:1, 0:rows] * block[:, 0:rows]
                + every[i, 1:2, 0:rows] * block[:, rows : 2 * rows]
            )
        partial = jnp.concatenate(parts, axis=1) * scale
        tile = lax.psum_scatter(partial, "nodes", scatter_dimension=1, tiled=True)
    return (modes, tile)


def solution(mesh):
    in_specs = (
        P("cols", ("groups", "nodes")),
        P(None, ("groups", "nodes")),
        P(("groups", "nodes")),
        P(("groups", "nodes"), None, None),
    )
    out_specs = (P("cols", ("groups", "nodes")), P(("groups", "cols"), "nodes"))
    return jax.shard_map(
        on_device, mesh=mesh, in_specs=in_specs, out_specs=out_specs, check_vma=False
    )
```

time: 140 us -> 74.3 us (0.53)
  the two profiles are of different devices: /device:TPU:0 before, /device:TPU:2 now
where the time goes in v1:
time: 74.3 us; the launch traced here: 73.9 us
  starting transfers between devices  24.7 us (33%)
  waiting for transfers between devices  24.7 us (33%)
  Pallas kernels  19.3 us (26%)
  local copies, waits for them, and re-layouts  4.26 us (6%)
  between operations  0.95 us (1%)
    pallas_call x6, Pallas kernels, call(): pl.pallas_call(kernel, out_shape=[jax.ShapeDtypeStruct(shape, F32) for sh...  19.3 us
    ppermute x17, starting transfers between devices, swapped(): lax.ppermute(block, axis, [(i, i ^ bit) for i in range(lax.axis_size(axis...  15.2 us
    ppermute x17, waiting for transfers between devices, swapped(): lax.ppermute(block, axis, [(i, i ^ bit) for i in range(lax.axis_size(axis...  13.8 us
    ppermute x1, waiting for transfers between devices, on_device(): got_a = lax.ppermute(d_a, 'nodes', pairs(nodes, 0))  5.58 us
    ppermute x1, waiting for transfers between devices, on_device(): theirs = lax.ppermute(coeffs, ('nodes', 'cols'), turn)  5.37 us
    ppermute x1, starting transfers between devices, on_device(): next_a = lax.ppermute(w_a, 'nodes', pairs(nodes, 0))  4.49 us
    unnamed x54, local copies, waits for them, and re-layouts  3.18 us
    ppermute x1, starting transfers between devices, on_device(): theirs = lax.ppermute(coeffs, ('nodes', 'cols'), turn)  1.91 us
  transfers between devices with their start and end apart: 22, of which 7 were waited for; matrix products, arithmetic and copies ran while one was open for 1% of the time, Pallas kernels for 13%

profile of v1, /device:TPU:2, one launch (start us, length us, event | category | flops | bytes accessed | tf_op | source)
XLA Modules:
  0.0 73.9 jit_solution(14264453363719182540)
XLA Ops:
  0.6 2.7 %first.1 = (f32[72,1024]{1,0:T(8,128)}, f32[72,1024]{1,0:T(8,128)}) custom-call(f32[64,2048]{1,0:T(8,128)} %forces.3, f32[3,2048]{1,0:T(4,128)} %couplings.5, f32[16,128,128]{2,1,0:T(8,128)} %precond.5), custom_call_target="tpu_custom_call" | custom-call | tf_op jit(solution)/shard_map/first/pallas_call | solution.py:255
  3.4 1.6 %collective-permute-start = (f32[72,1024]{1,0:T(8,128)}, f32[72,1024]{1,0:T(8,128)S(1)}, u32[]{:S(2)}, u32[]{:S(2)}) collective-permute-start(f32[72,1024]{1,0:T(8,128)} %get-tuple-element.15.d_a.refs_4_), channel_id=1, source_target_pairs={{0,4},{4,0},{8,12},{12,8},{1,5},{5,1},{9,13},{13,9},{2,6},{6,2},{1... | collective-permute-start | bytes 884744 | tf_op jit(solution)/shard_map/ppermute | solution.py:295
  4.9 0.7 collective-permute-start.1
  5.6 0.6 collective-permute-start.9
  6.2 0.5 collective-permute-start.8
  6.7 5.6 %collective-permute-done.got_a = f32[72,1024]{1,0:T(8,128)S(1)} collective-permute-done((f32[72,1024]{1,0:T(8,128)}, f32[72,1024]{1,0:T(8,128)S(1)}, u32[]{:S(2)}, u32[]{:S(2)}) %collective-permute-start) | collective-permute-done | bytes 294944 | tf_op jit(solution)/shard_map/ppermute | solution.py:295
  12.3 0.7 copy-done.1
  13.1 3.3 %second.1 = (f32[2,64,1024]{2,1,0:T(8,128)}, f32[64,1024]{1,0:T(8,128)}, f32[64,1024]{1,0:T(8,128)}) custom-call(f32[3,2048]{1,0:T(4,128)} %couplings.5, f32[1,2048]{1,0:T(1,128)} %bitcast.5, f32[16,128,128]{2,1,0:T(8,128)} %precond.5, f32[72,1024]{1,0:T(8,128)} %get-tuple-element.15.d_a.refs_4_, f32[72,1024]{1,0:T(8,128)} %get-tuple-element.16.d_b.refs_5_, ...), custom_call_target="tpu_custom_call" | custom-call | tf_op jit(solution)/shard_map/second/pallas_call | solution.py:255
  16.4 4.5 %collective-permute-start.2 = (f32[64,1024]{1,0:T(8,128)}, f32[64,1024]{1,0:T(8,128)S(1)}, u32[]{:S(2)}, u32[]{:S(2)}) collective-permute-start(f32[64,1024]{1,0:T(8,128)} %get-tuple-element.18.w_a.refs_14_), channel_id=1, source_target_pairs={{0,4},{4,0},{8,12},{12,8},{1,5},{5,1},{9,13},{13,9},{2,6},{6,2},{1... | collective-permute-start | bytes 786440 | tf_op jit(solution)/shard_map/ppermute | solution.py:311
  20.9 0.8 %collective-permute-start.3 = (f32[64,1024]{1,0:T(8,128)}, f32[64,1024]{1,0:T(8,128)S(1)}, u32[]{:S(2)}, u32[]{:S(2)}) collective-permute-start(f32[64,1024]{1,0:T(8,128)} %get-tuple-element.19.w_b.refs_15_), channel_id=1, source_target_pairs={{4,8},{8,4},{5,9},{9,5},{6,10},{10,6},{7,11},{11,7},{20,24},{24,20... | collective-permute-start | bytes 786440 | tf_op jit(solution)/shard_map/ppermute | solution.py:312
  21.7 0.6 collective-permute-start.14
  22.4 1.5 %collective-permute-start.15 = (f32[64,1024]{1,0:T(8,128)}, f32[64,1024]{1,0:T(8,128)S(1)}, u32[]{:S(2)}, u32[]{:S(2)}) collective-permute-start(f32[64,1024]{1,0:T(8,128)} %get-tuple-element.19.w_b.refs_15_), channel_id=1, source_target_pairs={{0,2},{1,3},{2,0},{3,1},{4,6},{5,7},{6,4},{7,5},{8,10},{9,11},{10,... | collective-permute-start | bytes 786440 | tf_op jit(solution)/shard_map/ppermute | solution.py:273
  23.9 0.8 %copy-done.6 = f32[64,2048]{1,0:T(8,128)} copy-done((f32[64,2048]{1,0:T(8,128)}, f32[64,2048]{1,0:T(8,128)S(1)}, u32[]{:S(2)}) %copy-start.6) | copy-done | bytes 524312
  24.6 2.7 %other.1 = f32[2,64,1024]{2,1,0:T(8,128)} custom-call(f32[64,2048]{1,0:T(8,128)} %copy-done.6, f32[16,128,128]{2,1,0:T(8,128)} %precond.5), custom_call_target="tpu_custom_call" | custom-call | tf_op jit(solution)/shard_map/other/pallas_call | solution.py:255
  27.5 1.1 %slice_bitcast_fusion = (f32[64,1024]{1,0:T(8,128)S(1)}, f32[64,1024]{1,0:T(8,128)S(1)}) fusion(f32[2,64,1024]{2,1,0:T(8,128)} %other.1), kind=kLoop, calls=%fused_computation | loop fusion | bytes 1048576 | tf_op jit(solution)/shard_map/squeeze | solution.py:301
  28.6 0.5 collective-permute-start.10
  29.2 2.1 %collective-permute-done.14.refs_18_ = f32[64,1024]{1,0:T(8,128)S(1)} collective-permute-done((f32[64,1024]{1,0:T(8,128)}, f32[64,1024]{1,0:T(8,128)S(1)}, u32[]{:S(2)}, u32[]{:S(2)}) %collective-permute-start.14) | collective-permute-done | bytes 262176 | tf_op jit(solution)/shard_map/ppermute | solution.py:273
  31.3 3.3 %collective-permute-done.15.refs_19_ = f32[64,1024]{1,0:T(8,128)S(1)} collective-permute-done((f32[64,1024]{1,0:T(8,128)}, f32[64,1024]{1,0:T(8,128)S(1)}, u32[]{:S(2)}, u32[]{:S(2)}) %collective-permute-start.15) | collective-permute-done | bytes 262176 | tf_op jit(solution)/shard_map/ppermute | solution.py:273
  35.1 3.4 %third.1 = (f32[2,64,1024]{2,1,0:T(8,128)}, f32[8,128]{1,0:T(8,128)}) custom-call(f32[64,2048]{1,0:T(8,128)} %forces.3, f32[3,2048]{1,0:T(4,128)} %couplings.5, f32[1,2048]{1,0:T(1,128)} %bitcast.6, f32[72,1024]{1,0:T(8,128)} %get-tuple-element.15.d_a.refs_4_, f32[72,1024]{1,0:T(8,128)} %get-tuple-element.16.d_b.refs_5_, f32[72,1024]{1,0:T(8,128)} %copy-done.1, ...), custom_call_target="tpu_custom_call" | custom-call | tf_op jit(solution)/shard_map/third/pallas_call | solution.py:255
  38.6 2.7 %collective-permute-start.4 = (f32[8,128]{1,0:T(8,128)}, f32[8,128]{1,0:T(8,128)S(1)}, u32[]{:S(2)}, u32[]{:S(2)}) collective-permute-start(f32[8,128]{1,0:T(8,128)} %get-tuple-element.20.refs_0_), channel_id=1, source_target_pairs={{0,4},{4,0},{8,12},{12,8},{1,5},{5,1},{9,13},{13,9},{2,6},{6,2},{1... | collective-permute-start | bytes 12296 | tf_op jit(solution)/shard_map/ppermute | solution.py:273
  41.3 1.8 %collective-permute-done.4.refs_1_ = f32[8,128]{1,0:T(8,128)S(1)} collective-permute-done((f32[8,128]{1,0:T(8,128)}, f32[8,128]{1,0:T(8,128)S(1)}, u32[]{:S(2)}, u32[]{:S(2)}) %collective-permute-start.4) | collective-permute-done | bytes 4128 | tf_op jit(solution)/shard_map/ppermute | solution.py:273
  43.1 2.1 %collective-permute-start.5 = (f32[8,128]{1,0:T(8,128)}, f32[8,128]{1,0:T(8,128)S(1)}, u32[]{:S(2)}, u32[]{:S(2)}) collective-permute-start(f32[8,128]{1,0:T(8,128)} %get-tuple-element.20.refs_0_), channel_id=1, source_target_pairs={{0,8},{4,12},{8,0},{12,4},{1,9},{5,13},{9,1},{13,5},{2,10},{6,14},... | collective-permute-start | bytes 12296 | tf_op jit(solution)/shard_map/ppermute | solution.py:273
  45.1 2.6 %collective-permute-done.5.refs_2_ = f32[8,128]{1,0:T(8,128)S(1)} collective-permute-done((f32[8,128]{1,0:T(8,128)}, f32[8,128]{1,0:T(8,128)S(1)}, u32[]{:S(2)}, u32[]{:S(2)}) %collective-permute-start.5) | collective-permute-done | bytes 4128 | tf_op jit(solution)/shard_map/ppermute | solution.py:273
  47.8 1.7 %collective-permute-start.6 = (f32[8,128]{1,0:T(8,128)}, f32[8,128]{1,0:T(8,128)S(1)}, u32[]{:S(2)}, u32[]{:S(2)}) collective-permute-start(f32[8,128]{1,0:T(8,128)} %get-tuple-element.20.refs_0_), channel_id=1, source_target_pairs={{0,12},{4,8},{8,4},{12,0},{1,13},{5,9},{9,5},{13,1},{2,14},{6,10},... | collective-permute-start | bytes 12296 | tf_op jit(solution)/shard_map/ppermute | solution.py:273
  49.5 3.9 %collective-permute-done.6.refs_3_ = f32[8,128]{1,0:T(8,128)S(1)} collective-permute-done((f32[8,128]{1,0:T(8,128)}, f32[8,128]{1,0:T(8,128)S(1)}, u32[]{:S(2)}, u32[]{:S(2)}) %collective-permute-start.6) | collective-permute-done | bytes 4128 | tf_op jit(solution)/shard_map/ppermute | solution.py:273
  54.4 5.6 %fourth.1 = (f32[64,2048]{1,0:T(8,128)}, f32[8,128]{1,0:T(8,128)}, f32[64,128]{1,0:T(8,128)}, f32[64,128]{1,0:T(8,128)}, f32[64,128]{1,0:T(8,128)}, /*index=5*/f32[64,128]{1,0:T(8,128)}) custom-call(f32[8,128]{1,0:T(8,128)} %get-tuple-element.20.refs_0_, f32[8,128]{1,0:T(8,128)} %copy-done.23, f32[8,128]{1,0:T(8,128)} %copy-done.24, f32[8,128]{1,0:T(8,128)} %copy-done.25, ...), custom_call_target="tpu_custom_call" | custom-call | tf_op jit(solution)/shard_map/fourth/pallas_call | solution.py:255
  60.3 2.0 %collective-permute-start.19 = (f32[64,128]{1,0:T(8,128)}, f32[64,128]{1,0:T(8,128)S(1)}, u32[]{:S(2)}, u32[]{:S(2)}) collective-permute-start(f32[64,128]{1,0:T(8,128)} %get-tuple-element.25), channel_id=1, source_target_pairs={{0,8},{4,12},{8,0},{12,4},{1,9},{5,13},{9,1},{13,5},{2,10},{6,14},... | collective-permute-start | bytes 98312 | tf_op jit(solution)/shard_map/ppermute | solution.py:273
  62.3 2.2 %collective-permute-start.20 = (f32[64,128]{1,0:T(8,128)}, f32[64,128]{1,0:T(8,128)S(1)}, u32[]{:S(2)}, u32[]{:S(2)}) collective-permute-start(f32[64,128]{1,0:T(8,128)} %get-tuple-element.26), channel_id=1, source_target_pairs={{0,12},{4,8},{8,4},{12,0},{1,13},{5,9},{9,5},{13,1},{2,14},{6,10},... | collective-permute-start | bytes 98312 | tf_op jit(solution)/shard_map/ppermute | solution.py:273
  64.5 1.9 %collective-permute-start.21 = (f32[8,128]{1,0:T(8,128)S(1)}, f32[8,128]{1,0:T(8,128)S(1)}, u32[]{:S(2)}, u32[]{:S(2)}) collective-permute-start(f32[8,128]{1,0:T(8,128)S(1)} %copy-done.26), channel_id=1, source_target_pairs={{0,0},{1,4},{2,8},{3,12},{4,1},{5,5},{6,9},{7,13},{8,2},{9,6},{10,... | collective-permute-start | bytes 12296 | tf_op jit(solution)/shard_map/ppermute | solution.py:341
  66.4 5.4 %collective-permute-done.21.refs_4_ = f32[8,128]{1,0:T(8,128)S(1)} collective-permute-done((f32[8,128]{1,0:T(8,128)S(1)}, f32[8,128]{1,0:T(8,128)S(1)}, u32[]{:S(2)}, u32[]{:S(2)}) %collective-permute-start.21) | collective-permute-done | bytes 4128 | tf_op jit(solution)/shard_map/ppermute | solution.py:341
  71.8 0.5 copy-done.22
  72.4 1.5 %fifth.1 = f32[64,64]{1,0:T(8,128)} custom-call(f32[64,128]{1,0:T(8,128)} %get-tuple-element.23.refs_0_, f32[64,128]{1,0:T(8,128)} %copy-done.19, f32[64,128]{1,0:T(8,128)} %copy-done.20, f32[64,128]{1,0:T(8,128)} %copy-done.21, f32[8,128]{1,0:T(8,128)} %copy-done.22), custom_call_target="tpu_custom_call" | custom-call | tf_op jit(solution)/shard_map/fifth/pallas_call | solution.py:255
  (73 shorter events, 2.0 us)
Async XLA Ops:
  3.4 9.0 %collective-permute-start = (f32[72,1024]{1,0:T(8,128)}, f32[72,1024]{1,0:T(8,128)S(1)}, u32[]{:S(2)}, u32[]{:S(2)}) collective-permute-start(f32[72,1024]{1,0:T(8,128)} %get-tuple-element.15.d_a.refs_4_), channel_id=1, source_target_pairs={{0,4},{4,0},{8,12},{12,8},{1,5},{5,1},{9,13},{13,9},{2,6},{6,2},{1... | collective-permute-start | bytes 884744 | tf_op jit(solution)/shard_map/ppermute | solution.py:295
  4.9 7.4 %collective-permute-start.1 = (f32[72,1024]{1,0:T(8,128)}, f32[72,1024]{1,0:T(8,128)S(1)}, u32[]{:S(2)}, u32[]{:S(2)}) collective-permute-start(f32[72,1024]{1,0:T(8,128)} %get-tuple-element.16.d_b.refs_5_), channel_id=1, source_target_pairs={{4,8},{8,4},{5,9},{9,5},{6,10},{10,6},{7,11},{11,7},{20,24},{24,20... | collective-permute-start | bytes 884744 | tf_op jit(solution)/shard_map/ppermute | solution.py:296
  5.6 18.2 %collective-permute-start.9 = (f32[64,2048]{1,0:T(8,128)S(1)}, f32[64,2048]{1,0:T(8,128)S(1)}, u32[]{:S(2)}, u32[]{:S(2)}) collective-permute-start(f32[64,2048]{1,0:T(8,128)S(1)} %copy-done), channel_id=1, source_target_pairs={{0,2},{1,3},{2,0},{3,1},{4,6},{5,7},{6,4},{7,5},{8,10},{9,11},{10,... | collective-permute-start | bytes 1572872 | tf_op jit(solution)/shard_map/ppermute | solution.py:273
  6.2 15.5 %collective-permute-start.7 = (f32[72,1024]{1,0:T(8,128)}, f32[72,1024]{1,0:T(8,128)S(1)}, u32[]{:S(2)}, u32[]{:S(2)}) collective-permute-start(f32[72,1024]{1,0:T(8,128)} %get-tuple-element.15.d_a.refs_4_), channel_id=1, source_target_pairs={{0,1},{1,0},{2,3},{3,2},{4,5},{5,4},{6,7},{7,6},{8,9},{9,8},{10,11... | collective-permute-start | bytes 884744 | tf_op jit(solution)/shard_map/ppermute | solution.py:273
  6.2 16.1 %collective-permute-start.8 = (f32[72,1024]{1,0:T(8,128)}, f32[72,1024]{1,0:T(8,128)S(1)}, u32[]{:S(2)}, u32[]{:S(2)}) collective-permute-start(f32[72,1024]{1,0:T(8,128)} %get-tuple-element.16.d_b.refs_5_), channel_id=1, source_target_pairs={{0,1},{1,0},{2,3},{3,2},{4,5},{5,4},{6,7},{7,6},{8,9},{9,8},{10,11... | collective-permute-start | bytes 884744 | tf_op jit(solution)/shard_map/ppermute | solution.py:273
  16.4 11.0 %collective-permute-start.2 = (f32[64,1024]{1,0:T(8,128)}, f32[64,1024]{1,0:T(8,128)S(1)}, u32[]{:S(2)}, u32[]{:S(2)}) collective-permute-start(f32[64,1024]{1,0:T(8,128)} %get-tuple-element.18.w_a.refs_14_), channel_id=1, source_target_pairs={{0,4},{4,0},{8,12},{12,8},{1,5},{5,1},{9,13},{13,9},{2,6},{6,2},{1... | collective-permute-start | bytes 786440 | tf_op jit(solution)/shard_map/ppermute | solution.py:311
  20.9 6.5 %copy-start.3 = (f32[64,1024]{1,0:T(8,128)S(1)}, f32[64,1024]{1,0:T(8,128)}, u32[]{:S(2)}) copy-start(f32[64,1024]{1,0:T(8,128)} %get-tuple-element.19.w_b.refs_15_) | copy-start | bytes 786436
  20.9 7.7 %collective-permute-start.3 = (f32[64,1024]{1,0:T(8,128)}, f32[64,1024]{1,0:T(8,128)S(1)}, u32[]{:S(2)}, u32[]{:S(2)}) collective-permute-start(f32[64,1024]{1,0:T(8,128)} %get-tuple-element.19.w_b.refs_15_), channel_id=1, source_target_pairs={{4,8},{8,4},{5,9},{9,5},{6,10},{10,6},{7,11},{11,7},{20,24},{24,20... | collective-permute-start | bytes 786440 | tf_op jit(solution)/shard_map/ppermute | solution.py:312
  21.7 5.6 %copy-start.7 = (f32[72,1024]{1,0:T(8,128)}, f32[72,1024]{1,0:T(8,128)S(1)}, u32[]{:S(2)}) copy-start(f32[72,1024]{1,0:T(8,128)S(1)} %collective-permute-done.7.refs_8_) | copy-start | bytes 884740
  21.7 9.5 %collective-permute-start.14 = (f32[64,1024]{1,0:T(8,128)}, f32[64,1024]{1,0:T(8,128)S(1)}, u32[]{:S(2)}, u32[]{:S(2)}) collective-permute-start(f32[64,1024]{1,0:T(8,128)} %get-tuple-element.18.w_a.refs_14_), channel_id=1, source_target_pairs={{0,2},{1,3},{2,0},{3,1},{4,6},{5,7},{6,4},{7,5},{8,10},{9,11},{10,... | collective-permute-start | bytes 786440 | tf_op jit(solution)/shard_map/ppermute | solution.py:273
  22.4 5.0 %copy-start.8 = (f32[72,1024]{1,0:T(8,128)}, f32[72,1024]{1,0:T(8,128)S(1)}, u32[]{:S(2)}) copy-start(f32[72,1024]{1,0:T(8,128)S(1)} %collective-permute-done.8.refs_9_) | copy-start | bytes 884740
  22.4 12.2 %collective-permute-start.15 = (f32[64,1024]{1,0:T(8,128)}, f32[64,1024]{1,0:T(8,128)S(1)}, u32[]{:S(2)}, u32[]{:S(2)}) collective-permute-start(f32[64,1024]{1,0:T(8,128)} %get-tuple-element.19.w_b.refs_15_), channel_id=1, source_target_pairs={{0,2},{1,3},{2,0},{3,1},{4,6},{5,7},{6,4},{7,5},{8,10},{9,11},{10,... | collective-permute-start | bytes 786440 | tf_op jit(solution)/shard_map/ppermute | solution.py:273
  23.8 10.7 %collective-permute-start.12 = (f32[64,1024]{1,0:T(8,128)}, f32[64,1024]{1,0:T(8,128)S(1)}, u32[]{:S(2)}, u32[]{:S(2)}) collective-permute-start(f32[64,1024]{1,0:T(8,128)} %get-tuple-element.18.w_a.refs_14_), channel_id=1, source_target_pairs={{0,1},{1,0},{2,3},{3,2},{4,5},{5,4},{6,7},{7,6},{8,9},{9,8},{10,11... | collective-permute-start | bytes 786440 | tf_op jit(solution)/shard_map/ppermute | solution.py:273
  27.4 11.1 %collective-permute-start.13 = (f32[64,1024]{1,0:T(8,128)S(1)}, f32[64,1024]{1,0:T(8,128)S(1)}, u32[]{:S(2)}, u32[]{:S(2)}) collective-permute-start(f32[64,1024]{1,0:T(8,128)S(1)} %copy-done.3), channel_id=1, source_target_pairs={{0,1},{1,0},{2,3},{3,2},{4,5},{5,4},{6,7},{7,6},{8,9},{9,8},{10,11... | collective-permute-start | bytes 786440 | tf_op jit(solution)/shard_map/ppermute | solution.py:273
  28.6 9.9 %copy-start.4 = (f32[64,1024]{1,0:T(8,128)}, f32[64,1024]{1,0:T(8,128)S(1)}, u32[]{:S(2)}) copy-start(f32[64,1024]{1,0:T(8,128)S(1)} %get-tuple-element.28.refs_11_) | copy-start | bytes 786436
  28.6 9.9 %copy-start.5 = (f32[64,1024]{1,0:T(8,128)}, f32[64,1024]{1,0:T(8,128)S(1)}, u32[]{:S(2)}) copy-start(f32[64,1024]{1,0:T(8,128)S(1)} %get-tuple-element.29.refs_10_) | copy-start | bytes 786436
  28.6 6.4 %copy-start.10 = (f32[64,1024]{1,0:T(8,128)}, f32[64,1024]{1,0:T(8,128)S(1)}, u32[]{:S(2)}) copy-start(f32[64,1024]{1,0:T(8,128)S(1)} %collective-permute-done.3.next_b) | copy-start | bytes 786436
  28.6 24.8 %collective-permute-start.10 = (f32[64,1024]{1,0:T(8,128)S(1)}, f32[64,1024]{1,0:T(8,128)S(1)}, u32[]{:S(2)}, u32[]{:S(2)}) collective-permute-start(f32[64,1024]{1,0:T(8,128)S(1)} %get-tuple-element.29.refs_10_), channel_id=1, source_target_pairs={{0,1},{1,0},{2,3},{3,2},{4,5},{5,4},{6,7},{7,6},{8,9},{9,8},{10,11... | collective-permute-start | bytes 786440 | tf_op jit(solution)/shard_map/ppermute | solution.py:273
  31.3 7.2 %copy-start.11 = (f32[64,1024]{1,0:T(8,128)}, f32[64,1024]{1,0:T(8,128)S(1)}, u32[]{:S(2)}) copy-start(f32[64,1024]{1,0:T(8,128)S(1)} %collective-permute-done.14.refs_18_) | copy-start | bytes 786436
  31.3 22.1 %collective-permute-start.11 = (f32[64,1024]{1,0:T(8,128)S(1)}, f32[64,1024]{1,0:T(8,128)S(1)}, u32[]{:S(2)}, u32[]{:S(2)}) collective-permute-start(f32[64,1024]{1,0:T(8,128)S(1)} %get-tuple-element.28.refs_11_), channel_id=1, source_target_pairs={{0,1},{1,0},{2,3},{3,2},{4,5},{5,4},{6,7},{7,6},{8,9},{9,8},{10,11... | collective-permute-start | bytes 786440 | tf_op jit(solution)/shard_map/ppermute | solution.py:273
  34.5 18.9 %collective-permute-start.16 = (f32[64,1024]{1,0:T(8,128)S(1)}, f32[64,1024]{1,0:T(8,128)S(1)}, u32[]{:S(2)}, u32[]{:S(2)}) collective-permute-start(f32[64,1024]{1,0:T(8,128)S(1)} %collective-permute-done.14.refs_18_), channel_id=1, source_target_pairs={{0,1},{1,0},{2,3},{3,2},{4,5},{5,4},{6,7},{7,6},{8,9},{9,8},{10,11... | collective-permute-start | bytes 786440 | tf_op jit(solution)/shard_map/ppermute | solution.py:273
  34.6 18.9 %collective-permute-start.17 = (f32[64,1024]{1,0:T(8,128)S(1)}, f32[64,1024]{1,0:T(8,128)S(1)}, u32[]{:S(2)}, u32[]{:S(2)}) collective-permute-start(f32[64,1024]{1,0:T(8,128)S(1)} %collective-permute-done.15.refs_19_), channel_id=1, source_target_pairs={{0,1},{1,0},{2,3},{3,2},{4,5},{5,4},{6,7},{7,6},{8,9},{9,8},{10,11... | collective-permute-start | bytes 786440 | tf_op jit(solution)/shard_map/ppermute | solution.py:273
  38.5 14.9 %copy-start.14 = (f32[64,1024]{1,0:T(8,128)}, f32[64,1024]{1,0:T(8,128)S(1)}, u32[]{:S(2)}) copy-start(f32[64,1024]{1,0:T(8,128)S(1)} %collective-permute-done.13.refs_17_) | copy-start | bytes 786436
  38.6 4.5 %collective-permute-start.4 = (f32[8,128]{1,0:T(8,128)}, f32[8,128]{1,0:T(8,128)S(1)}, u32[]{:S(2)}, u32[]{:S(2)}) collective-permute-start(f32[8,128]{1,0:T(8,128)} %get-tuple-element.20.refs_0_), channel_id=1, source_target_pairs={{0,4},{4,0},{8,12},{12,8},{1,5},{5,1},{9,13},{13,9},{2,6},{6,2},{1... | collective-permute-start | bytes 12296 | tf_op jit(solution)/shard_map/ppermute | solution.py:273
  43.1 10.4 %copy-start.23 = (f32[8,128]{1,0:T(8,128)}, f32[8,128]{1,0:T(8,128)S(1)}, u32[]{:S(2)}) copy-start(f32[8,128]{1,0:T(8,128)S(1)} %collective-permute-done.4.refs_1_) | copy-start | bytes 12292
  43.1 4.7 %collective-permute-start.5 = (f32[8,128]{1,0:T(8,128)}, f32[8,128]{1,0:T(8,128)S(1)}, u32[]{:S(2)}, u32[]{:S(2)}) collective-permute-start(f32[8,128]{1,0:T(8,128)} %get-tuple-element.20.refs_0_), channel_id=1, source_target_pairs={{0,8},{4,12},{8,0},{12,4},{1,9},{5,13},{9,1},{13,5},{2,10},{6,14},... | collective-permute-start | bytes 12296 | tf_op jit(solution)/shard_map/ppermute | solution.py:273
  47.8 5.7 %copy-start.24 = (f32[8,128]{1,0:T(8,128)}, f32[8,128]{1,0:T(8,128)S(1)}, u32[]{:S(2)}) copy-start(f32[8,128]{1,0:T(8,128)S(1)} %collective-permute-done.5.refs_2_) | copy-start | bytes 12292
  47.8 5.6 %collective-permute-start.6 = (f32[8,128]{1,0:T(8,128)}, f32[8,128]{1,0:T(8,128)S(1)}, u32[]{:S(2)}, u32[]{:S(2)}) collective-permute-start(f32[8,128]{1,0:T(8,128)} %get-tuple-element.20.refs_0_), channel_id=1, source_target_pairs={{0,12},{4,8},{8,4},{12,0},{1,13},{5,9},{9,5},{13,1},{2,14},{6,10},... | collective-permute-start | bytes 12296 | tf_op jit(solution)/shard_map/ppermute | solution.py:273
  60.0 11.7 %collective-permute-start.18 = (f32[64,128]{1,0:T(8,128)}, f32[64,128]{1,0:T(8,128)S(1)}, u32[]{:S(2)}, u32[]{:S(2)}) collective-permute-start(f32[64,128]{1,0:T(8,128)} %get-tuple-element.24), channel_id=1, source_target_pairs={{0,4},{4,0},{8,12},{12,8},{1,5},{5,1},{9,13},{13,9},{2,6},{6,2},{1... | collective-permute-start | bytes 98312 | tf_op jit(solution)/shard_map/ppermute | solution.py:273
  60.3 11.5 %collective-permute-start.19 = (f32[64,128]{1,0:T(8,128)}, f32[64,128]{1,0:T(8,128)S(1)}, u32[]{:S(2)}, u32[]{:S(2)}) collective-permute-start(f32[64,128]{1,0:T(8,128)} %get-tuple-element.25), channel_id=1, source_target_pairs={{0,8},{4,12},{8,0},{12,4},{1,9},{5,13},{9,1},{13,5},{2,10},{6,14},... | collective-permute-start | bytes 98312 | tf_op jit(solution)/shard_map/ppermute | solution.py:273
  62.3 9.5 %collective-permute-start.20 = (f32[64,128]{1,0:T(8,128)}, f32[64,128]{1,0:T(8,128)S(1)}, u32[]{:S(2)}, u32[]{:S(2)}) collective-permute-start(f32[64,128]{1,0:T(8,128)} %get-tuple-element.26), channel_id=1, source_target_pairs={{0,12},{4,8},{8,4},{12,0},{1,13},{5,9},{9,5},{13,1},{2,14},{6,10},... | collective-permute-start | bytes 98312 | tf_op jit(solution)/shard_map/ppermute | solution.py:273
  64.5 7.3 %collective-permute-start.21 = (f32[8,128]{1,0:T(8,128)S(1)}, f32[8,128]{1,0:T(8,128)S(1)}, u32[]{:S(2)}, u32[]{:S(2)}) collective-permute-start(f32[8,128]{1,0:T(8,128)S(1)} %copy-done.26), channel_id=1, source_target_pairs={{0,0},{1,4},{2,8},{3,12},{4,1},{5,5},{6,9},{7,13},{8,2},{9,6},{10,... | collective-permute-start | bytes 12296 | tf_op jit(solution)/shard_map/ppermute | solution.py:341
  (17 other events, 27.3 us)

commit v2 on v1

v2 whole, which is shorter than its diff:
```python
import functools

import jax
import jax.numpy as jnp
from jax import lax
from jax.experimental import pallas as pl
from jax.experimental.pallas import tpu as pltpu
from jax.sharding import PartitionSpec as P

GRID_X = 32
GRID_Y = 32
PLANE = GRID_X * GRID_Y
LANES = 128
CHUNKS = PLANE // LANES
F32 = jnp.float32
KERNEL_BYTES = 8 * 2**20


def slot_planes():
    odd = lax.rem(lax.axis_index("nodes"), 2)
    return 1 - odd, odd


def split(x):
    high = x.astype(jnp.bfloat16)
    return high, (x - high.astype(F32)).astype(jnp.bfloat16)


def product(left, right, dims):
    left_high, left_low = left
    right_high, right_low = right
    dot = functools.partial(
        lax.dot_general, dimension_numbers=(dims, ((), ())), preferred_element_type=F32
    )
    return dot(left_high, right_high) + (
        dot(left_low, right_high) + dot(left_high, right_low)
    )


def block_product(x, matrix):
    return product(split(x), split(matrix), ((1,), (0,)))


def chunk(k):
    return slice(k * LANES, (k + 1) * LANES)


def plane_chunk(plane, k):
    return pl.ds(pl.multiple_of(plane * PLANE + k * LANES, LANES), LANES)


def lane_index(rows=8):
    return lax.broadcasted_iota(jnp.int32, (rows, LANES), 1)


def ahead_row(here, after):
    lane = lax.broadcasted_iota(jnp.int32, here.shape, here.ndim - 1)
    mixed = here if after is None else jnp.where(lane < GRID_X, after, here)
    return pltpu.roll(mixed, LANES - GRID_X, mixed.ndim - 1)


def behind_row(before, here):
    lane = lax.broadcasted_iota(jnp.int32, here.shape, here.ndim - 1)
    mixed = here if before is None else jnp.where(lane >= LANES - GRID_X, before, here)
    return pltpu.roll(mixed, GRID_X, mixed.ndim - 1)


def plane_springs(couplings, ground, plane, middle, crossing, meets):
    lane = lane_index()
    inside_x = lane % GRID_X < GRID_X - 1

    def row(ref, index, k):
        return jnp.broadcast_to(ref[index : index + 1, plane_chunk(plane, k)], (8, LANES))

    along_y = []
    for k in range(CHUNKS):
        spring = row(couplings, 1, k)
        if k == CHUNKS - 1:
            spring = jnp.where(lane < LANES - GRID_X, spring, 0.0)
        along_y.append(spring)
    result = []
    for k in range(CHUNKS):
        right = jnp.where(inside_x, row(couplings, 0, k), 0.0)
        left = pltpu.roll(right, 1, 1)
        up = along_y[k]
        before = along_y[k - 1] if k else jnp.zeros_like(up)
        down = behind_row(before, up)
        diag = row(ground, 0, k) + (right + left) + (up + down) + (middle[k] + crossing[k])
        halo = jnp.where(meets, crossing[k], 0.0)
        result.append((diag, right, left, up, down, middle[k], halo))
    return result


def all_springs(couplings, ground, got, rows):
    place, count = lax.axis_index("nodes"), lax.axis_size("nodes")
    odd = lax.rem(place, 2)
    own, mid = [], []
    for k in range(CHUNKS):
        own.append(
            jnp.broadcast_to(
                couplings[2:3, PLANE + k * LANES : PLANE + (k + 1) * LANES], (8, LANES)
            )
        )
        mid.append(jnp.broadcast_to(couplings[2:3, chunk(k)], (8, LANES)))
    result = []
    for slot, plane in enumerate(slot_planes()):
        below = odd == (1 - slot)
        meets = jnp.where(below, place > 0, place < count - 1)
        crossing = [
            jnp.where(
                below,
                jnp.where(place > 0, got[slot][rows : rows + 8, chunk(k)], 0.0),
                own[k],
            )
            for k in range(CHUNKS)
        ]
        result.append(plane_springs(couplings, ground, plane, mid, crossing, meets))
    return result


def stiff_chunk(springs, k, field, other, halo, rows):
    def load(ref, index):
        return ref[0:rows, chunk(index)].reshape(rows // 8, 8, LANES)

    diag, right, left, up, down, middle, crossing = springs[k]
    here = load(field, k)
    before = load(field, k - 1) if k else None
    after = load(field, k + 1) if k < CHUNKS - 1 else None
    result = diag * here
    result = result - right * pltpu.roll(here, LANES - 1, 2)
    result = result - left * pltpu.roll(here, 1, 2)
    result = result - up * ahead_row(here, after)
    result = result - down * behind_row(before, here)
    result = result - middle * load(other, k)
    result = result - crossing * load(halo, k)
    return result.reshape(rows, LANES)


def first_kernel(forces, couplings, precond, out_a, out_b, field, matrices, springs, sems):
    rows = forces.shape[0]
    copies = []
    for slot, plane in enumerate(slot_planes()):
        here = pl.ds(pl.multiple_of(plane * PLANE, PLANE), PLANE)
        copies.append(
            (
                pltpu.make_async_copy(forces.at[:, here], field.at[slot], sems.at[slot, 0]),
                pltpu.make_async_copy(
                    precond.at[pl.ds(plane * CHUNKS, CHUNKS)], matrices.at[slot], sems.at[slot, 1]
                ),
            )
        )
    spring_copy = pltpu.make_async_copy(couplings, springs, sems.at[2, 0])
    for pair in copies:
        for copy in pair:
            copy.start()
    spring_copy.start()
    for slot, out in enumerate((out_a, out_b)):
        for copy in copies[slot]:
            copy.wait()
        for k in range(CHUNKS):
            out[0:rows, chunk(k)] = block_product(field[slot, :, chunk(k)], matrices[slot, k])
    spring_copy.wait()
    for out in (out_a, out_b):
        for k in range(CHUNKS):
            out[rows : rows + 8, chunk(k)] = jnp.broadcast_to(
                springs[2:3, PLANE + k * LANES : PLANE + (k + 1) * LANES], (8, LANES)
            )


def other_kernel(forces, precond, out):
    for slot, plane in enumerate(slot_planes()):
        for k in range(CHUNKS):
            out[slot, :, chunk(k)] = block_product(
                forces[:, plane_chunk(plane, k)], precond[plane * CHUNKS + k]
            )


def second_kernel(couplings, ground, precond, d_a, d_b, got_a, got_b, q, w_a, w_b, near):
    rows = w_a.shape[0]
    springs = all_springs(couplings, ground, (got_a, got_b), rows)
    fields = (d_a, d_b)
    for slot, plane in enumerate(slot_planes()):
        for k in range(CHUNKS):
            image = stiff_chunk(
                springs[slot], k, fields[slot], fields[1 - slot], (got_a, got_b)[slot], rows
            )
            q[slot, :, chunk(k)] = image
            w = block_product(image, precond[plane * CHUNKS + k])
            (w_a, w_b)[slot][:, chunk(k)] = w
            near[slot, 0:rows, chunk(k)] = fields[slot][0:rows, chunk(k)]
            near[slot, rows : 2 * rows, chunk(k)] = w


def place_sums(packed, first, sums):
    lane = lane_index(packed.shape[0])
    for index, value in enumerate(sums):
        total = jnp.sum(value, axis=1, keepdims=True)
        packed = jnp.where(lane == first + index, total, packed)
    return packed


def side_kernel(forces, q, near, packed):
    rows = forces.shape[0]
    sums = [jnp.zeros((rows, LANES), F32) for _ in range(3)]
    for slot, plane in enumerate(slot_planes()):
        for k in range(CHUNKS):
            d_here = near[slot, 0:rows, chunk(k)]
            q_here = q[slot, :, chunk(k)]
            sums[0] += forces[:, plane_chunk(plane, k)] * d_here
            sums[1] += d_here * q_here
            sums[2] += q_here * near[slot, rows : 2 * rows, chunk(k)]
    packed[...] = place_sums(jnp.zeros((rows, LANES), F32), 0, sums)


def third_kernel(couplings, ground, got_a, got_b, w_a, w_b, next_a, next_b, packed, v, dots):
    rows = w_a.shape[0]
    springs = all_springs(couplings, ground, (got_a, got_b), rows)
    fields = (w_a, w_b)
    total = jnp.zeros((rows, LANES), F32)
    for slot in range(2):
        for k in range(CHUNKS):
            image = stiff_chunk(
                springs[slot], k, fields[slot], fields[1 - slot], (next_a, next_b)[slot], rows
            )
            v[slot, :, chunk(k)] = image
            total += fields[slot][:, chunk(k)] * image
    values = place_sums(packed[...], 3, [total])
    if rows < LANES:
        values = jnp.concatenate([values, jnp.zeros((LANES - rows, LANES), F32)], axis=0)
    dots[...] = values.T[0:8, :]


def columns_of(field, slot, rows):
    return jnp.concatenate([part[slot, 0:rows, :] for part in field], axis=0)


def early_kernel(n_near, n_far, q, v, *refs):
    near, d_far = refs[:n_near], refs[n_near : n_near + n_far]
    qv_high, qv_low, near_gram, far_gram = refs[n_near + n_far :]
    rows = q.shape[1]
    near_sums, far_sum = [None] * n_near, None
    for slot in range(2):
        images = split(jnp.concatenate([q[slot], v[slot]], axis=0))
        qv_high[slot], qv_low[slot] = images
        for i in range(n_near):
            term = product(images, split(near[i][slot]), ((1,), (1,)))
            near_sums[i] = term if slot == 0 else near_sums[i] + term
        term = product(images, split(columns_of(d_far, slot, rows)), ((1,), (1,)))
        far_sum = term if slot == 0 else far_sum + term
    for i in range(n_near):
        near_gram[i] = near_sums[i]
    far_gram[...] = far_sum


def late_kernel(n_dots, n_near, n_far, exchange, *refs):
    dots, refs = refs[:n_dots], refs[n_dots:]
    qv_high, qv_low, near_gram, far_gram, refs = *refs[:4], refs[4:]
    w_far, coeffs, outs, gram = refs[: 2 * n_far], refs[2 * n_far], refs[2 * n_far + 1 : -1], refs[-1]
    rows = near_gram.shape[1] // 2
    far_sum = None
    for slot in range(2):
        columns = jnp.concatenate([w_far[2 * i + slot][...] for i in range(n_far)], axis=0)
        term = product((qv_high[slot], qv_low[slot]), split(columns), ((1,), (1,)))
        far_sum = term if slot == 0 else far_sum + term
    total = dots[0][...]
    for piece in dots[1:]:
        total = total + piece[...]
    rz0, dq, qw, wv = (total[i : i + 1, :] for i in range(4))
    alpha0 = rz0 / dq
    rz1 = alpha0 * alpha0 * qw - rz0
    grow = 1.0 + rz1 / rz0
    curve1 = grow * grow * dq - 2.0 * alpha0 * grow * qw + alpha0 * alpha0 * wv
    alpha1 = rz1 / curve1
    used = lane_index(1) < rows
    on_d = jnp.where(used, alpha0 + alpha1 * grow, 0.0)
    on_w = jnp.where(used, -alpha0 * alpha1, 0.0)
    coeffs[...] = jnp.concatenate([on_d, on_w, jnp.zeros((6, LANES), F32)], axis=0)
    p, s = turned(coeffs, rows)
    if not exchange:
        gram = outs[0]
    for i in range(n_near):
        gram[i] = p * near_gram[i, 0:rows] + s * near_gram[i, rows : 2 * rows]
    d_part, w_part = far_gram[...], far_sum
    for i in range(n_far):
        there = slice(i * rows, (i + 1) * rows)
        both = jnp.concatenate([d_part[:, there], w_part[:, there]], axis=1)
        gram[n_near + i] = p * both[0:rows] + s * both[rows : 2 * rows]
    if exchange:
        mine = lax.axis_index("nodes") ^ lax.axis_index("cols")
        for i in range(n_near + n_far):
            outs[i][...] = gram[mine ^ i]


def turned(coeffs, rows):
    table = jnp.concatenate([coeffs[...], jnp.zeros((LANES - 8, LANES), F32)], axis=0).T
    return [jnp.broadcast_to(table[0:rows, i : i + 1], (rows, LANES)) for i in range(2)]


def modes_kernel(coeffs, near, modes):
    rows = modes.shape[0]
    p, s = turned(coeffs, rows)
    for slot, plane in enumerate(slot_planes()):
        for k in range(CHUNKS):
            modes[:, plane_chunk(plane, k)] = (
                p * near[slot, 0:rows, chunk(k)] + s * near[slot, rows : 2 * rows, chunk(k)]
            )


def fifth_kernel(scale, n_sums, *refs):
    sums, own, theirs, tile = refs[:n_sums], refs[n_sums], refs[n_sums + 1], refs[n_sums + 2]
    rows = tile.shape[0]
    total = sums[0][...]
    for piece in sums[1:]:
        total = total + piece[...]
    here = lax.axis_index("nodes") == lax.axis_index("cols")
    coeffs = jnp.where(here, own[...], theirs[...])
    tile[...] = (
        coeffs[0:1, 0:rows] * total[:, 0:rows] + coeffs[1:2, 0:rows] * total[:, rows : 2 * rows]
    ) * scale


def call(kernel, name, args, shapes, scratch=(), space=pltpu.VMEM):
    shapes = [
        shape if isinstance(shape, jax.ShapeDtypeStruct) else jax.ShapeDtypeStruct(shape, F32)
        for shape in shapes
    ]
    return pl.pallas_call(
        kernel,
        out_shape=shapes,
        in_specs=[pl.BlockSpec(memory_space=space)] * len(args),
        out_specs=[pl.BlockSpec(memory_space=pltpu.VMEM)] * len(shapes),
        scratch_shapes=scratch,
        compiler_params=pltpu.CompilerParams(vmem_limit_bytes=KERNEL_BYTES),
        name=name,
    )(*args)


def neighbours(block, first):
    nodes, cols = lax.axis_size("nodes"), lax.axis_size("cols")
    route = []
    for n in range(nodes):
        other = n + 1 if n % 2 == first else n - 1
        for c in range(cols):
            here = n * cols + c
            if 0 <= other < nodes:
                route.append((here, other * cols + c))
            elif cols % 2 == 0:
                route.append((here, here ^ 1))
    return lax.ppermute(block, ("nodes", "cols"), route)


def transposed(block):
    nodes, cols = lax.axis_size("nodes"), lax.axis_size("cols")
    route = []
    for n in range(nodes):
        for c in range(cols):
            there = c * cols + n if n != c else (n ^ 1) * (cols + 1)
            route.append((n * cols + c, there))
    return lax.ppermute(block, ("nodes", "cols"), route)


def swapped(block, axis, bit):
    return lax.ppermute(block, axis, [(i, i ^ bit) for i in range(lax.axis_size(axis))])


def on_device(forces, couplings, ground, precond):
    rows, length = forces.shape
    nodes, cols = lax.axis_size("nodes"), lax.axis_size("cols")
    ground = ground.reshape(1, length)
    bits = []
    while 2 ** len(bits) < cols:
        bits.append(2 ** len(bits))
    top = cols // 2

    def shared(block):
        held = {0: block}
        for bit in bits[:-1]:
            for key in list(held):
                held[key ^ bit] = swapped(held[key], "cols", bit)
        return [held[key] for key in range(max(top, 1))]

    field = (rows, PLANE)
    d_a, d_b = call(
        first_kernel,
        "first",
        (forces, couplings, precond),
        [(rows + 8, PLANE)] * 2,
        [
            pltpu.VMEM((2, rows, PLANE), F32),
            pltpu.VMEM((2, CHUNKS, LANES, LANES), F32),
            pltpu.VMEM(couplings.shape, F32),
            pltpu.SemaphoreType.DMA((3, 2)),
        ],
        pl.ANY,
    )
    got_a, got_b = neighbours(d_a, 0), neighbours(d_b, 1)
    forces_far = swapped(forces, "cols", top)
    got_a, got_b, forces_far = lax.optimization_barrier((got_a, got_b, forces_far))
    q, w_a, w_b, near = call(
        second_kernel,
        "second",
        (couplings, ground, precond, d_a, d_b, got_a, got_b),
        [(2,) + field, field, field, (2, 2 * rows, PLANE)],
    )
    next_a, next_b = neighbours(w_a, 0), neighbours(w_b, 1)
    w_far_a, w_far_b = swapped(w_a, "cols", top), swapped(w_b, "cols", top)
    near = shared(near)
    (d_far,) = call(other_kernel, "other", (forces_far, precond), [(2,) + field])
    d_far = shared(d_far)
    (packed,) = call(side_kernel, "side", (forces, q, near[0]), [(rows, LANES)])
    next_a, next_b, near, d_far, packed = lax.optimization_barrier(
        (next_a, next_b, near, d_far, packed)
    )
    v, dots = call(
        third_kernel,
        "third",
        (couplings, ground, got_a, got_b, w_a, w_b, next_a, next_b, packed),
        [(2,) + field, (8, LANES)],
    )
    exchange = nodes == cols
    if exchange:
        dots = [dots] + [swapped(dots, "nodes", i) for i in range(1, nodes)]
    else:
        dots = [lax.psum(dots, "nodes")]
    halves = jax.ShapeDtypeStruct((2, 2 * rows, PLANE), jnp.bfloat16)
    qv_high, qv_low, near_gram, far_gram = call(
        functools.partial(early_kernel, len(near), len(d_far)),
        "early",
        (q, v, *near, *d_far),
        [halves, halves, (len(near), 2 * rows, 2 * rows), (2 * rows, len(d_far) * rows)],
    )
    w_far_a, w_far_b, near_gram, *dots = lax.optimization_barrier(
        (w_far_a, w_far_b, near_gram, *dots)
    )
    w_far = [x for pair in zip(shared(w_far_a), shared(w_far_b)) for x in pair]
    coeffs, *grams = call(
        functools.partial(late_kernel, len(dots), len(near), len(d_far), exchange),
        "late",
        (*dots, qv_high, qv_low, near_gram, far_gram, *w_far),
        [(8, LANES)] + ([(rows, LANES)] * cols if exchange else [(cols, rows, LANES)]),
        [pltpu.VMEM((cols, rows, LANES), F32)],
    )
    (modes,) = call(modes_kernel, "modes", (coeffs, near[0]), [(rows, length)])
    scale = 1.0 / (length * nodes)
    if exchange:
        theirs = transposed(coeffs)
        sums = [grams[0]] + [swapped(grams[i], "nodes", i) for i in range(1, nodes)]
        (tile,) = call(
            functools.partial(fifth_kernel, scale, nodes),
            "fifth",
            (*sums, coeffs, theirs),
            [(rows, rows)],
        )
    else:
        gram = grams[0]
        every = lax.all_gather(coeffs, "cols")
        mine = lax.axis_index("cols")
        parts = []
        for i in range(cols):
            block = lax.dynamic_index_in_dim(gram, mine ^ i, 0, keepdims=False)
            parts.append(
                every[i, 0:1, 0:rows] * block[:, 0:rows]
                + every[i, 1:2, 0:rows] * block[:, rows : 2 * rows]
            )
        partial = jnp.concatenate(parts, axis=1) * scale
        tile = lax.psum_scatter(partial, "nodes", scatter_dimension=1, tiled=True)
    return (modes, tile)


def solution(mesh):
    in_specs = (
        P("cols", ("groups", "nodes")),
        P(None, ("groups", "nodes")),
        P(("groups", "nodes")),
        P(("groups", "nodes"), None, None),
    )
    out_specs = (P("cols", ("groups", "nodes")), P(("groups", "cols"), "nodes"))
    return jax.shard_map(
        on_device, mesh=mesh, in_specs=in_specs, out_specs=out_specs, check_vma=False
    )
```

time: 74.3 us -> 49.5 us (0.67)
  the two profiles are of different devices: /device:TPU:2 before, /device:TPU:0 now
where the time goes in v2:
time: 49.5 us; the launch traced here: 49.1 us
  waiting for transfers between devices  20 us (40%)
  starting transfers between devices  18.1 us (37%)
  Pallas kernels  7.31 us (15%)
  local copies, waits for them, and re-layouts  3.04 us (6%)
  between operations  0.73 us (1%)
    ppermute x13, starting transfers between devices, swapped(): lax.ppermute(block, axis, [(i, i ^ bit) for i in range(lax.axis_size(axis...  13.7 us
    ppermute x4, waiting for transfers between devices, neighbours(): return lax.ppermute(block, ('nodes', 'cols'), route)  12.9 us
    pallas_call x9, Pallas kernels, call(): pl.pallas_call(kernel, out_shape=shapes, in_specs=[pl.BlockSpec(memory_sp...  7.31 us
    ppermute x13, waiting for transfers between devices, swapped(): lax.ppermute(block, axis, [(i, i ^ bit) for i in range(lax.axis_size(axis...  5.04 us
    ppermute x4, starting transfers between devices, neighbours(): return lax.ppermute(block, ('nodes', 'cols'), route)  4.34 us
    unnamed x12, local copies, waits for them, and re-layouts  3.04 us
    ppermute x1, waiting for transfers between devices, transposed(): return lax.ppermute(block, ('nodes', 'cols'), route)  2.03 us
  transfers between devices with their start and end apart: 18, of which 8 were waited for; matrix products, arithmetic and copies ran while one was open for 0% of the time, Pallas kernels for 10%

profile of v2, /device:TPU:0, one launch (start us, length us, event | category | flops | bytes accessed | tf_op | source)
XLA Modules:
  0.0 49.1 jit_solution(16479641336434124365)
XLA Ops:
  0.6 3.0 %collective-permute-start.2 = (f32[64,2048]{1,0:T(8,128)}, f32[64,2048]{1,0:T(8,128)S(1)}, u32[]{:S(2)}, u32[]{:S(2)}) collective-permute-start(f32[64,2048]{1,0:T(8,128)} %forces.3), channel_id=1, source_target_pairs={{0,2},{1,3},{2,0},{3,1},{4,6},{5,7},{6,4},{7,5},{8,10},{9,11},{10,... | collective-permute-start | bytes 1572872 | tf_op jit(solution)/shard_map/ppermute | solution.py:363
  3.6 1.2 %copy-done = f32[16,128,128]{2,1,0:T(8,128)S(1)} copy-done((f32[16,128,128]{2,1,0:T(8,128)S(1)}, f32[16,128,128]{2,1,0:T(8,128)}, u32[]{:S(2)}) %copy-start) | copy-done | bytes 1048600
  4.9 1.0 %copy-done.2 = f32[64,2048]{1,0:T(8,128)S(1)} copy-done((f32[64,2048]{1,0:T(8,128)S(1)}, f32[64,2048]{1,0:T(8,128)}, u32[]{:S(2)}) %copy-start.2) | copy-done | bytes 524312
  5.9 0.8 %copy-done.4 = f32[3,2048]{1,0:T(4,128)S(1)} copy-done((f32[3,2048]{1,0:T(4,128)S(1)}, f32[3,2048]{1,0:T(4,128)}, u32[]{:S(2)}) %copy-start.4) | copy-done | bytes 24600
  6.7 0.9 %first.1 = (f32[72,1024]{1,0:T(8,128)S(1)}, f32[72,1024]{1,0:T(8,128)S(1)}) custom-call(f32[64,2048]{1,0:T(8,128)S(1)} %copy-done.2, f32[3,2048]{1,0:T(4,128)S(1)} %copy-done.4, f32[16,128,128]{2,1,0:T(8,128)S(1)} %copy-done), custom_call_target="tpu_custom_call" | custom-call | tf_op jit(solution)/shard_map/first/pallas_call | solution.py:327
  7.6 1.6 %collective-permute-start = (f32[72,1024]{1,0:T(8,128)S(1)}, f32[72,1024]{1,0:T(8,128)S(1)}, u32[]{:S(2)}, u32[]{:S(2)}) collective-permute-start(f32[72,1024]{1,0:T(8,128)S(1)} %get-tuple-element.36.d_a), channel_id=1, source_target_pairs={{0,4},{1,5},{2,6},{3,7},{4,0},{5,1},{6,2},{7,3},{8,12},{9,13},{10,... | collective-permute-start | bytes 884744 | tf_op jit(solution)/shard_map/ppermute | solution.py:349
  9.2 6.9 %collective-permute-done.got_a = f32[72,1024]{1,0:T(8,128)S(1)} collective-permute-done((f32[72,1024]{1,0:T(8,128)S(1)}, f32[72,1024]{1,0:T(8,128)S(1)}, u32[]{:S(2)}, u32[]{:S(2)}) %collective-permute-start) | collective-permute-done | bytes 294944 | tf_op jit(solution)/shard_map/ppermute | solution.py:349
  16.1 1.0 %second.1 = (f32[2,64,1024]{2,1,0:T(8,128)S(1)}, f32[64,1024]{1,0:T(8,128)S(1)}, f32[64,1024]{1,0:T(8,128)S(1)}, f32[2,128,1024]{2,1,0:T(8,128)S(1)}) custom-call(f32[3,2048]{1,0:T(4,128)S(1)} %copy-done.4, f32[1,2048]{1,0:T(1,128)S(1)} %bitcast.1, f32[16,128,128]{2,1,0:T(8,128)S(1)} %copy-done.1, f32[72,1024]{1,0:T(8,128)S(1)} %get-tuple-element.36.d_a, ...), custom_call_target="tpu_custom_call" | custom-call | tf_op jit(solution)/shard_map/second/pallas_call | solution.py:327
  17.2 0.6 %other.1.refs_2_ = f32[2,64,1024]{2,1,0:T(8,128)S(1)} custom-call(f32[64,2048]{1,0:T(8,128)S(1)} %collective-permute-done.2.forces, f32[16,128,128]{2,1,0:T(8,128)S(1)} %copy-done.1), custom_call_target="tpu_custom_call" | custom-call | tf_op jit(solution)/shard_map/other/pallas_call | solution.py:327
  17.8 0.5 %collective-permute-start.8 = (f32[2,64,1024]{2,1,0:T(8,128)S(1)}, f32[2,64,1024]{2,1,0:T(8,128)S(1)}, u32[]{:S(2)}, u32[]{:S(2)}) collective-permute-start(f32[2,64,1024]{2,1,0:T(8,128)S(1)} %other.1.refs_2_), channel_id=1, source_target_pairs={{0,1},{1,0},{2,3},{3,2},{4,5},{5,4},{6,7},{7,6},{8,9},{9,8},{10,11... | collective-permute-start | bytes 1572872 | tf_op jit(solution)/shard_map/ppermute | solution.py:363
  18.3 2.7 %collective-permute-start.5 = (f32[64,1024]{1,0:T(8,128)S(1)}, f32[64,1024]{1,0:T(8,128)S(1)}, u32[]{:S(2)}, u32[]{:S(2)}) collective-permute-start(f32[64,1024]{1,0:T(8,128)S(1)} %get-tuple-element.40.w_a), channel_id=1, source_target_pairs={{0,4},{1,5},{2,6},{3,7},{4,0},{5,1},{6,2},{7,3},{8,12},{9,13},{10,... | collective-permute-start | bytes 786440 | tf_op jit(solution)/shard_map/ppermute | solution.py:349
  21.0 0.5 %collective-permute-start.3 = (f32[64,1024]{1,0:T(8,128)S(1)}, f32[64,1024]{1,0:T(8,128)S(1)}, u32[]{:S(2)}, u32[]{:S(2)}) collective-permute-start(f32[64,1024]{1,0:T(8,128)S(1)} %get-tuple-element.40.w_a), channel_id=1, source_target_pairs={{0,2},{1,3},{2,0},{3,1},{4,6},{5,7},{6,4},{7,5},{8,10},{9,11},{10,... | collective-permute-start | bytes 786440 | tf_op jit(solution)/shard_map/ppermute | solution.py:363
  21.5 6.0 %collective-permute-done.5.next_a = f32[64,1024]{1,0:T(8,128)S(1)} collective-permute-done((f32[64,1024]{1,0:T(8,128)S(1)}, f32[64,1024]{1,0:T(8,128)S(1)}, u32[]{:S(2)}, u32[]{:S(2)}) %collective-permute-start.5) | collective-permute-done | bytes 262176 | tf_op jit(solution)/shard_map/ppermute | solution.py:349
  27.5 0.5 %collective-permute-start.4 = (f32[64,1024]{1,0:T(8,128)S(1)}, f32[64,1024]{1,0:T(8,128)S(1)}, u32[]{:S(2)}, u32[]{:S(2)}) collective-permute-start(f32[64,1024]{1,0:T(8,128)S(1)} %get-tuple-element.41.w_b), channel_id=1, source_target_pairs={{0,2},{1,3},{2,0},{3,1},{4,6},{5,7},{6,4},{7,5},{8,10},{9,11},{10,... | collective-permute-start | bytes 786440 | tf_op jit(solution)/shard_map/ppermute | solution.py:363
  28.1 0.3 side.1.packed
  28.3 0.8 %third.1 = (f32[2,64,1024]{2,1,0:T(8,128)S(1)}, f32[8,128]{1,0:T(8,128)S(1)}) custom-call(f32[3,2048]{1,0:T(4,128)S(1)} %copy-done.4, f32[1,2048]{1,0:T(1,128)S(1)} %bitcast.2, f32[72,1024]{1,0:T(8,128)S(1)} %collective-permute-done.got_a, f32[72,1024]{1,0:T(8,128)S(1)} %collective-permute-done.1.got_b, f32[64,1024]{1,0:T(8,128)S(1)} %get-tuple-element.40.w_a, ...), custom_call_target="tpu_custom_call" | custom-call | tf_op jit(solution)/shard_map/third/pallas_call | solution.py:327
  29.1 2.9 %collective-permute-start.10 = (f32[8,128]{1,0:T(8,128)S(1)}, f32[8,128]{1,0:T(8,128)S(1)}, u32[]{:S(2)}, u32[]{:S(2)}) collective-permute-start(f32[8,128]{1,0:T(8,128)S(1)} %get-tuple-element.55.refs_0_), channel_id=1, source_target_pairs={{0,8},{4,12},{8,0},{12,4},{1,9},{5,13},{9,1},{13,5},{2,10},{6,14},... | collective-permute-start | bytes 12296 | tf_op jit(solution)/shard_map/ppermute | solution.py:363
  32.1 1.2 %collective-permute-start.11 = (f32[8,128]{1,0:T(8,128)S(1)}, f32[8,128]{1,0:T(8,128)S(1)}, u32[]{:S(2)}, u32[]{:S(2)}) collective-permute-start(f32[8,128]{1,0:T(8,128)S(1)} %get-tuple-element.55.refs_0_), channel_id=1, source_target_pairs={{0,12},{4,8},{8,4},{12,0},{1,13},{5,9},{9,5},{13,1},{2,14},{6,10},... | collective-permute-start | bytes 12296 | tf_op jit(solution)/shard_map/ppermute | solution.py:363
  33.3 1.4 %early.1 = (bf16[2,128,1024]{2,1,0:T(8,128)(2,1)S(1)}, bf16[2,128,1024]{2,1,0:T(8,128)(2,1)S(1)}, f32[2,128,128]{2,1,0:T(8,128)S(1)}, f32[128,128]{1,0:T(8,128)S(1)}) custom-call(f32[2,64,1024]{2,1,0:T(8,128)S(1)} %get-tuple-element.42.q, f32[2,64,1024]{2,1,0:T(8,128)S(1)} %get-tuple-element.48.v, f32[2,128,1024]{2,1,0:T(8,128)S(1)} %get-tuple-element.49.near.refs_0_, ...), custom_call_target="tpu_custom_call" | custom-call | tf_op jit(solution)/shard_map/early/pallas_call | solution.py:327
  34.7 0.6 %collective-permute-done.4.refs_9_ = f32[64,1024]{1,0:T(8,128)S(1)} collective-permute-done((f32[64,1024]{1,0:T(8,128)S(1)}, f32[64,1024]{1,0:T(8,128)S(1)}, u32[]{:S(2)}, u32[]{:S(2)}) %collective-permute-start.4) | collective-permute-done | bytes 262176 | tf_op jit(solution)/shard_map/ppermute | solution.py:363
  35.3 2.2 %collective-permute-done.11.refs_3_ = f32[8,128]{1,0:T(8,128)S(1)} collective-permute-done((f32[8,128]{1,0:T(8,128)S(1)}, f32[8,128]{1,0:T(8,128)S(1)}, u32[]{:S(2)}, u32[]{:S(2)}) %collective-permute-start.11) | collective-permute-done | bytes 4128 | tf_op jit(solution)/shard_map/ppermute | solution.py:363
  37.5 0.5 %collective-permute-start.13 = (f32[64,1024]{1,0:T(8,128)S(1)}, f32[64,1024]{1,0:T(8,128)S(1)}, u32[]{:S(2)}, u32[]{:S(2)}) collective-permute-start(f32[64,1024]{1,0:T(8,128)S(1)} %collective-permute-done.4.refs_9_), channel_id=1, source_target_pairs={{0,1},{1,0},{2,3},{3,2},{4,5},{5,4},{6,7},{7,6},{8,9},{9,8},{10,11... | collective-permute-start | bytes 786440 | tf_op jit(solution)/shard_map/ppermute | solution.py:363
  38.0 1.0 %collective-permute-done.12.refs_10_ = f32[64,1024]{1,0:T(8,128)S(1)} collective-permute-done((f32[64,1024]{1,0:T(8,128)S(1)}, f32[64,1024]{1,0:T(8,128)S(1)}, u32[]{:S(2)}, u32[]{:S(2)}) %collective-permute-start.12) | collective-permute-done | bytes 262176 | tf_op jit(solution)/shard_map/ppermute | solution.py:363
  39.0 0.4 collective-permute-done.13.refs_11_
  39.4 0.7 %late.1 = (f32[8,128]{1,0:T(8,128)S(1)}, f32[64,128]{1,0:T(8,128)S(1)}, f32[64,128]{1,0:T(8,128)S(1)}, f32[64,128]{1,0:T(8,128)S(1)}, f32[64,128]{1,0:T(8,128)S(1)}) custom-call(f32[8,128]{1,0:T(8,128)S(1)} %get-tuple-element.55.refs_0_, f32[8,128]{1,0:T(8,128)S(1)} %collective-permute-done.9.refs_1_, f32[8,128]{1,0:T(8,128)S(1)} %collective-permute-done.10.refs_2_, ...), custom_call_target="tpu_custom_call" | custom-call | tf_op jit(solution)/shard_map/late/pallas_call | solution.py:327
  40.1 0.1 collective-permute-start.14
  40.1 2.6 %collective-permute-start.15 = (f32[64,128]{1,0:T(8,128)S(1)}, f32[64,128]{1,0:T(8,128)S(1)}, u32[]{:S(2)}, u32[]{:S(2)}) collective-permute-start(f32[64,128]{1,0:T(8,128)S(1)} %get-tuple-element.68), channel_id=1, source_target_pairs={{0,8},{4,12},{8,0},{12,4},{1,9},{5,13},{9,1},{13,5},{2,10},{6,14},... | collective-permute-start | bytes 98312 | tf_op jit(solution)/shard_map/ppermute | solution.py:363
  42.7 1.8 %collective-permute-start.16 = (f32[64,128]{1,0:T(8,128)S(1)}, f32[64,128]{1,0:T(8,128)S(1)}, u32[]{:S(2)}, u32[]{:S(2)}) collective-permute-start(f32[64,128]{1,0:T(8,128)S(1)} %get-tuple-element.69), channel_id=1, source_target_pairs={{0,12},{4,8},{8,4},{12,0},{1,13},{5,9},{9,5},{13,1},{2,14},{6,10},... | collective-permute-start | bytes 98312 | tf_op jit(solution)/shard_map/ppermute | solution.py:363
  44.5 1.0 %modes.1 = f32[64,2048]{1,0:T(8,128)} custom-call(f32[8,128]{1,0:T(8,128)S(1)} %get-tuple-element.65.coeffs.refs_4_, f32[2,128,1024]{2,1,0:T(8,128)S(1)} %get-tuple-element.49.near.refs_0_), custom_call_target="tpu_custom_call" | custom-call | tf_op jit(solution)/shard_map/modes/pallas_call | solution.py:327
  45.5 2.0 %collective-permute-done.17.refs_5_ = f32[8,128]{1,0:T(8,128)S(1)} collective-permute-done((f32[8,128]{1,0:T(8,128)S(1)}, f32[8,128]{1,0:T(8,128)S(1)}, u32[]{:S(2)}, u32[]{:S(2)}) %collective-permute-start.17) | collective-permute-done | bytes 4128 | tf_op jit(solution)/shard_map/ppermute | solution.py:359
  47.6 0.9 %collective-permute-done.16.refs_3_ = f32[64,128]{1,0:T(8,128)S(1)} collective-permute-done((f32[64,128]{1,0:T(8,128)S(1)}, f32[64,128]{1,0:T(8,128)S(1)}, u32[]{:S(2)}, u32[]{:S(2)}) %collective-permute-start.16) | collective-permute-done | bytes 32800 | tf_op jit(solution)/shard_map/ppermute | solution.py:363
  48.4 0.7 %fifth.1 = f32[64,64]{1,0:T(8,128)} custom-call(f32[64,128]{1,0:T(8,128)S(1)} %get-tuple-element.66.refs_0_, f32[64,128]{1,0:T(8,128)S(1)} %collective-permute-done.14.refs_1_, f32[64,128]{1,0:T(8,128)S(1)} %collective-permute-done.15.refs_2_, f32[64,128]{1,0:T(8,128)S(1)} %collective-permute-done.16.refs_3_, f32[8,128]{1,0:T(8,128)S(1)} %get-tuple-element.65.coeffs.refs_4_, ...), custom_call_target="tpu_custom_call" | custom-call | tf_op jit(solution)/shard_map/fifth/pallas_call | solution.py:327
  (25 shorter events, 0.1 us)
Async XLA Ops:
  0.6 15.5 %collective-permute-start.2 = (f32[64,2048]{1,0:T(8,128)}, f32[64,2048]{1,0:T(8,128)S(1)}, u32[]{:S(2)}, u32[]{:S(2)}) collective-permute-start(f32[64,2048]{1,0:T(8,128)} %forces.3), channel_id=1, source_target_pairs={{0,2},{1,3},{2,0},{3,1},{4,6},{5,7},{6,4},{7,5},{8,10},{9,11},{10,... | collective-permute-start | bytes 1572872 | tf_op jit(solution)/shard_map/ppermute | solution.py:363
  3.6 1.2 %copy-start = (f32[16,128,128]{2,1,0:T(8,128)S(1)}, f32[16,128,128]{2,1,0:T(8,128)}, u32[]{:S(2)}) copy-start(f32[16,128,128]{2,1,0:T(8,128)} %precond.5) | copy-start | bytes 3145732
  4.9 1.0 %copy-start.2 = (f32[64,2048]{1,0:T(8,128)S(1)}, f32[64,2048]{1,0:T(8,128)}, u32[]{:S(2)}) copy-start(f32[64,2048]{1,0:T(8,128)} %forces.3) | copy-start | bytes 1572868
  5.9 0.8 %copy-start.4 = (f32[3,2048]{1,0:T(4,128)S(1)}, f32[3,2048]{1,0:T(4,128)}, u32[]{:S(2)}) copy-start(f32[3,2048]{1,0:T(4,128)} %couplings.5) | copy-start | bytes 73732
  6.7 9.5 %copy-start.1 = (f32[16,128,128]{2,1,0:T(8,128)S(1)}, f32[16,128,128]{2,1,0:T(8,128)}, u32[]{:S(2)}) copy-start(f32[16,128,128]{2,1,0:T(8,128)} %precond.5) | copy-start | bytes 3145732
  6.7 9.5 %copy-start.5 = (f32[2048]{0:T(1024)S(1)}, f32[2048]{0:T(1024)}, u32[]{:S(2)}) copy-start(f32[2048]{0:T(1024)} %param.6) | copy-start | bytes 24580
  7.6 8.5 %collective-permute-start = (f32[72,1024]{1,0:T(8,128)S(1)}, f32[72,1024]{1,0:T(8,128)S(1)}, u32[]{:S(2)}, u32[]{:S(2)}) collective-permute-start(f32[72,1024]{1,0:T(8,128)S(1)} %get-tuple-element.36.d_a), channel_id=1, source_target_pairs={{0,4},{1,5},{2,6},{3,7},{4,0},{5,1},{6,2},{7,3},{8,12},{9,13},{10,... | collective-permute-start | bytes 884744 | tf_op jit(solution)/shard_map/ppermute | solution.py:349
  9.2 6.9 %collective-permute-start.1 = (f32[72,1024]{1,0:T(8,128)S(1)}, f32[72,1024]{1,0:T(8,128)S(1)}, u32[]{:S(2)}, u32[]{:S(2)}) collective-permute-start(f32[72,1024]{1,0:T(8,128)S(1)} %get-tuple-element.37.d_b), channel_id=1, source_target_pairs={{0,1},{1,0},{2,3},{3,2},{4,8},{5,9},{6,10},{7,11},{8,4},{9,5},{10,... | collective-permute-start | bytes 884744 | tf_op jit(solution)/shard_map/ppermute | solution.py:349
  17.1 10.9 %copy-start.3 = (f32[64,2048]{1,0:T(8,128)S(1)}, f32[64,2048]{1,0:T(8,128)}, u32[]{:S(2)}) copy-start(f32[64,2048]{1,0:T(8,128)} %forces.3) | copy-start | bytes 1572868
  17.1 11.2 %collective-permute-start.7 = (f32[2,128,1024]{2,1,0:T(8,128)S(1)}, f32[2,128,1024]{2,1,0:T(8,128)S(1)}, u32[]{:S(2)}, u32[]{:S(2)}) collective-permute-start(f32[2,128,1024]{2,1,0:T(8,128)S(1)} %get-tuple-element.49.near.refs_0_), channel_id=1, source_target_pairs={{0,1},{1,0},{2,3},{3,2},{4,5},{5,4},{6,7},{7,6},{8,9},{9,8},{10,11... | collective-permute-start | bytes 3145736 | tf_op jit(solution)/shard_map/ppermute | solution.py:363
  17.8 10.6 %collective-permute-start.8 = (f32[2,64,1024]{2,1,0:T(8,128)S(1)}, f32[2,64,1024]{2,1,0:T(8,128)S(1)}, u32[]{:S(2)}, u32[]{:S(2)}) collective-permute-start(f32[2,64,1024]{2,1,0:T(8,128)S(1)} %other.1.refs_2_), channel_id=1, source_target_pairs={{0,1},{1,0},{2,3},{3,2},{4,5},{5,4},{6,7},{7,6},{8,9},{9,8},{10,11... | collective-permute-start | bytes 1572872 | tf_op jit(solution)/shard_map/ppermute | solution.py:363
  18.3 9.2 %collective-permute-start.5 = (f32[64,1024]{1,0:T(8,128)S(1)}, f32[64,1024]{1,0:T(8,128)S(1)}, u32[]{:S(2)}, u32[]{:S(2)}) collective-permute-start(f32[64,1024]{1,0:T(8,128)S(1)} %get-tuple-element.40.w_a), channel_id=1, source_target_pairs={{0,4},{1,5},{2,6},{3,7},{4,0},{5,1},{6,2},{7,3},{8,12},{9,13},{10,... | collective-permute-start | bytes 786440 | tf_op jit(solution)/shard_map/ppermute | solution.py:349
  21.0 7.4 %collective-permute-start.6 = (f32[64,1024]{1,0:T(8,128)S(1)}, f32[64,1024]{1,0:T(8,128)S(1)}, u32[]{:S(2)}, u32[]{:S(2)}) collective-permute-start(f32[64,1024]{1,0:T(8,128)S(1)} %get-tuple-element.41.w_b), channel_id=1, source_target_pairs={{0,1},{1,0},{2,3},{3,2},{4,8},{5,9},{6,10},{7,11},{8,4},{9,5},{10,... | collective-permute-start | bytes 786440 | tf_op jit(solution)/shard_map/ppermute | solution.py:349
  21.0 13.7 %collective-permute-start.3 = (f32[64,1024]{1,0:T(8,128)S(1)}, f32[64,1024]{1,0:T(8,128)S(1)}, u32[]{:S(2)}, u32[]{:S(2)}) collective-permute-start(f32[64,1024]{1,0:T(8,128)S(1)} %get-tuple-element.40.w_a), channel_id=1, source_target_pairs={{0,2},{1,3},{2,0},{3,1},{4,6},{5,7},{6,4},{7,5},{8,10},{9,11},{10,... | collective-permute-start | bytes 786440 | tf_op jit(solution)/shard_map/ppermute | solution.py:363
  27.5 7.8 %collective-permute-start.4 = (f32[64,1024]{1,0:T(8,128)S(1)}, f32[64,1024]{1,0:T(8,128)S(1)}, u32[]{:S(2)}, u32[]{:S(2)}) collective-permute-start(f32[64,1024]{1,0:T(8,128)S(1)} %get-tuple-element.41.w_b), channel_id=1, source_target_pairs={{0,2},{1,3},{2,0},{3,1},{4,6},{5,7},{6,4},{7,5},{8,10},{9,11},{10,... | collective-permute-start | bytes 786440 | tf_op jit(solution)/shard_map/ppermute | solution.py:363
  29.1 6.2 %collective-permute-start.10 = (f32[8,128]{1,0:T(8,128)S(1)}, f32[8,128]{1,0:T(8,128)S(1)}, u32[]{:S(2)}, u32[]{:S(2)}) collective-permute-start(f32[8,128]{1,0:T(8,128)S(1)} %get-tuple-element.55.refs_0_), channel_id=1, source_target_pairs={{0,8},{4,12},{8,0},{12,4},{1,9},{5,13},{9,1},{13,5},{2,10},{6,14},... | collective-permute-start | bytes 12296 | tf_op jit(solution)/shard_map/ppermute | solution.py:363
  32.1 5.4 %collective-permute-start.11 = (f32[8,128]{1,0:T(8,128)S(1)}, f32[8,128]{1,0:T(8,128)S(1)}, u32[]{:S(2)}, u32[]{:S(2)}) collective-permute-start(f32[8,128]{1,0:T(8,128)S(1)} %get-tuple-element.55.refs_0_), channel_id=1, source_target_pairs={{0,12},{4,8},{8,4},{12,0},{1,13},{5,9},{9,5},{13,1},{2,14},{6,10},... | collective-permute-start | bytes 12296 | tf_op jit(solution)/shard_map/ppermute | solution.py:363
  33.3 4.2 %collective-permute-start.9 = (f32[8,128]{1,0:T(8,128)S(1)}, f32[8,128]{1,0:T(8,128)S(1)}, u32[]{:S(2)}, u32[]{:S(2)}) collective-permute-start(f32[8,128]{1,0:T(8,128)S(1)} %get-tuple-element.55.refs_0_), channel_id=1, source_target_pairs={{0,4},{4,0},{8,12},{12,8},{1,5},{5,1},{9,13},{13,9},{2,6},{6,2},{1... | collective-permute-start | bytes 12296 | tf_op jit(solution)/shard_map/ppermute | solution.py:363
  37.5 1.5 %collective-permute-start.12 = (f32[64,1024]{1,0:T(8,128)S(1)}, f32[64,1024]{1,0:T(8,128)S(1)}, u32[]{:S(2)}, u32[]{:S(2)}) collective-permute-start(f32[64,1024]{1,0:T(8,128)S(1)} %collective-permute-done.3.refs_8_), channel_id=1, source_target_pairs={{0,1},{1,0},{2,3},{3,2},{4,5},{5,4},{6,7},{7,6},{8,9},{9,8},{10,11... | collective-permute-start | bytes 786440 | tf_op jit(solution)/shard_map/ppermute | solution.py:363
  37.5 1.9 %collective-permute-start.13 = (f32[64,1024]{1,0:T(8,128)S(1)}, f32[64,1024]{1,0:T(8,128)S(1)}, u32[]{:S(2)}, u32[]{:S(2)}) collective-permute-start(f32[64,1024]{1,0:T(8,128)S(1)} %collective-permute-done.4.refs_9_), channel_id=1, source_target_pairs={{0,1},{1,0},{2,3},{3,2},{4,5},{5,4},{6,7},{7,6},{8,9},{9,8},{10,11... | collective-permute-start | bytes 786440 | tf_op jit(solution)/shard_map/ppermute | solution.py:363
  40.1 7.5 %collective-permute-start.14 = (f32[64,128]{1,0:T(8,128)S(1)}, f32[64,128]{1,0:T(8,128)S(1)}, u32[]{:S(2)}, u32[]{:S(2)}) collective-permute-start(f32[64,128]{1,0:T(8,128)S(1)} %get-tuple-element.67), channel_id=1, source_target_pairs={{0,4},{4,0},{8,12},{12,8},{1,5},{5,1},{9,13},{13,9},{2,6},{6,2},{1... | collective-permute-start | bytes 98312 | tf_op jit(solution)/shard_map/ppermute | solution.py:363
  40.1 7.4 %collective-permute-start.15 = (f32[64,128]{1,0:T(8,128)S(1)}, f32[64,128]{1,0:T(8,128)S(1)}, u32[]{:S(2)}, u32[]{:S(2)}) collective-permute-start(f32[64,128]{1,0:T(8,128)S(1)} %get-tuple-element.68), channel_id=1, source_target_pairs={{0,8},{4,12},{8,0},{12,4},{1,9},{5,13},{9,1},{13,5},{2,10},{6,14},... | collective-permute-start | bytes 98312 | tf_op jit(solution)/shard_map/ppermute | solution.py:363
  42.7 5.7 %collective-permute-start.16 = (f32[64,128]{1,0:T(8,128)S(1)}, f32[64,128]{1,0:T(8,128)S(1)}, u32[]{:S(2)}, u32[]{:S(2)}) collective-permute-start(f32[64,128]{1,0:T(8,128)S(1)} %get-tuple-element.69), channel_id=1, source_target_pairs={{0,12},{4,8},{8,4},{12,0},{1,13},{5,9},{9,5},{13,1},{2,14},{6,10},... | collective-permute-start | bytes 98312 | tf_op jit(solution)/shard_map/ppermute | solution.py:363
  44.5 3.0 %collective-permute-start.17 = (f32[8,128]{1,0:T(8,128)S(1)}, f32[8,128]{1,0:T(8,128)S(1)}, u32[]{:S(2)}, u32[]{:S(2)}) collective-permute-start(f32[8,128]{1,0:T(8,128)S(1)} %get-tuple-element.65.coeffs.refs_4_), channel_id=1, source_target_pairs={{0,5},{1,4},{2,8},{3,12},{4,1},{5,0},{6,9},{7,13},{8,2},{9,6},{10,... | collective-permute-start | bytes 12296 | tf_op jit(solution)/shard_map/ppermute | solution.py:359

commit v3 on v2

--- a/solution.py
+++ b/solution.py
@@ -18,7 +18,7 @@
 
 def slot_planes():
     odd = lax.rem(lax.axis_index("nodes"), 2)
-    return 1 - odd, odd
+    return odd, 1 - odd
 
 
 def split(x):
@@ -91,7 +91,10 @@
     return result
 
 
-def all_springs(couplings, ground, got, rows):
+def all_springs(couplings, ground, got):
+    def row_before(slot, k):
+        return jnp.broadcast_to(got[slot][0:1, chunk(k)], (8, LANES))
+
     place, count = lax.axis_index("nodes"), lax.axis_size("nodes")
     odd = lax.rem(place, 2)
     own, mid = [], []
@@ -104,12 +107,12 @@
         mid.append(jnp.broadcast_to(couplings[2:3, chunk(k)], (8, LANES)))
     result = []
     for slot, plane in enumerate(slot_planes()):
-        below = odd == (1 - slot)
+        below = odd == slot
         meets = jnp.where(below, place > 0, place < count - 1)
         crossing = [
             jnp.where(
                 below,
-                jnp.where(place > 0, got[slot][rows : rows + 8, chunk(k)], 0.0),
+                jnp.where(place > 0, row_before(slot, k), 0.0),
                 own[k],
             )
             for k in range(CHUNKS)
@@ -136,8 +139,8 @@
     return result.reshape(rows, LANES)
 
 
-def first_kernel(forces, couplings, precond, out_a, out_b, field, matrices, springs, sems):
-    rows = forces.shape[0]
+def first_kernel(forces, precond, out_a, out_b, first_rows, field, matrices, sems):
+    early = first_rows.shape[1]
     copies = []
     for slot, plane in enumerate(slot_planes()):
         here = pl.ds(pl.multiple_of(plane * PLANE, PLANE), PLANE)
@@ -149,35 +152,22 @@
                 ),
             )
         )
-    spring_copy = pltpu.make_async_copy(couplings, springs, sems.at[2, 0])
     for pair in copies:
         for copy in pair:
             copy.start()
-    spring_copy.start()
     for slot, out in enumerate((out_a, out_b)):
         for copy in copies[slot]:
             copy.wait()
         for k in range(CHUNKS):
-            out[0:rows, chunk(k)] = block_product(field[slot, :, chunk(k)], matrices[slot, k])
-    spring_copy.wait()
-    for out in (out_a, out_b):
-        for k in range(CHUNKS):
-            out[rows : rows + 8, chunk(k)] = jnp.broadcast_to(
-                springs[2:3, PLANE + k * LANES : PLANE + (k + 1) * LANES], (8, LANES)
-            )
-
-
-def other_kernel(forces, precond, out):
-    for slot, plane in enumerate(slot_planes()):
-        for k in range(CHUNKS):
-            out[slot, :, chunk(k)] = block_product(
-                forces[:, plane_chunk(plane, k)], precond[plane * CHUNKS + k]
-            )
-
-
-def second_kernel(couplings, ground, precond, d_a, d_b, got_a, got_b, q, w_a, w_b, near):
+            d = block_product(field[slot, :, chunk(k)], matrices[slot, k])
+            out[:, chunk(k)] = d
+            first_rows[slot, :, chunk(k)] = d[0:early]
+
+
+def second_kernel(couplings, ground, before_a, before_b, precond, d_a, d_b, got_a, got_b, q, w_a, w_b, beside, near):
     rows = w_a.shape[0]
-    springs = all_springs(couplings, ground, (got_a, got_b), rows)
+    early = 2 * rows - beside.shape[1]
+    springs = all_springs(couplings, ground, (before_a, before_b))
     fields = (d_a, d_b)
     for slot, plane in enumerate(slot_planes()):
         for k in range(CHUNKS):
@@ -187,7 +177,9 @@
             q[slot, :, chunk(k)] = image
             w = block_product(image, precond[plane * CHUNKS + k])
             (w_a, w_b)[slot][:, chunk(k)] = w
-            near[slot, 0:rows, chunk(k)] = fields[slot][0:rows, chunk(k)]
+            beside[slot, 0:rows, chunk(k)] = w
+            beside[slot, rows:, chunk(k)] = fields[slot][early:, chunk(k)]
+            near[slot, 0:rows, chunk(k)] = fields[slot][:, chunk(k)]
             near[slot, rows : 2 * rows, chunk(k)] = w
 
 
@@ -212,9 +204,9 @@
     packed[...] = place_sums(jnp.zeros((rows, LANES), F32), 0, sums)
 
 
-def third_kernel(couplings, ground, got_a, got_b, w_a, w_b, next_a, next_b, packed, v, dots):
+def third_kernel(couplings, ground, before_a, before_b, w_a, w_b, next_a, next_b, packed, v, dots):
     rows = w_a.shape[0]
-    springs = all_springs(couplings, ground, (got_a, got_b), rows)
+    springs = all_springs(couplings, ground, (before_a, before_b))
     fields = (w_a, w_b)
     total = jnp.zeros((rows, LANES), F32)
     for slot in range(2):
@@ -230,8 +222,8 @@
     dots[...] = values.T[0:8, :]
 
 
-def columns_of(field, slot, rows):
-    return jnp.concatenate([part[slot, 0:rows, :] for part in field], axis=0)
+def columns_of(fields, slot):
+    return jnp.concatenate([field[slot] for field in fields], axis=0)
 
 
 def early_kernel(n_near, n_far, q, v, *refs):
@@ -245,23 +237,15 @@
         for i in range(n_near):
             term = product(images, split(near[i][slot]), ((1,), (1,)))
             near_sums[i] = term if slot == 0 else near_sums[i] + term
-        term = product(images, split(columns_of(d_far, slot, rows)), ((1,), (1,)))
+        term = product(images, split(columns_of(d_far, slot)), ((1,), (1,)))
         far_sum = term if slot == 0 else far_sum + term
     for i in range(n_near):
         near_gram[i] = near_sums[i]
     far_gram[...] = far_sum
 
 
-def late_kernel(n_dots, n_near, n_far, exchange, *refs):
-    dots, refs = refs[:n_dots], refs[n_dots:]
-    qv_high, qv_low, near_gram, far_gram, refs = *refs[:4], refs[4:]
-    w_far, coeffs, outs, gram = refs[: 2 * n_far], refs[2 * n_far], refs[2 * n_far + 1 : -1], refs[-1]
-    rows = near_gram.shape[1] // 2
-    far_sum = None
-    for slot in range(2):
-        columns = jnp.concatenate([w_far[2 * i + slot][...] for i in range(n_far)], axis=0)
-        term = product((qv_high[slot], qv_low[slot]), split(columns), ((1,), (1,)))
-        far_sum = term if slot == 0 else far_sum + term
+def coeffs_kernel(rows, *refs):
+    dots, coeffs = refs[:-1], refs[-1]
     total = dots[0][...]
     for piece in dots[1:]:
         total = total + piece[...]
@@ -274,16 +258,35 @@
     used = lane_index(1) < rows
     on_d = jnp.where(used, alpha0 + alpha1 * grow, 0.0)
     on_w = jnp.where(used, -alpha0 * alpha1, 0.0)
-    coeffs[...] = jnp.concatenate([on_d, on_w, jnp.zeros((6, LANES), F32)], axis=0)
+    pair = jnp.concatenate([on_d, on_w, jnp.zeros((6, LANES), F32)], axis=0)
+    for i in range(coeffs.shape[0] // 8):
+        coeffs[8 * i : 8 * i + 8, :] = pair
+
+
+def late_kernel(n_near, n_far, exchange, coeffs, qv_high, qv_low, near_gram, far_gram, *refs):
+    far, outs, gram = refs[:n_far], refs[n_far:-1], refs[-1]
+    rows = near_gram.shape[1] // 2
+    far_sum = None
+    for slot in range(2):
+        images = (qv_high[slot], qv_low[slot])
+        term = product(images, split(columns_of(far, slot)), ((1,), (1,)))
+        far_sum = term if slot == 0 else far_sum + term
     p, s = turned(coeffs, rows)
     if not exchange:
         gram = outs[0]
     for i in range(n_near):
         gram[i] = p * near_gram[i, 0:rows] + s * near_gram[i, rows : 2 * rows]
-    d_part, w_part = far_gram[...], far_sum
+    first_part = far_gram[...]
+    early, width = first_part.shape[1] // n_far, far[0].shape[1]
     for i in range(n_far):
-        there = slice(i * rows, (i + 1) * rows)
-        both = jnp.concatenate([d_part[:, there], w_part[:, there]], axis=1)
+        both = jnp.concatenate(
+            [
+                first_part[:, i * early : (i + 1) * early],
+                far_sum[:, i * width + rows : (i + 1) * width],
+                far_sum[:, i * width : i * width + rows],
+            ],
+            axis=1,
+        )
         gram[n_near + i] = p * both[0:rows] + s * both[rows : 2 * rows]
     if exchange:
         mine = lax.axis_index("nodes") ^ lax.axis_index("cols")
@@ -292,7 +295,7 @@
 
 
 def turned(coeffs, rows):
-    table = jnp.concatenate([coeffs[...], jnp.zeros((LANES - 8, LANES), F32)], axis=0).T
+    table = jnp.concatenate([coeffs[0:8, :], jnp.zeros((LANES - 8, LANES), F32)], axis=0).T
     return [jnp.broadcast_to(table[0:rows, i : i + 1], (rows, LANES)) for i in range(2)]
 
 
@@ -313,7 +316,7 @@
     for piece in sums[1:]:
         total = total + piece[...]
     here = lax.axis_index("nodes") == lax.axis_index("cols")
-    coeffs = jnp.where(here, own[...], theirs[...])
+    coeffs = jnp.where(here, own[0:8, :], theirs[0:8, :])
     tile[...] = (
         coeffs[0:1, 0:rows] * total[:, 0:rows] + coeffs[1:2, 0:rows] * total[:, rows : 2 * rows]
     ) * scale
@@ -380,46 +383,46 @@
         return [held[key] for key in range(max(top, 1))]
 
     field = (rows, PLANE)
-    d_a, d_b = call(
+    early = rows * 3 // 4
+    d_a, d_b, d_far = call(
         first_kernel,
         "first",
-        (forces, couplings, precond),
-        [(rows + 8, PLANE)] * 2,
+        [pltpu.with_memory_space_constraint(x, pltpu.HBM) for x in (forces, precond)],
+        [field, field, (2, early, PLANE)],
         [
             pltpu.VMEM((2, rows, PLANE), F32),
             pltpu.VMEM((2, CHUNKS, LANES, LANES), F32),
-            pltpu.VMEM(couplings.shape, F32),
-            pltpu.SemaphoreType.DMA((3, 2)),
+            pltpu.SemaphoreType.DMA((2, 2)),
         ],
-        pl.ANY,
-    )
-    got_a, got_b = neighbours(d_a, 0), neighbours(d_b, 1)
-    forces_far = swapped(forces, "cols", top)
-    got_a, got_b, forces_far = lax.optimization_barrier((got_a, got_b, forces_far))
-    q, w_a, w_b, near = call(
+        pltpu.HBM,
+    )
+    got_a, got_b = neighbours(d_a, 1), neighbours(d_b, 0)
+    d_far = swapped(d_far, "cols", top)
+    last = couplings[2:3, length - PLANE :]
+    before_a, before_b = neighbours(last, 1), neighbours(last, 0)
+    got_a, got_b, d_far = lax.optimization_barrier((got_a, got_b, d_far))
+    edges = (couplings, ground, before_a, before_b)
+    q, w_a, w_b, beside, near = call(
         second_kernel,
         "second",
-        (couplings, ground, precond, d_a, d_b, got_a, got_b),
-        [(2,) + field, field, field, (2, 2 * rows, PLANE)],
-    )
-    next_a, next_b = neighbours(w_a, 0), neighbours(w_b, 1)
-    w_far_a, w_far_b = swapped(w_a, "cols", top), swapped(w_b, "cols", top)
+        (*edges, precond, d_a, d_b, got_a, got_b),
+        [(2,) + field, field, field, (2, 2 * rows - early, PLANE), (2, 2 * rows, PLANE)],
+    )
+    next_a, next_b = neighbours(w_a, 1), neighbours(w_b, 0)
+    far = swapped(beside, "cols", top)
     near = shared(near)
-    (d_far,) = call(other_kernel, "other", (forces_far, precond), [(2,) + field])
+    next_a, next_b, d_far, near = lax.optimization_barrier((next_a, next_b, d_far, near))
     d_far = shared(d_far)
     (packed,) = call(side_kernel, "side", (forces, q, near[0]), [(rows, LANES)])
-    next_a, next_b, near, d_far, packed = lax.optimization_barrier(
-        (next_a, next_b, near, d_far, packed)
-    )
     v, dots = call(
         third_kernel,
         "third",
-        (couplings, ground, got_a, got_b, w_a, w_b, next_a, next_b, packed),
+        (*edges, w_a, w_b, next_a, next_b, packed),
         [(2,) + field, (8, LANES)],
     )
     exchange = nodes == cols
     if exchange:
-        dots = [dots] + [swapped(dots, "nodes", i) for i in range(1, nodes)]
+        dots = [dots] + [swapped(dots, "nodes", i) for i in reversed(range(1, nodes))]
     else:
         dots = [lax.psum(dots, "nodes")]
     halves = jax.ShapeDtypeStruct((2, 2 * rows, PLANE), jnp.bfloat16)
@@ -427,24 +430,23 @@
         functools.partial(early_kernel, len(near), len(d_far)),
         "early",
         (q, v, *near, *d_far),
-        [halves, halves, (len(near), 2 * rows, 2 * rows), (2 * rows, len(d_far) * rows)],
-    )
-    w_far_a, w_far_b, near_gram, *dots = lax.optimization_barrier(
-        (w_far_a, w_far_b, near_gram, *dots)
-    )
-    w_far = [x for pair in zip(shared(w_far_a), shared(w_far_b)) for x in pair]
-    coeffs, *grams = call(
-        functools.partial(late_kernel, len(dots), len(near), len(d_far), exchange),
+        [halves, halves, (len(near), 2 * rows, 2 * rows), (2 * rows, len(d_far) * early)],
+    )
+    far, near_gram, *dots = lax.optimization_barrier((far, near_gram, *dots))
+    far = shared(far)
+    (coeffs,) = call(functools.partial(coeffs_kernel, rows), "coeffs", dots, [(rows + 8, LANES)])
+    grams = call(
+        functools.partial(late_kernel, len(near), len(d_far), exchange),
         "late",
-        (*dots, qv_high, qv_low, near_gram, far_gram, *w_far),
-        [(8, LANES)] + ([(rows, LANES)] * cols if exchange else [(cols, rows, LANES)]),
+        (coeffs, qv_high, qv_low, near_gram, far_gram, *far),
+        [(rows, LANES)] * cols if exchange else [(cols, rows, LANES)],
         [pltpu.VMEM((cols, rows, LANES), F32)],
     )
+    scale = 1.0 / (length * nodes)
     (modes,) = call(modes_kernel, "modes", (coeffs, near[0]), [(rows, length)])
-    scale = 1.0 / (length * nodes)
     if exchange:
         theirs = transposed(coeffs)
-        sums = [grams[0]] + [swapped(grams[i], "nodes", i) for i in range(1, nodes)]
+        sums = [grams[0]] + [swapped(grams[i], "nodes", i) for i in reversed(range(1, nodes))]
         (tile,) = call(
             functools.partial(fifth_kernel, scale, nodes),
             "fifth",

time: 49.5 us -> 47.5 us (0.960)
  starting transfers between devices: 18.1 us -> 22.2 us
  waiting for transfers between devices: 20 us -> 16.4 us
  local copies, waits for them, and re-layouts: 3.04 us -> 0.03 us
  Pallas kernels: 7.31 us -> 8.01 us
    ppermute x4 -> x6, starting transfers between devices: 4.34 us -> 8.26 us  [neighbours(): return lax.ppermute(block, ('nodes', 'cols'), route)]
    ppermute x4 -> x6, waiting for transfers between devices: 12.9 us -> 9.27 us  [neighbours(): return lax.ppermute(block, ('nodes', 'cols'), route)]
    unnamed x12 -> x8, local copies, waits for them, and re-layouts: 3.04 us -> 0.02 us
    ppermute x13 -> x11, waiting for transfers between devices: 5.04 us -> 7.1 us  [swapped(): lax.ppermute(block, axis, [(i, i ^ bit) for i in range(lax.axis_size(axis...]
    ppermute x1, waiting for transfers between devices: 2.03 us -> 0.01 us  [transposed(): return lax.ppermute(block, ('nodes', 'cols'), route)]
    pallas_call x9, Pallas kernels: 7.31 us -> 8.01 us  [call(): pl.pallas_call(kernel, out_shape=shapes, in_specs=[pl.BlockSpec(memory_sp...]
    ppermute x13 -> x11, starting transfers between devices: 13.7 us -> 13.5 us  [swapped(): lax.ppermute(block, axis, [(i, i ^ bit) for i in range(lax.axis_size(axis...]
  transfers between devices with their start and end apart: 18 -> 18, of which waited for: 8 -> 7; matrix products, arithmetic and copies ran while one was open for 0% -> 0% of each run, Pallas kernels for 10% -> 9%
where the time goes in v3:
time: 47.5 us; the launch traced here: 47.4 us
  starting transfers between devices  22.2 us (47%)
  waiting for transfers between devices  16.4 us (35%)
  Pallas kernels  8.01 us (17%)
  between operations  0.76 us (2%)
    ppermute x11, starting transfers between devices, swapped(): lax.ppermute(block, axis, [(i, i ^ bit) for i in range(lax.axis_size(axis...  13.5 us
    ppermute x6, waiting for transfers between devices, neighbours(): return lax.ppermute(block, ('nodes', 'cols'), route)  9.27 us
    ppermute x6, starting transfers between devices, neighbours(): return lax.ppermute(block, ('nodes', 'cols'), route)  8.26 us
    pallas_call x9, Pallas kernels, call(): pl.pallas_call(kernel, out_shape=shapes, in_specs=[pl.BlockSpec(memory_sp...  8.01 us
    ppermute x11, waiting for transfers between devices, swapped(): lax.ppermute(block, axis, [(i, i ^ bit) for i in range(lax.axis_size(axis...  7.1 us
  transfers between devices with their start and end apart: 18, of which 7 were waited for; matrix products, arithmetic and copies ran while one was open for 0% of the time, Pallas kernels for 9%

profile of v3, /device:TPU:0, one launch (start us, length us, event | category | flops | bytes accessed | tf_op | source)
XLA Modules:
  0.0 47.4 jit_solution(3193179008044994224)
XLA Ops:
  0.6 1.9 %first.1 = (f32[64,1024]{1,0:T(8,128)S(1)}, f32[64,1024]{1,0:T(8,128)S(1)}, f32[2,48,1024]{2,1,0:T(8,128)S(1)}) custom-call(f32[64,2048]{1,0:T(8,128)} %forces.3, f32[16,128,128]{2,1,0:T(8,128)} %precond.3), custom_call_target="tpu_custom_call" | custom-call | tf_op jit(solution)/shard_map/first/pallas_call | solution.py:330
  2.6 0.0 copy-start.3
  2.6 3.0 %collective-permute-start.4 = (f32[2,48,1024]{2,1,0:T(8,128)S(1)}, f32[2,48,1024]{2,1,0:T(8,128)S(1)}, u32[]{:S(2)}, u32[]{:S(2)}) collective-permute-start(f32[2,48,1024]{2,1,0:T(8,128)S(1)} %get-tuple-element.36), channel_id=1, source_target_pairs={{0,2},{1,3},{2,0},{3,1},{4,6},{5,7},{6,4},{7,5},{8,10},{9,11},{10,... | collective-permute-start | bytes 1179656 | tf_op jit(solution)/shard_map/ppermute | solution.py:366
  5.6 3.2 %collective-permute-start.3 = (f32[64,1024]{1,0:T(8,128)S(1)}, f32[64,1024]{1,0:T(8,128)S(1)}, u32[]{:S(2)}, u32[]{:S(2)}) collective-permute-start(f32[64,1024]{1,0:T(8,128)S(1)} %get-tuple-element.35.d_b), channel_id=1, source_target_pairs={{0,4},{1,5},{2,6},{3,7},{4,0},{5,1},{6,2},{7,3},{8,12},{9,13},{10,... | collective-permute-start | bytes 786440 | tf_op jit(solution)/shard_map/ppermute | solution.py:352
  8.8 0.1 collective-permute-start
  8.9 1.6 %collective-permute-start.1 = (f32[1,1024]{1,0:T(1,128)S(1)}, f32[1,1024]{1,0:T(1,128)S(1)}, u32[]{:S(2)}, u32[]{:S(2)}) collective-permute-start(f32[1,1024]{1,0:T(1,128)S(1)} %slice.3), channel_id=1, source_target_pairs={{0,4},{1,5},{2,6},{3,7},{4,0},{5,1},{6,2},{7,3},{8,12},{9,13},{10,... | collective-permute-start | bytes 12296 | tf_op jit(solution)/shard_map/ppermute | solution.py:352
  10.4 4.1 %collective-permute-done.3.got_b = f32[64,1024]{1,0:T(8,128)S(1)} collective-permute-done((f32[64,1024]{1,0:T(8,128)S(1)}, f32[64,1024]{1,0:T(8,128)S(1)}, u32[]{:S(2)}, u32[]{:S(2)}) %collective-permute-start.3) | collective-permute-done | bytes 262176 | tf_op jit(solution)/shard_map/ppermute | solution.py:352
  14.6 0.2 collective-permute-done.4.refs_2_
  14.8 0.0 copy-start.1
  14.8 1.0 %second.1 = (f32[2,64,1024]{2,1,0:T(8,128)S(1)}, f32[64,1024]{1,0:T(8,128)S(1)}, f32[64,1024]{1,0:T(8,128)S(1)}, f32[2,80,1024]{2,1,0:T(8,128)S(1)}, f32[2,128,1024]{2,1,0:T(8,128)S(1)}) custom-call(f32[3,2048]{1,0:T(4,128)S(1)} %copy-done.2, f32[1,2048]{1,0:T(1,128)S(1)} %bitcast.1, f32[1,1024]{1,0:T(1,128)S(1)} %collective-permute-done.before_a, ...), custom_call_target="tpu_custom_call" | custom-call | tf_op jit(solution)/shard_map/second/pallas_call | solution.py:330
  15.8 0.1 collective-permute-start.8
  15.9 0.5 %collective-permute-start.6 = (f32[64,1024]{1,0:T(8,128)S(1)}, f32[64,1024]{1,0:T(8,128)S(1)}, u32[]{:S(2)}, u32[]{:S(2)}) collective-permute-start(f32[64,1024]{1,0:T(8,128)S(1)} %get-tuple-element.41.w_a), channel_id=1, source_target_pairs={{0,1},{1,0},{2,3},{3,2},{4,8},{5,9},{6,10},{7,11},{8,4},{9,5},{10,... | collective-permute-start | bytes 786440 | tf_op jit(solution)/shard_map/ppermute | solution.py:352
  16.3 3.0 %collective-permute-start.7 = (f32[64,1024]{1,0:T(8,128)S(1)}, f32[64,1024]{1,0:T(8,128)S(1)}, u32[]{:S(2)}, u32[]{:S(2)}) collective-permute-start(f32[64,1024]{1,0:T(8,128)S(1)} %get-tuple-element.42.w_b), channel_id=1, source_target_pairs={{0,4},{1,5},{2,6},{3,7},{4,0},{5,1},{6,2},{7,3},{8,12},{9,13},{10,... | collective-permute-start | bytes 786440 | tf_op jit(solution)/shard_map/ppermute | solution.py:352
  19.3 1.5 %collective-permute-start.5 = (f32[2,80,1024]{2,1,0:T(8,128)S(1)}, f32[2,80,1024]{2,1,0:T(8,128)S(1)}, u32[]{:S(2)}, u32[]{:S(2)}) collective-permute-start(f32[2,80,1024]{2,1,0:T(8,128)S(1)} %get-tuple-element.39), channel_id=1, source_target_pairs={{0,2},{1,3},{2,0},{3,1},{4,6},{5,7},{6,4},{7,5},{8,10},{9,11},{10,... | collective-permute-start | bytes 1966088 | tf_op jit(solution)/shard_map/ppermute | solution.py:366
  20.8 5.1 %collective-permute-done.7.next_b = f32[64,1024]{1,0:T(8,128)S(1)} collective-permute-done((f32[64,1024]{1,0:T(8,128)S(1)}, f32[64,1024]{1,0:T(8,128)S(1)}, u32[]{:S(2)}, u32[]{:S(2)}) %collective-permute-start.7) | collective-permute-done | bytes 262176 | tf_op jit(solution)/shard_map/ppermute | solution.py:352
  26.0 0.3 side.1.packed
  26.2 0.8 %third.1 = (f32[2,64,1024]{2,1,0:T(8,128)S(1)}, f32[8,128]{1,0:T(8,128)S(1)}) custom-call(f32[3,2048]{1,0:T(4,128)S(1)} %copy-done.2, f32[1,2048]{1,0:T(1,128)S(1)} %bitcast.2, f32[1,1024]{1,0:T(1,128)S(1)} %collective-permute-done.before_a, f32[1,1024]{1,0:T(1,128)S(1)} %collective-permute-done.1.before_b, f32[64,1024]{1,0:T(8,128)S(1)} %get-tuple-element.41.w_a, ...), custom_call_target="tpu_custom_call" | custom-call | tf_op jit(solution)/shard_map/third/pallas_call | solution.py:330
  27.0 2.5 %collective-permute-start.10 = (f32[8,128]{1,0:T(8,128)S(1)}, f32[8,128]{1,0:T(8,128)S(1)}, u32[]{:S(2)}, u32[]{:S(2)}) collective-permute-start(f32[8,128]{1,0:T(8,128)S(1)} %get-tuple-element.53.refs_0_), channel_id=1, source_target_pairs={{0,12},{4,8},{8,4},{12,0},{1,13},{5,9},{9,5},{13,1},{2,14},{6,10},... | collective-permute-start | bytes 12296 | tf_op jit(solution)/shard_map/ppermute | solution.py:366
  29.6 0.7 %collective-permute-start.11 = (f32[8,128]{1,0:T(8,128)S(1)}, f32[8,128]{1,0:T(8,128)S(1)}, u32[]{:S(2)}, u32[]{:S(2)}) collective-permute-start(f32[8,128]{1,0:T(8,128)S(1)} %get-tuple-element.53.refs_0_), channel_id=1, source_target_pairs={{0,8},{4,12},{8,0},{12,4},{1,9},{5,13},{9,1},{13,5},{2,10},{6,14},... | collective-permute-start | bytes 12296 | tf_op jit(solution)/shard_map/ppermute | solution.py:366
  30.2 1.2 %collective-permute-start.12 = (f32[8,128]{1,0:T(8,128)S(1)}, f32[8,128]{1,0:T(8,128)S(1)}, u32[]{:S(2)}, u32[]{:S(2)}) collective-permute-start(f32[8,128]{1,0:T(8,128)S(1)} %get-tuple-element.53.refs_0_), channel_id=1, source_target_pairs={{0,4},{4,0},{8,12},{12,8},{1,5},{5,1},{9,13},{13,9},{2,6},{6,2},{1... | collective-permute-start | bytes 12296 | tf_op jit(solution)/shard_map/ppermute | solution.py:366
  31.4 1.4 %early.1 = (bf16[2,128,1024]{2,1,0:T(8,128)(2,1)S(1)}, bf16[2,128,1024]{2,1,0:T(8,128)(2,1)S(1)}, f32[2,128,128]{2,1,0:T(8,128)S(1)}, f32[128,96]{1,0:T(8,128)S(1)}) custom-call(f32[2,64,1024]{2,1,0:T(8,128)S(1)} %get-tuple-element.40.q, f32[2,64,1024]{2,1,0:T(8,128)S(1)} %get-tuple-element.48.v, f32[2,128,1024]{2,1,0:T(8,128)S(1)} %get-tuple-element.47.near.refs_0_, ...), custom_call_target="tpu_custom_call" | custom-call | tf_op jit(solution)/shard_map/early/pallas_call | solution.py:330
  32.8 3.0 %collective-permute-done.5.refs_0_ = f32[2,80,1024]{2,1,0:T(8,128)S(1)} collective-permute-done((f32[2,80,1024]{2,1,0:T(8,128)S(1)}, f32[2,80,1024]{2,1,0:T(8,128)S(1)}, u32[]{:S(2)}, u32[]{:S(2)}) %collective-permute-start.5) | collective-permute-done | bytes 655392 | tf_op jit(solution)/shard_map/ppermute | solution.py:366
  35.9 0.1 collective-permute-start.13
  36.0 0.4 collective-permute-start.17
  36.4 1.6 %collective-permute-done.13.refs_1_ = f32[2,80,1024]{2,1,0:T(8,128)S(1)} collective-permute-done((f32[2,80,1024]{2,1,0:T(8,128)S(1)}, f32[2,80,1024]{2,1,0:T(8,128)S(1)}, u32[]{:S(2)}, u32[]{:S(2)}) %collective-permute-start.13) | collective-permute-done | bytes 655392 | tf_op jit(solution)/shard_map/ppermute | solution.py:366
  38.0 0.9 %late.1 = (f32[64,128]{1,0:T(8,128)S(1)}, f32[64,128]{1,0:T(8,128)S(1)}, f32[64,128]{1,0:T(8,128)S(1)}, f32[64,128]{1,0:T(8,128)S(1)}) custom-call(f32[72,128]{1,0:T(8,128)S(1)} %coeffs.1.refs_4_, bf16[2,128,1024]{2,1,0:T(8,128)(2,1)S(1)} %get-tuple-element.57.qv_high, bf16[2,128,1024]{2,1,0:T(8,128)(2,1)S(1)} %get-tuple-element.58.qv_low, ...), custom_call_target="tpu_custom_call" | custom-call | tf_op jit(solution)/shard_map/late/pallas_call | solution.py:330
  38.9 2.9 %collective-permute-start.14 = (f32[64,128]{1,0:T(8,128)S(1)}, f32[64,128]{1,0:T(8,128)S(1)}, u32[]{:S(2)}, u32[]{:S(2)}) collective-permute-start(f32[64,128]{1,0:T(8,128)S(1)} %get-tuple-element.63), channel_id=1, source_target_pairs={{0,12},{4,8},{8,4},{12,0},{1,13},{5,9},{9,5},{13,1},{2,14},{6,10},... | collective-permute-start | bytes 98312 | tf_op jit(solution)/shard_map/ppermute | solution.py:366
  41.8 1.5 %collective-permute-start.16 = (f32[64,128]{1,0:T(8,128)S(1)}, f32[64,128]{1,0:T(8,128)S(1)}, u32[]{:S(2)}, u32[]{:S(2)}) collective-permute-start(f32[64,128]{1,0:T(8,128)S(1)} %get-tuple-element.65), channel_id=1, source_target_pairs={{0,4},{4,0},{8,12},{12,8},{1,5},{5,1},{9,13},{13,9},{2,6},{6,2},{1... | collective-permute-start | bytes 98312 | tf_op jit(solution)/shard_map/ppermute | solution.py:366
  43.4 1.0 %modes.1 = f32[64,2048]{1,0:T(8,128)} custom-call(f32[72,128]{1,0:T(8,128)S(1)} %coeffs.1.refs_4_, f32[2,128,1024]{2,1,0:T(8,128)S(1)} %get-tuple-element.47.near.refs_0_), custom_call_target="tpu_custom_call" | custom-call | tf_op jit(solution)/shard_map/modes/pallas_call | solution.py:330
  44.4 0.3 collective-permute-done.14.refs_1_
  44.7 2.0 %collective-permute-done.15.refs_2_ = f32[64,128]{1,0:T(8,128)S(1)} collective-permute-done((f32[64,128]{1,0:T(8,128)S(1)}, f32[64,128]{1,0:T(8,128)S(1)}, u32[]{:S(2)}, u32[]{:S(2)}) %collective-permute-start.15) | collective-permute-done | bytes 32800 | tf_op jit(solution)/shard_map/ppermute | solution.py:366
  46.7 0.7 %fifth.1 = f32[64,64]{1,0:T(8,128)} custom-call(f32[64,128]{1,0:T(8,128)S(1)} %get-tuple-element.62.refs_0_, f32[64,128]{1,0:T(8,128)S(1)} %collective-permute-done.14.refs_1_, f32[64,128]{1,0:T(8,128)S(1)} %collective-permute-done.15.refs_2_, f32[64,128]{1,0:T(8,128)S(1)} %collective-permute-done.16.refs_3_, f32[72,128]{1,0:T(8,128)S(1)} %coeffs.1.refs_4_, ...), custom_call_target="tpu_custom_call" | custom-call | tf_op jit(solution)/shard_map/fifth/pallas_call | solution.py:330
  (22 shorter events, 0.1 us)
Async XLA Ops:
  0.6 14.1 %copy-start = (f32[16,128,128]{2,1,0:T(8,128)S(1)}, f32[16,128,128]{2,1,0:T(8,128)}, u32[]{:S(2)}) copy-start(f32[16,128,128]{2,1,0:T(8,128)} %precond.3) | copy-start | bytes 3145732
  0.6 8.1 %copy-start.2 = (f32[3,2048]{1,0:T(4,128)S(1)}, f32[3,2048]{1,0:T(4,128)}, u32[]{:S(2)}) copy-start(f32[3,2048]{1,0:T(4,128)} %couplings.3) | copy-start | bytes 73732
  2.6 12.1 %copy-start.3 = (f32[2048]{0:T(1024)S(1)}, f32[2048]{0:T(1024)}, u32[]{:S(2)}) copy-start(f32[2048]{0:T(1024)} %param.6) | copy-start | bytes 24580
  2.6 12.1 %collective-permute-start.4 = (f32[2,48,1024]{2,1,0:T(8,128)S(1)}, f32[2,48,1024]{2,1,0:T(8,128)S(1)}, u32[]{:S(2)}, u32[]{:S(2)}) collective-permute-start(f32[2,48,1024]{2,1,0:T(8,128)S(1)} %get-tuple-element.36), channel_id=1, source_target_pairs={{0,2},{1,3},{2,0},{3,1},{4,6},{5,7},{6,4},{7,5},{8,10},{9,11},{10,... | collective-permute-start | bytes 1179656 | tf_op jit(solution)/shard_map/ppermute | solution.py:366
  5.6 4.8 %collective-permute-start.2 = (f32[64,1024]{1,0:T(8,128)S(1)}, f32[64,1024]{1,0:T(8,128)S(1)}, u32[]{:S(2)}, u32[]{:S(2)}) collective-permute-start(f32[64,1024]{1,0:T(8,128)S(1)} %get-tuple-element.34.d_a), channel_id=1, source_target_pairs={{0,1},{1,0},{2,3},{3,2},{4,8},{5,9},{6,10},{7,11},{8,4},{9,5},{10,... | collective-permute-start | bytes 786440 | tf_op jit(solution)/shard_map/ppermute | solution.py:352
  5.6 8.9 %collective-permute-start.3 = (f32[64,1024]{1,0:T(8,128)S(1)}, f32[64,1024]{1,0:T(8,128)S(1)}, u32[]{:S(2)}, u32[]{:S(2)}) collective-permute-start(f32[64,1024]{1,0:T(8,128)S(1)} %get-tuple-element.35.d_b), channel_id=1, source_target_pairs={{0,4},{1,5},{2,6},{3,7},{4,0},{5,1},{6,2},{7,3},{8,12},{9,13},{10,... | collective-permute-start | bytes 786440 | tf_op jit(solution)/shard_map/ppermute | solution.py:352
  8.8 6.0 %collective-permute-start = (f32[1,1024]{1,0:T(1,128)S(1)}, f32[1,1024]{1,0:T(1,128)S(1)}, u32[]{:S(2)}, u32[]{:S(2)}) collective-permute-start(f32[1,1024]{1,0:T(1,128)S(1)} %slice.3), channel_id=1, source_target_pairs={{0,1},{1,0},{2,3},{3,2},{4,8},{5,9},{6,10},{7,11},{8,4},{9,5},{10,... | collective-permute-start | bytes 12296 | tf_op jit(solution)/shard_map/ppermute | solution.py:352
  8.9 5.9 %collective-permute-start.1 = (f32[1,1024]{1,0:T(1,128)S(1)}, f32[1,1024]{1,0:T(1,128)S(1)}, u32[]{:S(2)}, u32[]{:S(2)}) collective-permute-start(f32[1,1024]{1,0:T(1,128)S(1)} %slice.3), channel_id=1, source_target_pairs={{0,4},{1,5},{2,6},{3,7},{4,0},{5,1},{6,2},{7,3},{8,12},{9,13},{10,... | collective-permute-start | bytes 12296 | tf_op jit(solution)/shard_map/ppermute | solution.py:352
  14.8 11.2 %copy-start.1 = (f32[64,2048]{1,0:T(8,128)S(1)}, f32[64,2048]{1,0:T(8,128)}, u32[]{:S(2)}) copy-start(f32[64,2048]{1,0:T(8,128)} %forces.3) | copy-start | bytes 1572868
  15.8 10.2 %collective-permute-start.8 = (f32[2,128,1024]{2,1,0:T(8,128)S(1)}, f32[2,128,1024]{2,1,0:T(8,128)S(1)}, u32[]{:S(2)}, u32[]{:S(2)}) collective-permute-start(f32[2,128,1024]{2,1,0:T(8,128)S(1)} %get-tuple-element.47.near.refs_0_), channel_id=1, source_target_pairs={{0,1},{1,0},{2,3},{3,2},{4,5},{5,4},{6,7},{7,6},{8,9},{9,8},{10,11... | collective-permute-start | bytes 3145736 | tf_op jit(solution)/shard_map/ppermute | solution.py:366
  15.9 5.0 %collective-permute-start.6 = (f32[64,1024]{1,0:T(8,128)S(1)}, f32[64,1024]{1,0:T(8,128)S(1)}, u32[]{:S(2)}, u32[]{:S(2)}) collective-permute-start(f32[64,1024]{1,0:T(8,128)S(1)} %get-tuple-element.41.w_a), channel_id=1, source_target_pairs={{0,1},{1,0},{2,3},{3,2},{4,8},{5,9},{6,10},{7,11},{8,4},{9,5},{10,... | collective-permute-start | bytes 786440 | tf_op jit(solution)/shard_map/ppermute | solution.py:352
  16.3 9.6 %collective-permute-start.7 = (f32[64,1024]{1,0:T(8,128)S(1)}, f32[64,1024]{1,0:T(8,128)S(1)}, u32[]{:S(2)}, u32[]{:S(2)}) collective-permute-start(f32[64,1024]{1,0:T(8,128)S(1)} %get-tuple-element.42.w_b), channel_id=1, source_target_pairs={{0,4},{1,5},{2,6},{3,7},{4,0},{5,1},{6,2},{7,3},{8,12},{9,13},{10,... | collective-permute-start | bytes 786440 | tf_op jit(solution)/shard_map/ppermute | solution.py:352
  19.3 16.5 %collective-permute-start.5 = (f32[2,80,1024]{2,1,0:T(8,128)S(1)}, f32[2,80,1024]{2,1,0:T(8,128)S(1)}, u32[]{:S(2)}, u32[]{:S(2)}) collective-permute-start(f32[2,80,1024]{2,1,0:T(8,128)S(1)} %get-tuple-element.39), channel_id=1, source_target_pairs={{0,2},{1,3},{2,0},{3,1},{4,6},{5,7},{6,4},{7,5},{8,10},{9,11},{10,... | collective-permute-start | bytes 1966088 | tf_op jit(solution)/shard_map/ppermute | solution.py:366
  26.0 5.5 %collective-permute-start.9 = (f32[2,48,1024]{2,1,0:T(8,128)S(1)}, f32[2,48,1024]{2,1,0:T(8,128)S(1)}, u32[]{:S(2)}, u32[]{:S(2)}) collective-permute-start(f32[2,48,1024]{2,1,0:T(8,128)S(1)} %collective-permute-done.4.refs_2_), channel_id=1, source_target_pairs={{0,1},{1,0},{2,3},{3,2},{4,5},{5,4},{6,7},{7,6},{8,9},{9,8},{10,11... | collective-permute-start | bytes 1179656 | tf_op jit(solution)/shard_map/ppermute | solution.py:366
  27.0 8.8 %collective-permute-start.10 = (f32[8,128]{1,0:T(8,128)S(1)}, f32[8,128]{1,0:T(8,128)S(1)}, u32[]{:S(2)}, u32[]{:S(2)}) collective-permute-start(f32[8,128]{1,0:T(8,128)S(1)} %get-tuple-element.53.refs_0_), channel_id=1, source_target_pairs={{0,12},{4,8},{8,4},{12,0},{1,13},{5,9},{9,5},{13,1},{2,14},{6,10},... | collective-permute-start | bytes 12296 | tf_op jit(solution)/shard_map/ppermute | solution.py:366
  29.6 6.3 %collective-permute-start.11 = (f32[8,128]{1,0:T(8,128)S(1)}, f32[8,128]{1,0:T(8,128)S(1)}, u32[]{:S(2)}, u32[]{:S(2)}) collective-permute-start(f32[8,128]{1,0:T(8,128)S(1)} %get-tuple-element.53.refs_0_), channel_id=1, source_target_pairs={{0,8},{4,12},{8,0},{12,4},{1,9},{5,13},{9,1},{13,5},{2,10},{6,14},... | collective-permute-start | bytes 12296 | tf_op jit(solution)/shard_map/ppermute | solution.py:366
  30.2 5.6 %collective-permute-start.12 = (f32[8,128]{1,0:T(8,128)S(1)}, f32[8,128]{1,0:T(8,128)S(1)}, u32[]{:S(2)}, u32[]{:S(2)}) collective-permute-start(f32[8,128]{1,0:T(8,128)S(1)} %get-tuple-element.53.refs_0_), channel_id=1, source_target_pairs={{0,4},{4,0},{8,12},{12,8},{1,5},{5,1},{9,13},{13,9},{2,6},{6,2},{1... | collective-permute-start | bytes 12296 | tf_op jit(solution)/shard_map/ppermute | solution.py:366
  35.9 2.2 %collective-permute-start.13 = (f32[2,80,1024]{2,1,0:T(8,128)S(1)}, f32[2,80,1024]{2,1,0:T(8,128)S(1)}, u32[]{:S(2)}, u32[]{:S(2)}) collective-permute-start(f32[2,80,1024]{2,1,0:T(8,128)S(1)} %collective-permute-done.5.refs_0_), channel_id=1, source_target_pairs={{0,1},{1,0},{2,3},{3,2},{4,5},{5,4},{6,7},{7,6},{8,9},{9,8},{10,11... | collective-permute-start | bytes 1966088 | tf_op jit(solution)/shard_map/ppermute | solution.py:366
  36.0 8.4 %collective-permute-start.17 = (f32[72,128]{1,0:T(8,128)S(1)}, f32[72,128]{1,0:T(8,128)S(1)}, u32[]{:S(2)}, u32[]{:S(2)}) collective-permute-start(f32[72,128]{1,0:T(8,128)S(1)} %coeffs.1.refs_4_), channel_id=1, source_target_pairs={{0,5},{1,4},{2,8},{3,12},{4,1},{5,0},{6,9},{7,13},{8,2},{9,6},{10,... | collective-permute-start | bytes 110600 | tf_op jit(solution)/shard_map/ppermute | solution.py:362
  38.9 5.8 %collective-permute-start.14 = (f32[64,128]{1,0:T(8,128)S(1)}, f32[64,128]{1,0:T(8,128)S(1)}, u32[]{:S(2)}, u32[]{:S(2)}) collective-permute-start(f32[64,128]{1,0:T(8,128)S(1)} %get-tuple-element.63), channel_id=1, source_target_pairs={{0,12},{4,8},{8,4},{12,0},{1,13},{5,9},{9,5},{13,1},{2,14},{6,10},... | collective-permute-start | bytes 98312 | tf_op jit(solution)/shard_map/ppermute | solution.py:366
  41.8 4.8 %collective-permute-start.15 = (f32[64,128]{1,0:T(8,128)S(1)}, f32[64,128]{1,0:T(8,128)S(1)}, u32[]{:S(2)}, u32[]{:S(2)}) collective-permute-start(f32[64,128]{1,0:T(8,128)S(1)} %get-tuple-element.64), channel_id=1, source_target_pairs={{0,8},{4,12},{8,0},{12,4},{1,9},{5,13},{9,1},{13,5},{2,10},{6,14},... | collective-permute-start | bytes 98312 | tf_op jit(solution)/shard_map/ppermute | solution.py:366
  41.8 4.8 %collective-permute-start.16 = (f32[64,128]{1,0:T(8,128)S(1)}, f32[64,128]{1,0:T(8,128)S(1)}, u32[]{:S(2)}, u32[]{:S(2)}) collective-permute-start(f32[64,128]{1,0:T(8,128)S(1)} %get-tuple-element.65), channel_id=1, source_target_pairs={{0,4},{4,0},{8,12},{12,8},{1,5},{5,1},{9,13},{13,9},{2,6},{6,2},{1... | collective-permute-start | bytes 98312 | tf_op jit(solution)/shard_map/ppermute | solution.py:366

commit v4 on v3

--- a/solution.py
+++ b/solution.py
@@ -139,8 +139,7 @@
     return result.reshape(rows, LANES)
 
 
-def first_kernel(forces, precond, out_a, out_b, first_rows, field, matrices, sems):
-    early = first_rows.shape[1]
+def first_kernel(forces, precond, out_a, out_b, field, matrices, sems):
     copies = []
     for slot, plane in enumerate(slot_planes()):
         here = pl.ds(pl.multiple_of(plane * PLANE, PLANE), PLANE)
@@ -159,14 +158,19 @@
         for copy in copies[slot]:
             copy.wait()
         for k in range(CHUNKS):
-            d = block_product(field[slot, :, chunk(k)], matrices[slot, k])
-            out[:, chunk(k)] = d
-            first_rows[slot, :, chunk(k)] = d[0:early]
-
-
-def second_kernel(couplings, ground, before_a, before_b, precond, d_a, d_b, got_a, got_b, q, w_a, w_b, beside, near):
+            out[:, chunk(k)] = block_product(field[slot, :, chunk(k)], matrices[slot, k])
+
+
+def other_kernel(forces, precond, out):
+    for slot, plane in enumerate(slot_planes()):
+        for k in range(CHUNKS):
+            out[slot, :, chunk(k)] = block_product(
+                forces[:, plane_chunk(plane, k)], precond[plane * CHUNKS + k]
+            )
+
+
+def second_kernel(couplings, ground, before_a, before_b, precond, d_a, d_b, got_a, got_b, q, w_a, w_b, w_both, near):
     rows = w_a.shape[0]
-    early = 2 * rows - beside.shape[1]
     springs = all_springs(couplings, ground, (before_a, before_b))
     fields = (d_a, d_b)
     for slot, plane in enumerate(slot_planes()):
@@ -177,8 +181,7 @@
             q[slot, :, chunk(k)] = image
             w = block_product(image, precond[plane * CHUNKS + k])
             (w_a, w_b)[slot][:, chunk(k)] = w
-            beside[slot, 0:rows, chunk(k)] = w
-            beside[slot, rows:, chunk(k)] = fields[slot][early:, chunk(k)]
+            w_both[slot, :, chunk(k)] = w
             near[slot, 0:rows, chunk(k)] = fields[slot][:, chunk(k)]
             near[slot, rows : 2 * rows, chunk(k)] = w
 
@@ -226,22 +229,27 @@
     return jnp.concatenate([field[slot] for field in fields], axis=0)
 
 
-def early_kernel(n_near, n_far, q, v, *refs):
-    near, d_far = refs[:n_near], refs[n_near : n_near + n_far]
-    qv_high, qv_low, near_gram, far_gram = refs[n_near + n_far :]
-    rows = q.shape[1]
-    near_sums, far_sum = [None] * n_near, None
+def early_kernel(n_near, q, v, *refs):
+    near, (qv_high, qv_low, near_gram) = refs[:n_near], refs[n_near:]
+    sums = [None] * n_near
     for slot in range(2):
         images = split(jnp.concatenate([q[slot], v[slot]], axis=0))
         qv_high[slot], qv_low[slot] = images
         for i in range(n_near):
             term = product(images, split(near[i][slot]), ((1,), (1,)))
-            near_sums[i] = term if slot == 0 else near_sums[i] + term
+            sums[i] = term if slot == 0 else sums[i] + term
+    for i in range(n_near):
+        near_gram[i] = sums[i]
+
+
+def far_kernel(qv_high, qv_low, *refs):
+    d_far, far_gram = refs[:-1], refs[-1]
+    total = None
+    for slot in range(2):
+        images = (qv_high[slot], qv_low[slot])
         term = product(images, split(columns_of(d_far, slot)), ((1,), (1,)))
-        far_sum = term if slot == 0 else far_sum + term
-    for i in range(n_near):
-        near_gram[i] = near_sums[i]
-    far_gram[...] = far_sum
+        total = term if slot == 0 else total + term
+    far_gram[...] = total
 
 
 def coeffs_kernel(rows, *refs):
@@ -276,17 +284,10 @@
         gram = outs[0]
     for i in range(n_near):
         gram[i] = p * near_gram[i, 0:rows] + s * near_gram[i, rows : 2 * rows]
-    first_part = far_gram[...]
-    early, width = first_part.shape[1] // n_far, far[0].shape[1]
+    d_part = far_gram[...]
     for i in range(n_far):
-        both = jnp.concatenate(
-            [
-                first_part[:, i * early : (i + 1) * early],
-                far_sum[:, i * width + rows : (i + 1) * width],
-                far_sum[:, i * width : i * width + rows],
-            ],
-            axis=1,
-        )
+        there = slice(i * rows, (i + 1) * rows)
+        both = jnp.concatenate([d_part[:, there], far_sum[:, there]], axis=1)
         gram[n_near + i] = p * both[0:rows] + s * both[rows : 2 * rows]
     if exchange:
         mine = lax.axis_index("nodes") ^ lax.axis_index("cols")
@@ -310,13 +311,15 @@
 
 
 def fifth_kernel(scale, n_sums, *refs):
-    sums, own, theirs, tile = refs[:n_sums], refs[n_sums], refs[n_sums + 1], refs[n_sums + 2]
+    sums, coeffs_of, tile = refs[:n_sums], refs[n_sums:-1], refs[-1]
     rows = tile.shape[0]
     total = sums[0][...]
     for piece in sums[1:]:
         total = total + piece[...]
-    here = lax.axis_index("nodes") == lax.axis_index("cols")
-    coeffs = jnp.where(here, own[0:8, :], theirs[0:8, :])
+    mine = lax.axis_index("nodes") ^ lax.axis_index("cols")
+    coeffs = coeffs_of[0][0:8, :]
+    for i in range(1, n_sums):
+        coeffs = jnp.where(mine == i, coeffs_of[i][0:8, :], coeffs)
     tile[...] = (
         coeffs[0:1, 0:rows] * total[:, 0:rows] + coeffs[1:2, 0:rows] * total[:, rows : 2 * rows]
     ) * scale
@@ -352,16 +355,6 @@
     return lax.ppermute(block, ("nodes", "cols"), route)
 
 
-def transposed(block):
-    nodes, cols = lax.axis_size("nodes"), lax.axis_size("cols")
-    route = []
-    for n in range(nodes):
-        for c in range(cols):
-            there = c * cols + n if n != c else (n ^ 1) * (cols + 1)
-            route.append((n * cols + c, there))
-    return lax.ppermute(block, ("nodes", "cols"), route)
-
-
 def swapped(block, axis, bit):
     return lax.ppermute(block, axis, [(i, i ^ bit) for i in range(lax.axis_size(axis))])
 
@@ -383,12 +376,11 @@
         return [held[key] for key in range(max(top, 1))]
 
     field = (rows, PLANE)
-    early = rows * 3 // 4
-    d_a, d_b, d_far = call(
+    d_a, d_b = call(
         first_kernel,
         "first",
         [pltpu.with_memory_space_constraint(x, pltpu.HBM) for x in (forces, precond)],
-        [field, field, (2, early, PLANE)],
+        [field] * 2,
         [
             pltpu.VMEM((2, rows, PLANE), F32),
             pltpu.VMEM((2, CHUNKS, LANES, LANES), F32),
@@ -397,20 +389,21 @@
         pltpu.HBM,
     )
     got_a, got_b = neighbours(d_a, 1), neighbours(d_b, 0)
-    d_far = swapped(d_far, "cols", top)
+    forces_far = swapped(forces, "cols", top)
     last = couplings[2:3, length - PLANE :]
     before_a, before_b = neighbours(last, 1), neighbours(last, 0)
-    got_a, got_b, d_far = lax.optimization_barrier((got_a, got_b, d_far))
+    got_a, got_b, forces_far = lax.optimization_barrier((got_a, got_b, forces_far))
     edges = (couplings, ground, before_a, before_b)
-    q, w_a, w_b, beside, near = call(
+    q, w_a, w_b, w_both, near = call(
         second_kernel,
         "second",
         (*edges, precond, d_a, d_b, got_a, got_b),
-        [(2,) + field, field, field, (2, 2 * rows - early, PLANE), (2, 2 * rows, PLANE)],
+        [(2,) + field, field, field, (2,) + field, (2, 2 * rows, PLANE)],
     )
     next_a, next_b = neighbours(w_a, 1), neighbours(w_b, 0)
-    far = swapped(beside, "cols", top)
+    far = swapped(w_both, "cols", top)
     near = shared(near)
+    (d_far,) = call(other_kernel, "other", (forces_far, precond), [(2,) + field])
     next_a, next_b, d_far, near = lax.optimization_barrier((next_a, next_b, d_far, near))
     d_far = shared(d_far)
     (packed,) = call(side_kernel, "side", (forces, q, near[0]), [(rows, LANES)])
@@ -422,17 +415,21 @@
     )
     exchange = nodes == cols
     if exchange:
-        dots = [dots] + [swapped(dots, "nodes", i) for i in reversed(range(1, nodes))]
+        dots = [dots] + [swapped(dots, "nodes", i) for i in range(1, nodes)]
     else:
         dots = [lax.psum(dots, "nodes")]
     halves = jax.ShapeDtypeStruct((2, 2 * rows, PLANE), jnp.bfloat16)
-    qv_high, qv_low, near_gram, far_gram = call(
-        functools.partial(early_kernel, len(near), len(d_far)),
+    qv_high, qv_low, near_gram = call(
+        functools.partial(early_kernel, len(near)),
         "early",
-        (q, v, *near, *d_far),
-        [halves, halves, (len(near), 2 * rows, 2 * rows), (2 * rows, len(d_far) * early)],
-    )
-    far, near_gram, *dots = lax.optimization_barrier((far, near_gram, *dots))
+        (q, v, *near),
+        [halves, halves, (len(near), 2 * rows, 2 * rows)],
+    )
+    d_far, far = lax.optimization_barrier((d_far, far))
+    (far_gram,) = call(
+        far_kernel, "far", (qv_high, qv_low, *d_far), [(2 * rows, len(d_far) * rows)]
+    )
+    far, far_gram, *dots = lax.optimization_barrier((far, far_gram, *dots))
     far = shared(far)
     (coeffs,) = call(functools.partial(coeffs_kernel, rows), "coeffs", dots, [(rows + 8, LANES)])
     grams = call(
@@ -445,12 +442,12 @@
     scale = 1.0 / (length * nodes)
     (modes,) = call(modes_kernel, "modes", (coeffs, near[0]), [(rows, length)])
     if exchange:
-        theirs = transposed(coeffs)
+        theirs = [coeffs] + [swapped(coeffs, "cols", i) for i in range(1, cols)]
         sums = [grams[0]] + [swapped(grams[i], "nodes", i) for i in reversed(range(1, nodes))]
         (tile,) = call(
             functools.partial(fifth_kernel, scale, nodes),
             "fifth",
-            (*sums, coeffs, theirs),
+            (*sums, *theirs),
             [(rows, rows)],
         )
     else:

time: 47.5 us -> 46.2 us (0.973)
  waiting for transfers between devices: 16.4 us -> 14.3 us
    ppermute x11 -> x14, waiting for transfers between devices: 7.1 us -> 4.08 us  [swapped(): lax.ppermute(block, axis, [(i, i ^ bit) for i in range(lax.axis_size(axis...]
    ppermute x11 -> x14, starting transfers between devices: 13.5 us -> 15.7 us  [swapped(): lax.ppermute(block, axis, [(i, i ^ bit) for i in range(lax.axis_size(axis...]
    ppermute x6, starting transfers between devices: 8.26 us -> 6.82 us  [neighbours(): return lax.ppermute(block, ('nodes', 'cols'), route)]
    ppermute x6, waiting for transfers between devices: 9.27 us -> 10.2 us  [neighbours(): return lax.ppermute(block, ('nodes', 'cols'), route)]
    pallas_call x9 -> x11, Pallas kernels: 8.01 us -> 8.44 us  [call(): pl.pallas_call(kernel, out_shape=shapes, in_specs=[pl.BlockSpec(memory_sp...]
  transfers between devices with their start and end apart: 18 -> 20, of which waited for: 7 -> 6; matrix products, arithmetic and copies ran while one was open for 0% -> 0% of each run, Pallas kernels for 9% -> 15%
where the time goes in v4:
time: 46.2 us; the launch traced here: 46.1 us
  starting transfers between devices  22.5 us (49%)
  waiting for transfers between devices  14.3 us (31%)
  Pallas kernels  8.44 us (18%)
  between operations  0.8 us (2%)
    ppermute x14, starting transfers between devices, swapped(): lax.ppermute(block, axis, [(i, i ^ bit) for i in range(lax.axis_size(axis...  15.7 us
    ppermute x6, waiting for transfers between devices, neighbours(): return lax.ppermute(block, ('nodes', 'cols'), route)  10.2 us
    pallas_call x11, Pallas kernels, call(): pl.pallas_call(kernel, out_shape=shapes, in_specs=[pl.BlockSpec(memory_sp...  8.44 us
    ppermute x6, starting transfers between devices, neighbours(): return lax.ppermute(block, ('nodes', 'cols'), route)  6.82 us
    ppermute x14, waiting for transfers between devices, swapped(): lax.ppermute(block, axis, [(i, i ^ bit) for i in range(lax.axis_size(axis...  4.08 us
  transfers between devices with their start and end apart: 20, of which 6 were waited for; matrix products, arithmetic and copies ran while one was open for 0% of the time, Pallas kernels for 15%

profile of v4, /device:TPU:0, one launch (start us, length us, event | category | flops | bytes accessed | tf_op | source)
XLA Modules:
  0.0 46.1 jit_solution(4112500901155227908)
XLA Ops:
  0.6 3.0 %collective-permute-start.4 = (f32[64,2048]{1,0:T(8,128)}, f32[64,2048]{1,0:T(8,128)S(1)}, u32[]{:S(2)}, u32[]{:S(2)}) collective-permute-start(f32[64,2048]{1,0:T(8,128)} %forces.3), channel_id=1, source_target_pairs={{0,2},{1,3},{2,0},{3,1},{4,6},{5,7},{6,4},{7,5},{8,10},{9,11},{10,... | collective-permute-start | bytes 1572872 | tf_op jit(solution)/shard_map/ppermute | solution.py:359
  3.7 1.8 %first.1 = (f32[64,1024]{1,0:T(8,128)S(1)}, f32[64,1024]{1,0:T(8,128)S(1)}) custom-call(f32[64,2048]{1,0:T(8,128)} %forces.3, f32[16,128,128]{2,1,0:T(8,128)} %precond.5), custom_call_target="tpu_custom_call" | custom-call | tf_op jit(solution)/shard_map/first/pallas_call | solution.py:333
  5.5 0.1 collective-permute-start.2
  5.6 3.1 %collective-permute-start.3 = (f32[64,1024]{1,0:T(8,128)S(1)}, f32[64,1024]{1,0:T(8,128)S(1)}, u32[]{:S(2)}, u32[]{:S(2)}) collective-permute-start(f32[64,1024]{1,0:T(8,128)S(1)} %get-tuple-element.36.d_b), channel_id=1, source_target_pairs={{0,4},{1,5},{2,6},{3,7},{4,0},{5,1},{6,2},{7,3},{8,12},{9,13},{10,... | collective-permute-start | bytes 786440 | tf_op jit(solution)/shard_map/ppermute | solution.py:355
  8.8 0.1 collective-permute-start
  8.9 5.6 %collective-permute-done.3.got_b = f32[64,1024]{1,0:T(8,128)S(1)} collective-permute-done((f32[64,1024]{1,0:T(8,128)S(1)}, f32[64,1024]{1,0:T(8,128)S(1)}, u32[]{:S(2)}, u32[]{:S(2)}) %collective-permute-start.3) | collective-permute-done | bytes 262176 | tf_op jit(solution)/shard_map/ppermute | solution.py:355
  14.5 1.3 %collective-permute-done.4.forces = f32[64,2048]{1,0:T(8,128)S(1)} collective-permute-done((f32[64,2048]{1,0:T(8,128)}, f32[64,2048]{1,0:T(8,128)S(1)}, u32[]{:S(2)}, u32[]{:S(2)}) %collective-permute-start.4) | collective-permute-done | bytes 524320 | tf_op jit(solution)/shard_map/ppermute | solution.py:359
  15.8 1.0 %second.1 = (f32[2,64,1024]{2,1,0:T(8,128)S(1)}, f32[64,1024]{1,0:T(8,128)S(1)}, f32[64,1024]{1,0:T(8,128)S(1)}, f32[2,64,1024]{2,1,0:T(8,128)S(1)}, f32[2,128,1024]{2,1,0:T(8,128)S(1)}) custom-call(f32[3,2048]{1,0:T(4,128)S(1)} %copy-done.2, f32[1,2048]{1,0:T(1,128)S(1)} %bitcast.1, f32[1,1024]{1,0:T(1,128)S(1)} %collective-permute-done.before_a, ...), custom_call_target="tpu_custom_call" | custom-call | tf_op jit(solution)/shard_map/second/pallas_call | solution.py:333
  16.9 0.5 %collective-permute-start.5 = (f32[64,1024]{1,0:T(8,128)S(1)}, f32[64,1024]{1,0:T(8,128)S(1)}, u32[]{:S(2)}, u32[]{:S(2)}) collective-permute-start(f32[64,1024]{1,0:T(8,128)S(1)} %get-tuple-element.39.w_a), channel_id=1, source_target_pairs={{0,1},{1,0},{2,3},{3,2},{4,8},{5,9},{6,10},{7,11},{8,4},{9,5},{10,... | collective-permute-start | bytes 786440 | tf_op jit(solution)/shard_map/ppermute | solution.py:355
  17.4 3.0 %collective-permute-start.6 = (f32[64,1024]{1,0:T(8,128)S(1)}, f32[64,1024]{1,0:T(8,128)S(1)}, u32[]{:S(2)}, u32[]{:S(2)}) collective-permute-start(f32[64,1024]{1,0:T(8,128)S(1)} %get-tuple-element.40.w_b), channel_id=1, source_target_pairs={{0,4},{1,5},{2,6},{3,7},{4,0},{5,1},{6,2},{7,3},{8,12},{9,13},{10,... | collective-permute-start | bytes 786440 | tf_op jit(solution)/shard_map/ppermute | solution.py:355
  20.4 0.5 %other.1.refs_0_ = f32[2,64,1024]{2,1,0:T(8,128)S(1)} custom-call(f32[64,2048]{1,0:T(8,128)S(1)} %collective-permute-done.4.forces, f32[16,128,128]{2,1,0:T(8,128)S(1)} %copy-done), custom_call_target="tpu_custom_call" | custom-call | tf_op jit(solution)/shard_map/other/pallas_call | solution.py:333
  20.9 1.5 %collective-permute-start.9 = (f32[2,64,1024]{2,1,0:T(8,128)S(1)}, f32[2,64,1024]{2,1,0:T(8,128)S(1)}, u32[]{:S(2)}, u32[]{:S(2)}) collective-permute-start(f32[2,64,1024]{2,1,0:T(8,128)S(1)} %get-tuple-element.44), channel_id=1, source_target_pairs={{0,2},{1,3},{2,0},{3,1},{4,6},{5,7},{6,4},{7,5},{8,10},{9,11},{10,... | collective-permute-start | bytes 1572872 | tf_op jit(solution)/shard_map/ppermute | solution.py:359
  22.4 4.6 %collective-permute-done.6.next_b = f32[64,1024]{1,0:T(8,128)S(1)} collective-permute-done((f32[64,1024]{1,0:T(8,128)S(1)}, f32[64,1024]{1,0:T(8,128)S(1)}, u32[]{:S(2)}, u32[]{:S(2)}) %collective-permute-start.6) | collective-permute-done | bytes 262176 | tf_op jit(solution)/shard_map/ppermute | solution.py:355
  27.0 0.3 side.1.packed
  27.3 0.8 %third.1 = (f32[2,64,1024]{2,1,0:T(8,128)S(1)}, f32[8,128]{1,0:T(8,128)S(1)}) custom-call(f32[3,2048]{1,0:T(4,128)S(1)} %copy-done.2, f32[1,2048]{1,0:T(1,128)S(1)} %bitcast.2, f32[1,1024]{1,0:T(1,128)S(1)} %collective-permute-done.before_a, f32[1,1024]{1,0:T(1,128)S(1)} %collective-permute-done.1.before_b, f32[64,1024]{1,0:T(8,128)S(1)} %get-tuple-element.39.w_a, ...), custom_call_target="tpu_custom_call" | custom-call | tf_op jit(solution)/shard_map/third/pallas_call | solution.py:333
  28.1 2.5 %collective-permute-start.12 = (f32[8,128]{1,0:T(8,128)S(1)}, f32[8,128]{1,0:T(8,128)S(1)}, u32[]{:S(2)}, u32[]{:S(2)}) collective-permute-start(f32[8,128]{1,0:T(8,128)S(1)} %get-tuple-element.57.refs_0_), channel_id=1, source_target_pairs={{0,12},{4,8},{8,4},{12,0},{1,13},{5,9},{9,5},{13,1},{2,14},{6,10},... | collective-permute-start | bytes 12296 | tf_op jit(solution)/shard_map/ppermute | solution.py:359
  30.6 0.7 %collective-permute-start.11 = (f32[8,128]{1,0:T(8,128)S(1)}, f32[8,128]{1,0:T(8,128)S(1)}, u32[]{:S(2)}, u32[]{:S(2)}) collective-permute-start(f32[8,128]{1,0:T(8,128)S(1)} %get-tuple-element.57.refs_0_), channel_id=1, source_target_pairs={{0,8},{4,12},{8,0},{12,4},{1,9},{5,13},{9,1},{13,5},{2,10},{6,14},... | collective-permute-start | bytes 12296 | tf_op jit(solution)/shard_map/ppermute | solution.py:359
  31.3 1.2 %collective-permute-start.10 = (f32[8,128]{1,0:T(8,128)S(1)}, f32[8,128]{1,0:T(8,128)S(1)}, u32[]{:S(2)}, u32[]{:S(2)}) collective-permute-start(f32[8,128]{1,0:T(8,128)S(1)} %get-tuple-element.57.refs_0_), channel_id=1, source_target_pairs={{0,4},{4,0},{8,12},{12,8},{1,5},{5,1},{9,13},{13,9},{2,6},{6,2},{1... | collective-permute-start | bytes 12296 | tf_op jit(solution)/shard_map/ppermute | solution.py:359
  32.5 1.0 %early.1 = (bf16[2,128,1024]{2,1,0:T(8,128)(2,1)S(1)}, bf16[2,128,1024]{2,1,0:T(8,128)(2,1)S(1)}, f32[2,128,128]{2,1,0:T(8,128)S(1)}) custom-call(f32[2,64,1024]{2,1,0:T(8,128)S(1)} %get-tuple-element.46.q, f32[2,64,1024]{2,1,0:T(8,128)S(1)} %get-tuple-element.50.v, f32[2,128,1024]{2,1,0:T(8,128)S(1)} %get-tuple-element.49.near.refs_0_, ...), custom_call_target="tpu_custom_call" | custom-call | tf_op jit(solution)/shard_map/early/pallas_call | solution.py:333
  33.5 1.2 %collective-permute-done.9.refs_0_ = f32[2,64,1024]{2,1,0:T(8,128)S(1)} collective-permute-done((f32[2,64,1024]{2,1,0:T(8,128)S(1)}, f32[2,64,1024]{2,1,0:T(8,128)S(1)}, u32[]{:S(2)}, u32[]{:S(2)}) %collective-permute-start.9) | collective-permute-done | bytes 524320 | tf_op jit(solution)/shard_map/ppermute | solution.py:359
  34.7 0.6 %far.1.far_gram = f32[128,128]{1,0:T(8,128)S(1)} custom-call(bf16[2,128,1024]{2,1,0:T(8,128)(2,1)S(1)} %get-tuple-element.52.qv_high, bf16[2,128,1024]{2,1,0:T(8,128)(2,1)S(1)} %get-tuple-element.53.qv_low, f32[2,64,1024]{2,1,0:T(8,128)S(1)} %other.1.refs_0_, f32[2,64,1024]{2,1,0:T(8,128)S(1)} %collective-permute-done.8.refs_1_), custom_call_target="tpu_custom_call" | custom-call | tf_op jit(solution)/shard_map/far/pallas_call | solution.py:333
  35.3 0.1 collective-permute-start.13
  35.4 1.7 %collective-permute-start.19 = (f32[72,128]{1,0:T(8,128)S(1)}, f32[72,128]{1,0:T(8,128)S(1)}, u32[]{:S(2)}, u32[]{:S(2)}) collective-permute-start(f32[72,128]{1,0:T(8,128)S(1)} %coeffs.1.refs_4_), channel_id=1, source_target_pairs={{0,3},{1,2},{2,1},{3,0},{4,7},{5,6},{6,5},{7,4},{8,11},{9,10},{10,... | collective-permute-start | bytes 110600 | tf_op jit(solution)/shard_map/ppermute | solution.py:359
  37.1 0.5 %collective-permute-start.18 = (f32[72,128]{1,0:T(8,128)S(1)}, f32[72,128]{1,0:T(8,128)S(1)}, u32[]{:S(2)}, u32[]{:S(2)}) collective-permute-start(f32[72,128]{1,0:T(8,128)S(1)} %coeffs.1.refs_4_), channel_id=1, source_target_pairs={{0,2},{1,3},{2,0},{3,1},{4,6},{5,7},{6,4},{7,5},{8,10},{9,11},{10,... | collective-permute-start | bytes 110600 | tf_op jit(solution)/shard_map/ppermute | solution.py:359
  37.6 0.7 %late.1 = (f32[64,128]{1,0:T(8,128)S(1)}, f32[64,128]{1,0:T(8,128)S(1)}, f32[64,128]{1,0:T(8,128)S(1)}, f32[64,128]{1,0:T(8,128)S(1)}) custom-call(f32[72,128]{1,0:T(8,128)S(1)} %coeffs.1.refs_4_, bf16[2,128,1024]{2,1,0:T(8,128)(2,1)S(1)} %get-tuple-element.52.qv_high, bf16[2,128,1024]{2,1,0:T(8,128)(2,1)S(1)} %get-tuple-element.53.qv_low, ...), custom_call_target="tpu_custom_call" | custom-call | tf_op jit(solution)/shard_map/late/pallas_call | solution.py:333
  38.3 1.4 %collective-permute-start.14 = (f32[64,128]{1,0:T(8,128)S(1)}, f32[64,128]{1,0:T(8,128)S(1)}, u32[]{:S(2)}, u32[]{:S(2)}) collective-permute-start(f32[64,128]{1,0:T(8,128)S(1)} %get-tuple-element.65), channel_id=1, source_target_pairs={{0,12},{4,8},{8,4},{12,0},{1,13},{5,9},{9,5},{13,1},{2,14},{6,10},... | collective-permute-start | bytes 98312 | tf_op jit(solution)/shard_map/ppermute | solution.py:359
  39.7 0.8 %collective-permute-start.15 = (f32[64,128]{1,0:T(8,128)S(1)}, f32[64,128]{1,0:T(8,128)S(1)}, u32[]{:S(2)}, u32[]{:S(2)}) collective-permute-start(f32[64,128]{1,0:T(8,128)S(1)} %get-tuple-element.66), channel_id=1, source_target_pairs={{0,8},{4,12},{8,0},{12,4},{1,9},{5,13},{9,1},{13,5},{2,10},{6,14},... | collective-permute-start | bytes 98312 | tf_op jit(solution)/shard_map/ppermute | solution.py:359
  40.5 2.2 %collective-permute-start.16 = (f32[64,128]{1,0:T(8,128)S(1)}, f32[64,128]{1,0:T(8,128)S(1)}, u32[]{:S(2)}, u32[]{:S(2)}) collective-permute-start(f32[64,128]{1,0:T(8,128)S(1)} %get-tuple-element.67), channel_id=1, source_target_pairs={{0,4},{4,0},{8,12},{12,8},{1,5},{5,1},{9,13},{13,9},{2,6},{6,2},{1... | collective-permute-start | bytes 98312 | tf_op jit(solution)/shard_map/ppermute | solution.py:359
  42.7 1.0 %modes.1 = f32[64,2048]{1,0:T(8,128)} custom-call(f32[72,128]{1,0:T(8,128)S(1)} %coeffs.1.refs_4_, f32[2,128,1024]{2,1,0:T(8,128)S(1)} %get-tuple-element.49.near.refs_0_), custom_call_target="tpu_custom_call" | custom-call | tf_op jit(solution)/shard_map/modes/pallas_call | solution.py:333
  43.8 0.5 %collective-permute-done.14.refs_1_ = f32[64,128]{1,0:T(8,128)S(1)} collective-permute-done((f32[64,128]{1,0:T(8,128)S(1)}, f32[64,128]{1,0:T(8,128)S(1)}, u32[]{:S(2)}, u32[]{:S(2)}) %collective-permute-start.14) | collective-permute-done | bytes 32800 | tf_op jit(solution)/shard_map/ppermute | solution.py:359
  44.3 1.1 %collective-permute-done.15.refs_2_ = f32[64,128]{1,0:T(8,128)S(1)} collective-permute-done((f32[64,128]{1,0:T(8,128)S(1)}, f32[64,128]{1,0:T(8,128)S(1)}, u32[]{:S(2)}, u32[]{:S(2)}) %collective-permute-start.15) | collective-permute-done | bytes 32800 | tf_op jit(solution)/shard_map/ppermute | solution.py:359
  45.4 0.7 %fifth.1 = f32[64,64]{1,0:T(8,128)} custom-call(f32[64,128]{1,0:T(8,128)S(1)} %get-tuple-element.64.refs_0_, f32[64,128]{1,0:T(8,128)S(1)} %collective-permute-done.14.refs_1_, f32[64,128]{1,0:T(8,128)S(1)} %collective-permute-done.15.refs_2_, f32[64,128]{1,0:T(8,128)S(1)} %collective-permute-done.16.refs_3_, f32[72,128]{1,0:T(8,128)S(1)} %coeffs.1.refs_4_, ...), custom_call_target="tpu_custom_call" | custom-call | tf_op jit(solution)/shard_map/fifth/pallas_call | solution.py:333
  (28 shorter events, 0.2 us)
Async XLA Ops:
  0.6 15.2 %copy-start = (f32[16,128,128]{2,1,0:T(8,128)S(1)}, f32[16,128,128]{2,1,0:T(8,128)}, u32[]{:S(2)}) copy-start(f32[16,128,128]{2,1,0:T(8,128)} %precond.5) | copy-start | bytes 3145732
  0.6 8.1 %copy-start.2 = (f32[3,2048]{1,0:T(4,128)S(1)}, f32[3,2048]{1,0:T(4,128)}, u32[]{:S(2)}) copy-start(f32[3,2048]{1,0:T(4,128)} %couplings.3) | copy-start | bytes 73732
  0.6 15.1 %collective-permute-start.4 = (f32[64,2048]{1,0:T(8,128)}, f32[64,2048]{1,0:T(8,128)S(1)}, u32[]{:S(2)}, u32[]{:S(2)}) collective-permute-start(f32[64,2048]{1,0:T(8,128)} %forces.3), channel_id=1, source_target_pairs={{0,2},{1,3},{2,0},{3,1},{4,6},{5,7},{6,4},{7,5},{8,10},{9,11},{10,... | collective-permute-start | bytes 1572872 | tf_op jit(solution)/shard_map/ppermute | solution.py:359
  5.5 10.3 %copy-start.3 = (f32[2048]{0:T(1024)S(1)}, f32[2048]{0:T(1024)}, u32[]{:S(2)}) copy-start(f32[2048]{0:T(1024)} %param.6) | copy-start | bytes 24580
  5.5 3.4 %collective-permute-start.2 = (f32[64,1024]{1,0:T(8,128)S(1)}, f32[64,1024]{1,0:T(8,128)S(1)}, u32[]{:S(2)}, u32[]{:S(2)}) collective-permute-start(f32[64,1024]{1,0:T(8,128)S(1)} %get-tuple-element.35.d_a), channel_id=1, source_target_pairs={{0,1},{1,0},{2,3},{3,2},{4,8},{5,9},{6,10},{7,11},{8,4},{9,5},{10,... | collective-permute-start | bytes 786440 | tf_op jit(solution)/shard_map/ppermute | solution.py:355
  5.6 8.9 %collective-permute-start.3 = (f32[64,1024]{1,0:T(8,128)S(1)}, f32[64,1024]{1,0:T(8,128)S(1)}, u32[]{:S(2)}, u32[]{:S(2)}) collective-permute-start(f32[64,1024]{1,0:T(8,128)S(1)} %get-tuple-element.36.d_b), channel_id=1, source_target_pairs={{0,4},{1,5},{2,6},{3,7},{4,0},{5,1},{6,2},{7,3},{8,12},{9,13},{10,... | collective-permute-start | bytes 786440 | tf_op jit(solution)/shard_map/ppermute | solution.py:355
  8.8 7.0 %collective-permute-start.1 = (f32[1,1024]{1,0:T(1,128)S(1)}, f32[1,1024]{1,0:T(1,128)S(1)}, u32[]{:S(2)}, u32[]{:S(2)}) collective-permute-start(f32[1,1024]{1,0:T(1,128)S(1)} %slice.3), channel_id=1, source_target_pairs={{0,4},{1,5},{2,6},{3,7},{4,0},{5,1},{6,2},{7,3},{8,12},{9,13},{10,... | collective-permute-start | bytes 12296 | tf_op jit(solution)/shard_map/ppermute | solution.py:355
  8.8 7.0 %collective-permute-start = (f32[1,1024]{1,0:T(1,128)S(1)}, f32[1,1024]{1,0:T(1,128)S(1)}, u32[]{:S(2)}, u32[]{:S(2)}) collective-permute-start(f32[1,1024]{1,0:T(1,128)S(1)} %slice.3), channel_id=1, source_target_pairs={{0,1},{1,0},{2,3},{3,2},{4,8},{5,9},{6,10},{7,11},{8,4},{9,5},{10,... | collective-permute-start | bytes 12296 | tf_op jit(solution)/shard_map/ppermute | solution.py:355
  16.8 10.2 %collective-permute-start.7 = (f32[2,128,1024]{2,1,0:T(8,128)S(1)}, f32[2,128,1024]{2,1,0:T(8,128)S(1)}, u32[]{:S(2)}, u32[]{:S(2)}) collective-permute-start(f32[2,128,1024]{2,1,0:T(8,128)S(1)} %get-tuple-element.49.near.refs_0_), channel_id=1, source_target_pairs={{0,1},{1,0},{2,3},{3,2},{4,5},{5,4},{6,7},{7,6},{8,9},{9,8},{10,11... | collective-permute-start | bytes 3145736 | tf_op jit(solution)/shard_map/ppermute | solution.py:359
  16.9 5.5 %collective-permute-start.5 = (f32[64,1024]{1,0:T(8,128)S(1)}, f32[64,1024]{1,0:T(8,128)S(1)}, u32[]{:S(2)}, u32[]{:S(2)}) collective-permute-start(f32[64,1024]{1,0:T(8,128)S(1)} %get-tuple-element.39.w_a), channel_id=1, source_target_pairs={{0,1},{1,0},{2,3},{3,2},{4,8},{5,9},{6,10},{7,11},{8,4},{9,5},{10,... | collective-permute-start | bytes 786440 | tf_op jit(solution)/shard_map/ppermute | solution.py:355
  17.4 9.6 %copy-start.1 = (f32[64,2048]{1,0:T(8,128)S(1)}, f32[64,2048]{1,0:T(8,128)}, u32[]{:S(2)}) copy-start(f32[64,2048]{1,0:T(8,128)} %forces.3) | copy-start | bytes 1572868
  17.4 9.6 %collective-permute-start.6 = (f32[64,1024]{1,0:T(8,128)S(1)}, f32[64,1024]{1,0:T(8,128)S(1)}, u32[]{:S(2)}, u32[]{:S(2)}) collective-permute-start(f32[64,1024]{1,0:T(8,128)S(1)} %get-tuple-element.40.w_b), channel_id=1, source_target_pairs={{0,4},{1,5},{2,6},{3,7},{4,0},{5,1},{6,2},{7,3},{8,12},{9,13},{10,... | collective-permute-start | bytes 786440 | tf_op jit(solution)/shard_map/ppermute | solution.py:355
  20.9 13.7 %collective-permute-start.9 = (f32[2,64,1024]{2,1,0:T(8,128)S(1)}, f32[2,64,1024]{2,1,0:T(8,128)S(1)}, u32[]{:S(2)}, u32[]{:S(2)}) collective-permute-start(f32[2,64,1024]{2,1,0:T(8,128)S(1)} %get-tuple-element.44), channel_id=1, source_target_pairs={{0,2},{1,3},{2,0},{3,1},{4,6},{5,7},{6,4},{7,5},{8,10},{9,11},{10,... | collective-permute-start | bytes 1572872 | tf_op jit(solution)/shard_map/ppermute | solution.py:359
  27.0 7.7 %collective-permute-start.8 = (f32[2,64,1024]{2,1,0:T(8,128)S(1)}, f32[2,64,1024]{2,1,0:T(8,128)S(1)}, u32[]{:S(2)}, u32[]{:S(2)}) collective-permute-start(f32[2,64,1024]{2,1,0:T(8,128)S(1)} %other.1.refs_0_), channel_id=1, source_target_pairs={{0,1},{1,0},{2,3},{3,2},{4,5},{5,4},{6,7},{7,6},{8,9},{9,8},{10,11... | collective-permute-start | bytes 1572872 | tf_op jit(solution)/shard_map/ppermute | solution.py:359
  28.1 7.2 %collective-permute-start.12 = (f32[8,128]{1,0:T(8,128)S(1)}, f32[8,128]{1,0:T(8,128)S(1)}, u32[]{:S(2)}, u32[]{:S(2)}) collective-permute-start(f32[8,128]{1,0:T(8,128)S(1)} %get-tuple-element.57.refs_0_), channel_id=1, source_target_pairs={{0,12},{4,8},{8,4},{12,0},{1,13},{5,9},{9,5},{13,1},{2,14},{6,10},... | collective-permute-start | bytes 12296 | tf_op jit(solution)/shard_map/ppermute | solution.py:359
  30.6 4.6 %collective-permute-start.11 = (f32[8,128]{1,0:T(8,128)S(1)}, f32[8,128]{1,0:T(8,128)S(1)}, u32[]{:S(2)}, u32[]{:S(2)}) collective-permute-start(f32[8,128]{1,0:T(8,128)S(1)} %get-tuple-element.57.refs_0_), channel_id=1, source_target_pairs={{0,8},{4,12},{8,0},{12,4},{1,9},{5,13},{9,1},{13,5},{2,10},{6,14},... | collective-permute-start | bytes 12296 | tf_op jit(solution)/shard_map/ppermute | solution.py:359
  31.3 4.0 %collective-permute-start.10 = (f32[8,128]{1,0:T(8,128)S(1)}, f32[8,128]{1,0:T(8,128)S(1)}, u32[]{:S(2)}, u32[]{:S(2)}) collective-permute-start(f32[8,128]{1,0:T(8,128)S(1)} %get-tuple-element.57.refs_0_), channel_id=1, source_target_pairs={{0,4},{4,0},{8,12},{12,8},{1,5},{5,1},{9,13},{13,9},{2,6},{6,2},{1... | collective-permute-start | bytes 12296 | tf_op jit(solution)/shard_map/ppermute | solution.py:359
  35.3 2.3 %collective-permute-start.13 = (f32[2,64,1024]{2,1,0:T(8,128)S(1)}, f32[2,64,1024]{2,1,0:T(8,128)S(1)}, u32[]{:S(2)}, u32[]{:S(2)}) collective-permute-start(f32[2,64,1024]{2,1,0:T(8,128)S(1)} %collective-permute-done.9.refs_0_), channel_id=1, source_target_pairs={{0,1},{1,0},{2,3},{3,2},{4,5},{5,4},{6,7},{7,6},{8,9},{9,8},{10,11... | collective-permute-start | bytes 1572872 | tf_op jit(solution)/shard_map/ppermute | solution.py:359
  35.4 5.1 %collective-permute-start.19 = (f32[72,128]{1,0:T(8,128)S(1)}, f32[72,128]{1,0:T(8,128)S(1)}, u32[]{:S(2)}, u32[]{:S(2)}) collective-permute-start(f32[72,128]{1,0:T(8,128)S(1)} %coeffs.1.refs_4_), channel_id=1, source_target_pairs={{0,3},{1,2},{2,1},{3,0},{4,7},{5,6},{6,5},{7,4},{8,11},{9,10},{10,... | collective-permute-start | bytes 110600 | tf_op jit(solution)/shard_map/ppermute | solution.py:359
  37.1 6.7 %collective-permute-start.18 = (f32[72,128]{1,0:T(8,128)S(1)}, f32[72,128]{1,0:T(8,128)S(1)}, u32[]{:S(2)}, u32[]{:S(2)}) collective-permute-start(f32[72,128]{1,0:T(8,128)S(1)} %coeffs.1.refs_4_), channel_id=1, source_target_pairs={{0,2},{1,3},{2,0},{3,1},{4,6},{5,7},{6,4},{7,5},{8,10},{9,11},{10,... | collective-permute-start | bytes 110600 | tf_op jit(solution)/shard_map/ppermute | solution.py:359
  37.6 6.2 %collective-permute-start.17 = (f32[72,128]{1,0:T(8,128)S(1)}, f32[72,128]{1,0:T(8,128)S(1)}, u32[]{:S(2)}, u32[]{:S(2)}) collective-permute-start(f32[72,128]{1,0:T(8,128)S(1)} %coeffs.1.refs_4_), channel_id=1, source_target_pairs={{0,1},{1,0},{2,3},{3,2},{4,5},{5,4},{6,7},{7,6},{8,9},{9,8},{10,11... | collective-permute-start | bytes 110600 | tf_op jit(solution)/shard_map/ppermute | solution.py:359
  38.3 6.0 %collective-permute-start.14 = (f32[64,128]{1,0:T(8,128)S(1)}, f32[64,128]{1,0:T(8,128)S(1)}, u32[]{:S(2)}, u32[]{:S(2)}) collective-permute-start(f32[64,128]{1,0:T(8,128)S(1)} %get-tuple-element.65), channel_id=1, source_target_pairs={{0,12},{4,8},{8,4},{12,0},{1,13},{5,9},{9,5},{13,1},{2,14},{6,10},... | collective-permute-start | bytes 98312 | tf_op jit(solution)/shard_map/ppermute | solution.py:359
  39.7 5.6 %collective-permute-start.15 = (f32[64,128]{1,0:T(8,128)S(1)}, f32[64,128]{1,0:T(8,128)S(1)}, u32[]{:S(2)}, u32[]{:S(2)}) collective-permute-start(f32[64,128]{1,0:T(8,128)S(1)} %get-tuple-element.66), channel_id=1, source_target_pairs={{0,8},{4,12},{8,0},{12,4},{1,9},{5,13},{9,1},{13,5},{2,10},{6,14},... | collective-permute-start | bytes 98312 | tf_op jit(solution)/shard_map/ppermute | solution.py:359
  40.5 4.8 %collective-permute-start.16 = (f32[64,128]{1,0:T(8,128)S(1)}, f32[64,128]{1,0:T(8,128)S(1)}, u32[]{:S(2)}, u32[]{:S(2)}) collective-permute-start(f32[64,128]{1,0:T(8,128)S(1)} %get-tuple-element.67), channel_id=1, source_target_pairs={{0,4},{4,0},{8,12},{12,8},{1,5},{5,1},{9,13},{13,9},{2,6},{6,2},{1... | collective-permute-start | bytes 98312 | tf_op jit(solution)/shard_map/ppermute | solution.py:359

commit v5 on v4

--- a/solution.py
+++ b/solution.py
@@ -161,12 +161,28 @@
             out[:, chunk(k)] = block_product(field[slot, :, chunk(k)], matrices[slot, k])
 
 
-def other_kernel(forces, precond, out):
+def place_sums(packed, first, sums):
+    lane = lane_index(packed.shape[0])
+    for index, value in enumerate(sums):
+        total = jnp.sum(value, axis=1, keepdims=True)
+        packed = jnp.where(lane == first + index, total, packed)
+    return packed
+
+
+def other_kernel(forces_far, precond, forces, q, near, d_far, packed):
+    rows = forces.shape[0]
+    sums = [jnp.zeros((rows, LANES), F32) for _ in range(3)]
     for slot, plane in enumerate(slot_planes()):
         for k in range(CHUNKS):
-            out[slot, :, chunk(k)] = block_product(
-                forces[:, plane_chunk(plane, k)], precond[plane * CHUNKS + k]
-            )
+            d_far[slot, :, chunk(k)] = block_product(
+                forces_far[:, plane_chunk(plane, k)], precond[plane * CHUNKS + k]
+            )
+            d_here = near[slot, 0:rows, chunk(k)]
+            q_here = q[slot, :, chunk(k)]
+            sums[0] += forces[:, plane_chunk(plane, k)] * d_here
+            sums[1] += d_here * q_here
+            sums[2] += q_here * near[slot, rows : 2 * rows, chunk(k)]
+    packed[...] = place_sums(jnp.zeros((rows, LANES), F32), 0, sums)
 
 
 def second_kernel(couplings, ground, before_a, before_b, precond, d_a, d_b, got_a, got_b, q, w_a, w_b, w_both, near):
@@ -184,27 +200,6 @@
             w_both[slot, :, chunk(k)] = w
             near[slot, 0:rows, chunk(k)] = fields[slot][:, chunk(k)]
             near[slot, rows : 2 * rows, chunk(k)] = w
-
-
-def place_sums(packed, first, sums):
-    lane = lane_index(packed.shape[0])
-    for index, value in enumerate(sums):
-        total = jnp.sum(value, axis=1, keepdims=True)
-        packed = jnp.where(lane == first + index, total, packed)
-    return packed
-
-
-def side_kernel(forces, q, near, packed):
-    rows = forces.shape[0]
-    sums = [jnp.zeros((rows, LANES), F32) for _ in range(3)]
-    for slot, plane in enumerate(slot_planes()):
-        for k in range(CHUNKS):
-            d_here = near[slot, 0:rows, chunk(k)]
-            q_here = q[slot, :, chunk(k)]
-            sums[0] += forces[:, plane_chunk(plane, k)] * d_here
-            sums[1] += d_here * q_here
-            sums[2] += q_here * near[slot, rows : 2 * rows, chunk(k)]
-    packed[...] = place_sums(jnp.zeros((rows, LANES), F32), 0, sums)
 
 
 def third_kernel(couplings, ground, before_a, before_b, w_a, w_b, next_a, next_b, packed, v, dots):
@@ -403,10 +398,14 @@
     next_a, next_b = neighbours(w_a, 1), neighbours(w_b, 0)
     far = swapped(w_both, "cols", top)
     near = shared(near)
-    (d_far,) = call(other_kernel, "other", (forces_far, precond), [(2,) + field])
+    d_far, packed = call(
+        other_kernel,
+        "other",
+        (forces_far, precond, forces, q, near[0]),
+        [(2,) + field, (rows, LANES)],
+    )
     next_a, next_b, d_far, near = lax.optimization_barrier((next_a, next_b, d_far, near))
     d_far = shared(d_far)
-    (packed,) = call(side_kernel, "side", (forces, q, near[0]), [(rows, LANES)])
     v, dots = call(
         third_kernel,
         "third",

time: 46.2 us -> 45.7 us (0.989)
    pallas_call x11 -> x10, Pallas kernels: 8.44 us -> 8.28 us  [call(): pl.pallas_call(kernel, out_shape=shapes, in_specs=[pl.BlockSpec(memory_sp...]
  transfers between devices with their start and end apart: 20 -> 20, of which waited for: 6 -> 8; matrix products, arithmetic and copies ran while one was open for 0% -> 0% of each run, Pallas kernels for 15% -> 14%
where the time goes in v5:
time: 45.7 us; the launch traced here: 45.6 us
  starting transfers between devices  22.4 us (49%)
  waiting for transfers between devices  14.1 us (31%)
  Pallas kernels  8.28 us (18%)
  between operations  0.78 us (2%)
    ppermute x14, starting transfers between devices, swapped(): lax.ppermute(block, axis, [(i, i ^ bit) for i in range(lax.axis_size(axis...  15.6 us
    ppermute x6, waiting for transfers between devices, neighbours(): return lax.ppermute(block, ('nodes', 'cols'), route)  10.1 us
    pallas_call x10, Pallas kernels, call(): pl.pallas_call(kernel, out_shape=shapes, in_specs=[pl.BlockSpec(memory_sp...  8.28 us
    ppermute x6, starting transfers between devices, neighbours(): return lax.ppermute(block, ('nodes', 'cols'), route)  6.82 us
    ppermute x14, waiting for transfers between devices, swapped(): lax.ppermute(block, axis, [(i, i ^ bit) for i in range(lax.axis_size(axis...  3.94 us
  transfers between devices with their start and end apart: 20, of which 8 were waited for; matrix products, arithmetic and copies ran while one was open for 0% of the time, Pallas kernels for 14%

profile of v5, /device:TPU:0, one launch (start us, length us, event | category | flops | bytes accessed | tf_op | source)
XLA Modules:
  0.0 45.6 jit_solution(423930190649197980)
XLA Ops:
  0.6 3.0 %collective-permute-start.4 = (f32[64,2048]{1,0:T(8,128)}, f32[64,2048]{1,0:T(8,128)S(1)}, u32[]{:S(2)}, u32[]{:S(2)}) collective-permute-start(f32[64,2048]{1,0:T(8,128)} %forces.3), channel_id=1, source_target_pairs={{0,2},{1,3},{2,0},{3,1},{4,6},{5,7},{6,4},{7,5},{8,10},{9,11},{10,... | collective-permute-start | bytes 1572872 | tf_op jit(solution)/shard_map/ppermute | solution.py:354
  3.7 1.8 %first.1 = (f32[64,1024]{1,0:T(8,128)S(1)}, f32[64,1024]{1,0:T(8,128)S(1)}) custom-call(f32[64,2048]{1,0:T(8,128)} %forces.3, f32[16,128,128]{2,1,0:T(8,128)} %precond.5), custom_call_target="tpu_custom_call" | custom-call | tf_op jit(solution)/shard_map/first/pallas_call | solution.py:328
  5.5 0.1 collective-permute-start.2
  5.6 3.1 %collective-permute-start.3 = (f32[64,1024]{1,0:T(8,128)S(1)}, f32[64,1024]{1,0:T(8,128)S(1)}, u32[]{:S(2)}, u32[]{:S(2)}) collective-permute-start(f32[64,1024]{1,0:T(8,128)S(1)} %get-tuple-element.38.d_b), channel_id=1, source_target_pairs={{0,4},{1,5},{2,6},{3,7},{4,0},{5,1},{6,2},{7,3},{8,12},{9,13},{10,... | collective-permute-start | bytes 786440 | tf_op jit(solution)/shard_map/ppermute | solution.py:350
  8.8 0.1 collective-permute-start
  8.9 5.6 %collective-permute-done.3.got_b = f32[64,1024]{1,0:T(8,128)S(1)} collective-permute-done((f32[64,1024]{1,0:T(8,128)S(1)}, f32[64,1024]{1,0:T(8,128)S(1)}, u32[]{:S(2)}, u32[]{:S(2)}) %collective-permute-start.3) | collective-permute-done | bytes 262176 | tf_op jit(solution)/shard_map/ppermute | solution.py:350
  14.5 1.3 %collective-permute-done.4.forces_far = f32[64,2048]{1,0:T(8,128)S(1)} collective-permute-done((f32[64,2048]{1,0:T(8,128)}, f32[64,2048]{1,0:T(8,128)S(1)}, u32[]{:S(2)}, u32[]{:S(2)}) %collective-permute-start.4) | collective-permute-done | bytes 524320 | tf_op jit(solution)/shard_map/ppermute | solution.py:354
  15.8 1.0 %second.1 = (f32[2,64,1024]{2,1,0:T(8,128)S(1)}, f32[64,1024]{1,0:T(8,128)S(1)}, f32[64,1024]{1,0:T(8,128)S(1)}, f32[2,64,1024]{2,1,0:T(8,128)S(1)}, f32[2,128,1024]{2,1,0:T(8,128)S(1)}) custom-call(f32[3,2048]{1,0:T(4,128)S(1)} %copy-done.2, f32[1,2048]{1,0:T(1,128)S(1)} %bitcast.1, f32[1,1024]{1,0:T(1,128)S(1)} %collective-permute-done.before_a, ...), custom_call_target="tpu_custom_call" | custom-call | tf_op jit(solution)/shard_map/second/pallas_call | solution.py:328
  16.8 0.1 collective-permute-start.7
  16.9 0.5 %collective-permute-start.5 = (f32[64,1024]{1,0:T(8,128)S(1)}, f32[64,1024]{1,0:T(8,128)S(1)}, u32[]{:S(2)}, u32[]{:S(2)}) collective-permute-start(f32[64,1024]{1,0:T(8,128)S(1)} %get-tuple-element.41.w_a), channel_id=1, source_target_pairs={{0,1},{1,0},{2,3},{3,2},{4,8},{5,9},{6,10},{7,11},{8,4},{9,5},{10,... | collective-permute-start | bytes 786440 | tf_op jit(solution)/shard_map/ppermute | solution.py:350
  17.4 3.0 %collective-permute-start.6 = (f32[64,1024]{1,0:T(8,128)S(1)}, f32[64,1024]{1,0:T(8,128)S(1)}, u32[]{:S(2)}, u32[]{:S(2)}) collective-permute-start(f32[64,1024]{1,0:T(8,128)S(1)} %get-tuple-element.42.w_b), channel_id=1, source_target_pairs={{0,4},{1,5},{2,6},{3,7},{4,0},{5,1},{6,2},{7,3},{8,12},{9,13},{10,... | collective-permute-start | bytes 786440 | tf_op jit(solution)/shard_map/ppermute | solution.py:350
  20.4 1.5 %collective-permute-start.9 = (f32[2,64,1024]{2,1,0:T(8,128)S(1)}, f32[2,64,1024]{2,1,0:T(8,128)S(1)}, u32[]{:S(2)}, u32[]{:S(2)}) collective-permute-start(f32[2,64,1024]{2,1,0:T(8,128)S(1)} %get-tuple-element.48), channel_id=1, source_target_pairs={{0,2},{1,3},{2,0},{3,1},{4,6},{5,7},{6,4},{7,5},{8,10},{9,11},{10,... | collective-permute-start | bytes 1572872 | tf_op jit(solution)/shard_map/ppermute | solution.py:354
  21.9 0.6 %other.1 = (f32[2,64,1024]{2,1,0:T(8,128)S(1)}, f32[64,128]{1,0:T(8,128)S(1)}) custom-call(f32[64,2048]{1,0:T(8,128)S(1)} %collective-permute-done.4.forces_far, f32[16,128,128]{2,1,0:T(8,128)S(1)} %copy-done, f32[64,2048]{1,0:T(8,128)S(1)} %copy-done.1, f32[2,64,1024]{2,1,0:T(8,128)S(1)} %get-tuple-element.44.q, ...), custom_call_target="tpu_custom_call" | custom-call | tf_op jit(solution)/shard_map/other/pallas_call | solution.py:328
  22.5 4.5 %collective-permute-done.6.next_b = f32[64,1024]{1,0:T(8,128)S(1)} collective-permute-done((f32[64,1024]{1,0:T(8,128)S(1)}, f32[64,1024]{1,0:T(8,128)S(1)}, u32[]{:S(2)}, u32[]{:S(2)}) %collective-permute-start.6) | collective-permute-done | bytes 262176 | tf_op jit(solution)/shard_map/ppermute | solution.py:350
  27.0 0.8 %third.1 = (f32[2,64,1024]{2,1,0:T(8,128)S(1)}, f32[8,128]{1,0:T(8,128)S(1)}) custom-call(f32[3,2048]{1,0:T(4,128)S(1)} %copy-done.2, f32[1,2048]{1,0:T(1,128)S(1)} %bitcast.2, f32[1,1024]{1,0:T(1,128)S(1)} %collective-permute-done.before_a, f32[1,1024]{1,0:T(1,128)S(1)} %collective-permute-done.1.before_b, f32[64,1024]{1,0:T(8,128)S(1)} %get-tuple-element.41.w_a, ...), custom_call_target="tpu_custom_call" | custom-call | tf_op jit(solution)/shard_map/third/pallas_call | solution.py:328
  27.8 2.5 %collective-permute-start.12 = (f32[8,128]{1,0:T(8,128)S(1)}, f32[8,128]{1,0:T(8,128)S(1)}, u32[]{:S(2)}, u32[]{:S(2)}) collective-permute-start(f32[8,128]{1,0:T(8,128)S(1)} %get-tuple-element.61.refs_0_), channel_id=1, source_target_pairs={{0,12},{4,8},{8,4},{12,0},{1,13},{5,9},{9,5},{13,1},{2,14},{6,10},... | collective-permute-start | bytes 12296 | tf_op jit(solution)/shard_map/ppermute | solution.py:354
  30.4 0.7 %collective-permute-start.11 = (f32[8,128]{1,0:T(8,128)S(1)}, f32[8,128]{1,0:T(8,128)S(1)}, u32[]{:S(2)}, u32[]{:S(2)}) collective-permute-start(f32[8,128]{1,0:T(8,128)S(1)} %get-tuple-element.61.refs_0_), channel_id=1, source_target_pairs={{0,8},{4,12},{8,0},{12,4},{1,9},{5,13},{9,1},{13,5},{2,10},{6,14},... | collective-permute-start | bytes 12296 | tf_op jit(solution)/shard_map/ppermute | solution.py:354
  31.0 1.2 %collective-permute-start.10 = (f32[8,128]{1,0:T(8,128)S(1)}, f32[8,128]{1,0:T(8,128)S(1)}, u32[]{:S(2)}, u32[]{:S(2)}) collective-permute-start(f32[8,128]{1,0:T(8,128)S(1)} %get-tuple-element.61.refs_0_), channel_id=1, source_target_pairs={{0,4},{4,0},{8,12},{12,8},{1,5},{5,1},{9,13},{13,9},{2,6},{6,2},{1... | collective-permute-start | bytes 12296 | tf_op jit(solution)/shard_map/ppermute | solution.py:354
  32.2 1.0 %early.1 = (bf16[2,128,1024]{2,1,0:T(8,128)(2,1)S(1)}, bf16[2,128,1024]{2,1,0:T(8,128)(2,1)S(1)}, f32[2,128,128]{2,1,0:T(8,128)S(1)}) custom-call(f32[2,64,1024]{2,1,0:T(8,128)S(1)} %get-tuple-element.44.q, f32[2,64,1024]{2,1,0:T(8,128)S(1)} %get-tuple-element.53.v, f32[2,128,1024]{2,1,0:T(8,128)S(1)} %get-tuple-element.54.near.refs_0_, ...), custom_call_target="tpu_custom_call" | custom-call | tf_op jit(solution)/shard_map/early/pallas_call | solution.py:328
  33.2 0.9 %collective-permute-done.9.refs_0_ = f32[2,64,1024]{2,1,0:T(8,128)S(1)} collective-permute-done((f32[2,64,1024]{2,1,0:T(8,128)S(1)}, f32[2,64,1024]{2,1,0:T(8,128)S(1)}, u32[]{:S(2)}, u32[]{:S(2)}) %collective-permute-start.9) | collective-permute-done | bytes 524320 | tf_op jit(solution)/shard_map/ppermute | solution.py:354
  34.1 0.6 %far.1.far_gram = f32[128,128]{1,0:T(8,128)S(1)} custom-call(bf16[2,128,1024]{2,1,0:T(8,128)(2,1)S(1)} %get-tuple-element.56.qv_high, bf16[2,128,1024]{2,1,0:T(8,128)(2,1)S(1)} %get-tuple-element.57.qv_low, f32[2,64,1024]{2,1,0:T(8,128)S(1)} %get-tuple-element.58.refs_0_, f32[2,64,1024]{2,1,0:T(8,128)S(1)} %collective-permute-done.8.refs_1_), custom_call_target="tpu_custom_call" | custom-call | tf_op jit(solution)/shard_map/far/pallas_call | solution.py:328
  34.7 0.2 collective-permute-done.11.refs_2_
  34.9 1.7 %collective-permute-start.19 = (f32[72,128]{1,0:T(8,128)S(1)}, f32[72,128]{1,0:T(8,128)S(1)}, u32[]{:S(2)}, u32[]{:S(2)}) collective-permute-start(f32[72,128]{1,0:T(8,128)S(1)} %coeffs.1.refs_4_), channel_id=1, source_target_pairs={{0,3},{1,2},{2,1},{3,0},{4,7},{5,6},{6,5},{7,4},{8,11},{9,10},{10,... | collective-permute-start | bytes 110600 | tf_op jit(solution)/shard_map/ppermute | solution.py:354
  36.6 0.5 %collective-permute-start.18 = (f32[72,128]{1,0:T(8,128)S(1)}, f32[72,128]{1,0:T(8,128)S(1)}, u32[]{:S(2)}, u32[]{:S(2)}) collective-permute-start(f32[72,128]{1,0:T(8,128)S(1)} %coeffs.1.refs_4_), channel_id=1, source_target_pairs={{0,2},{1,3},{2,0},{3,1},{4,6},{5,7},{6,4},{7,5},{8,10},{9,11},{10,... | collective-permute-start | bytes 110600 | tf_op jit(solution)/shard_map/ppermute | solution.py:354
  37.1 0.7 %late.1 = (f32[64,128]{1,0:T(8,128)S(1)}, f32[64,128]{1,0:T(8,128)S(1)}, f32[64,128]{1,0:T(8,128)S(1)}, f32[64,128]{1,0:T(8,128)S(1)}) custom-call(f32[72,128]{1,0:T(8,128)S(1)} %coeffs.1.refs_4_, bf16[2,128,1024]{2,1,0:T(8,128)(2,1)S(1)} %get-tuple-element.56.qv_high, bf16[2,128,1024]{2,1,0:T(8,128)(2,1)S(1)} %get-tuple-element.57.qv_low, ...), custom_call_target="tpu_custom_call" | custom-call | tf_op jit(solution)/shard_map/late/pallas_call | solution.py:328
  37.8 1.6 %collective-permute-start.14 = (f32[64,128]{1,0:T(8,128)S(1)}, f32[64,128]{1,0:T(8,128)S(1)}, u32[]{:S(2)}, u32[]{:S(2)}) collective-permute-start(f32[64,128]{1,0:T(8,128)S(1)} %get-tuple-element.69), channel_id=1, source_target_pairs={{0,12},{4,8},{8,4},{12,0},{1,13},{5,9},{9,5},{13,1},{2,14},{6,10},... | collective-permute-start | bytes 98312 | tf_op jit(solution)/shard_map/ppermute | solution.py:354
  39.5 0.8 %collective-permute-start.15 = (f32[64,128]{1,0:T(8,128)S(1)}, f32[64,128]{1,0:T(8,128)S(1)}, u32[]{:S(2)}, u32[]{:S(2)}) collective-permute-start(f32[64,128]{1,0:T(8,128)S(1)} %get-tuple-element.70), channel_id=1, source_target_pairs={{0,8},{4,12},{8,0},{12,4},{1,9},{5,13},{9,1},{13,5},{2,10},{6,14},... | collective-permute-start | bytes 98312 | tf_op jit(solution)/shard_map/ppermute | solution.py:354
  40.3 2.0 %collective-permute-start.16 = (f32[64,128]{1,0:T(8,128)S(1)}, f32[64,128]{1,0:T(8,128)S(1)}, u32[]{:S(2)}, u32[]{:S(2)}) collective-permute-start(f32[64,128]{1,0:T(8,128)S(1)} %get-tuple-element.71), channel_id=1, source_target_pairs={{0,4},{4,0},{8,12},{12,8},{1,5},{5,1},{9,13},{13,9},{2,6},{6,2},{1... | collective-permute-start | bytes 98312 | tf_op jit(solution)/shard_map/ppermute | solution.py:354
  42.3 1.0 %modes.1 = f32[64,2048]{1,0:T(8,128)} custom-call(f32[72,128]{1,0:T(8,128)S(1)} %coeffs.1.refs_4_, f32[2,128,1024]{2,1,0:T(8,128)S(1)} %get-tuple-element.54.near.refs_0_), custom_call_target="tpu_custom_call" | custom-call | tf_op jit(solution)/shard_map/modes/pallas_call | solution.py:328
  43.3 0.5 %collective-permute-done.14.refs_1_ = f32[64,128]{1,0:T(8,128)S(1)} collective-permute-done((f32[64,128]{1,0:T(8,128)S(1)}, f32[64,128]{1,0:T(8,128)S(1)}, u32[]{:S(2)}, u32[]{:S(2)}) %collective-permute-start.14) | collective-permute-done | bytes 32800 | tf_op jit(solution)/shard_map/ppermute | solution.py:354
  43.8 1.1 %collective-permute-done.15.refs_2_ = f32[64,128]{1,0:T(8,128)S(1)} collective-permute-done((f32[64,128]{1,0:T(8,128)S(1)}, f32[64,128]{1,0:T(8,128)S(1)}, u32[]{:S(2)}, u32[]{:S(2)}) %collective-permute-start.15) | collective-permute-done | bytes 32800 | tf_op jit(solution)/shard_map/ppermute | solution.py:354
  44.9 0.7 %fifth.1 = f32[64,64]{1,0:T(8,128)} custom-call(f32[64,128]{1,0:T(8,128)S(1)} %get-tuple-element.68.refs_0_, f32[64,128]{1,0:T(8,128)S(1)} %collective-permute-done.14.refs_1_, f32[64,128]{1,0:T(8,128)S(1)} %collective-permute-done.15.refs_2_, f32[64,128]{1,0:T(8,128)S(1)} %collective-permute-done.16.refs_3_, f32[72,128]{1,0:T(8,128)S(1)} %coeffs.1.refs_4_, ...), custom_call_target="tpu_custom_call" | custom-call | tf_op jit(solution)/shard_map/fifth/pallas_call | solution.py:328
  (27 shorter events, 0.2 us)
Async XLA Ops:
  0.6 15.2 %copy-start = (f32[16,128,128]{2,1,0:T(8,128)S(1)}, f32[16,128,128]{2,1,0:T(8,128)}, u32[]{:S(2)}) copy-start(f32[16,128,128]{2,1,0:T(8,128)} %precond.5) | copy-start | bytes 3145732
  0.6 8.1 %copy-start.2 = (f32[3,2048]{1,0:T(4,128)S(1)}, f32[3,2048]{1,0:T(4,128)}, u32[]{:S(2)}) copy-start(f32[3,2048]{1,0:T(4,128)} %couplings.3) | copy-start | bytes 73732
  0.6 15.1 %collective-permute-start.4 = (f32[64,2048]{1,0:T(8,128)}, f32[64,2048]{1,0:T(8,128)S(1)}, u32[]{:S(2)}, u32[]{:S(2)}) collective-permute-start(f32[64,2048]{1,0:T(8,128)} %forces.3), channel_id=1, source_target_pairs={{0,2},{1,3},{2,0},{3,1},{4,6},{5,7},{6,4},{7,5},{8,10},{9,11},{10,... | collective-permute-start | bytes 1572872 | tf_op jit(solution)/shard_map/ppermute | solution.py:354
  5.5 10.3 %copy-start.3 = (f32[2048]{0:T(1024)S(1)}, f32[2048]{0:T(1024)}, u32[]{:S(2)}) copy-start(f32[2048]{0:T(1024)} %param.6) | copy-start | bytes 24580
  5.5 3.4 %collective-permute-start.2 = (f32[64,1024]{1,0:T(8,128)S(1)}, f32[64,1024]{1,0:T(8,128)S(1)}, u32[]{:S(2)}, u32[]{:S(2)}) collective-permute-start(f32[64,1024]{1,0:T(8,128)S(1)} %get-tuple-element.37.d_a), channel_id=1, source_target_pairs={{0,1},{1,0},{2,3},{3,2},{4,8},{5,9},{6,10},{7,11},{8,4},{9,5},{10,... | collective-permute-start | bytes 786440 | tf_op jit(solution)/shard_map/ppermute | solution.py:350
  5.6 8.9 %collective-permute-start.3 = (f32[64,1024]{1,0:T(8,128)S(1)}, f32[64,1024]{1,0:T(8,128)S(1)}, u32[]{:S(2)}, u32[]{:S(2)}) collective-permute-start(f32[64,1024]{1,0:T(8,128)S(1)} %get-tuple-element.38.d_b), channel_id=1, source_target_pairs={{0,4},{1,5},{2,6},{3,7},{4,0},{5,1},{6,2},{7,3},{8,12},{9,13},{10,... | collective-permute-start | bytes 786440 | tf_op jit(solution)/shard_map/ppermute | solution.py:350
  8.8 7.0 %collective-permute-start.1 = (f32[1,1024]{1,0:T(1,128)S(1)}, f32[1,1024]{1,0:T(1,128)S(1)}, u32[]{:S(2)}, u32[]{:S(2)}) collective-permute-start(f32[1,1024]{1,0:T(1,128)S(1)} %slice.3), channel_id=1, source_target_pairs={{0,4},{1,5},{2,6},{3,7},{4,0},{5,1},{6,2},{7,3},{8,12},{9,13},{10,... | collective-permute-start | bytes 12296 | tf_op jit(solution)/shard_map/ppermute | solution.py:350
  8.8 7.0 %collective-permute-start = (f32[1,1024]{1,0:T(1,128)S(1)}, f32[1,1024]{1,0:T(1,128)S(1)}, u32[]{:S(2)}, u32[]{:S(2)}) collective-permute-start(f32[1,1024]{1,0:T(1,128)S(1)} %slice.3), channel_id=1, source_target_pairs={{0,1},{1,0},{2,3},{3,2},{4,8},{5,9},{6,10},{7,11},{8,4},{9,5},{10,... | collective-permute-start | bytes 12296 | tf_op jit(solution)/shard_map/ppermute | solution.py:350
  15.8 6.1 %copy-start.1 = (f32[64,2048]{1,0:T(8,128)S(1)}, f32[64,2048]{1,0:T(8,128)}, u32[]{:S(2)}) copy-start(f32[64,2048]{1,0:T(8,128)} %forces.3) | copy-start | bytes 1572868
  16.8 10.2 %collective-permute-start.7 = (f32[2,128,1024]{2,1,0:T(8,128)S(1)}, f32[2,128,1024]{2,1,0:T(8,128)S(1)}, u32[]{:S(2)}, u32[]{:S(2)}) collective-permute-start(f32[2,128,1024]{2,1,0:T(8,128)S(1)} %get-tuple-element.54.near.refs_0_), channel_id=1, source_target_pairs={{0,1},{1,0},{2,3},{3,2},{4,5},{5,4},{6,7},{7,6},{8,9},{9,8},{10,11... | collective-permute-start | bytes 3145736 | tf_op jit(solution)/shard_map/ppermute | solution.py:354
  16.9 5.6 %collective-permute-start.5 = (f32[64,1024]{1,0:T(8,128)S(1)}, f32[64,1024]{1,0:T(8,128)S(1)}, u32[]{:S(2)}, u32[]{:S(2)}) collective-permute-start(f32[64,1024]{1,0:T(8,128)S(1)} %get-tuple-element.41.w_a), channel_id=1, source_target_pairs={{0,1},{1,0},{2,3},{3,2},{4,8},{5,9},{6,10},{7,11},{8,4},{9,5},{10,... | collective-permute-start | bytes 786440 | tf_op jit(solution)/shard_map/ppermute | solution.py:350
  17.4 9.6 %collective-permute-start.6 = (f32[64,1024]{1,0:T(8,128)S(1)}, f32[64,1024]{1,0:T(8,128)S(1)}, u32[]{:S(2)}, u32[]{:S(2)}) collective-permute-start(f32[64,1024]{1,0:T(8,128)S(1)} %get-tuple-element.42.w_b), channel_id=1, source_target_pairs={{0,4},{1,5},{2,6},{3,7},{4,0},{5,1},{6,2},{7,3},{8,12},{9,13},{10,... | collective-permute-start | bytes 786440 | tf_op jit(solution)/shard_map/ppermute | solution.py:350
  20.4 13.7 %collective-permute-start.9 = (f32[2,64,1024]{2,1,0:T(8,128)S(1)}, f32[2,64,1024]{2,1,0:T(8,128)S(1)}, u32[]{:S(2)}, u32[]{:S(2)}) collective-permute-start(f32[2,64,1024]{2,1,0:T(8,128)S(1)} %get-tuple-element.48), channel_id=1, source_target_pairs={{0,2},{1,3},{2,0},{3,1},{4,6},{5,7},{6,4},{7,5},{8,10},{9,11},{10,... | collective-permute-start | bytes 1572872 | tf_op jit(solution)/shard_map/ppermute | solution.py:354
  27.0 7.1 %collective-permute-start.8 = (f32[2,64,1024]{2,1,0:T(8,128)S(1)}, f32[2,64,1024]{2,1,0:T(8,128)S(1)}, u32[]{:S(2)}, u32[]{:S(2)}) collective-permute-start(f32[2,64,1024]{2,1,0:T(8,128)S(1)} %get-tuple-element.58.refs_0_), channel_id=1, source_target_pairs={{0,1},{1,0},{2,3},{3,2},{4,5},{5,4},{6,7},{7,6},{8,9},{9,8},{10,11... | collective-permute-start | bytes 1572872 | tf_op jit(solution)/shard_map/ppermute | solution.py:354
  27.8 6.9 %collective-permute-start.12 = (f32[8,128]{1,0:T(8,128)S(1)}, f32[8,128]{1,0:T(8,128)S(1)}, u32[]{:S(2)}, u32[]{:S(2)}) collective-permute-start(f32[8,128]{1,0:T(8,128)S(1)} %get-tuple-element.61.refs_0_), channel_id=1, source_target_pairs={{0,12},{4,8},{8,4},{12,0},{1,13},{5,9},{9,5},{13,1},{2,14},{6,10},... | collective-permute-start | bytes 12296 | tf_op jit(solution)/shard_map/ppermute | solution.py:354
  30.4 4.5 %collective-permute-start.11 = (f32[8,128]{1,0:T(8,128)S(1)}, f32[8,128]{1,0:T(8,128)S(1)}, u32[]{:S(2)}, u32[]{:S(2)}) collective-permute-start(f32[8,128]{1,0:T(8,128)S(1)} %get-tuple-element.61.refs_0_), channel_id=1, source_target_pairs={{0,8},{4,12},{8,0},{12,4},{1,9},{5,13},{9,1},{13,5},{2,10},{6,14},... | collective-permute-start | bytes 12296 | tf_op jit(solution)/shard_map/ppermute | solution.py:354
  31.0 3.8 %collective-permute-start.10 = (f32[8,128]{1,0:T(8,128)S(1)}, f32[8,128]{1,0:T(8,128)S(1)}, u32[]{:S(2)}, u32[]{:S(2)}) collective-permute-start(f32[8,128]{1,0:T(8,128)S(1)} %get-tuple-element.61.refs_0_), channel_id=1, source_target_pairs={{0,4},{4,0},{8,12},{12,8},{1,5},{5,1},{9,13},{13,9},{2,6},{6,2},{1... | collective-permute-start | bytes 12296 | tf_op jit(solution)/shard_map/ppermute | solution.py:354
  34.9 2.2 %collective-permute-start.13 = (f32[2,64,1024]{2,1,0:T(8,128)S(1)}, f32[2,64,1024]{2,1,0:T(8,128)S(1)}, u32[]{:S(2)}, u32[]{:S(2)}) collective-permute-start(f32[2,64,1024]{2,1,0:T(8,128)S(1)} %collective-permute-done.9.refs_0_), channel_id=1, source_target_pairs={{0,1},{1,0},{2,3},{3,2},{4,5},{5,4},{6,7},{7,6},{8,9},{9,8},{10,11... | collective-permute-start | bytes 1572872 | tf_op jit(solution)/shard_map/ppermute | solution.py:354
  34.9 5.4 %collective-permute-start.19 = (f32[72,128]{1,0:T(8,128)S(1)}, f32[72,128]{1,0:T(8,128)S(1)}, u32[]{:S(2)}, u32[]{:S(2)}) collective-permute-start(f32[72,128]{1,0:T(8,128)S(1)} %coeffs.1.refs_4_), channel_id=1, source_target_pairs={{0,3},{1,2},{2,1},{3,0},{4,7},{5,6},{6,5},{7,4},{8,11},{9,10},{10,... | collective-permute-start | bytes 110600 | tf_op jit(solution)/shard_map/ppermute | solution.py:354
  36.6 6.7 %collective-permute-start.18 = (f32[72,128]{1,0:T(8,128)S(1)}, f32[72,128]{1,0:T(8,128)S(1)}, u32[]{:S(2)}, u32[]{:S(2)}) collective-permute-start(f32[72,128]{1,0:T(8,128)S(1)} %coeffs.1.refs_4_), channel_id=1, source_target_pairs={{0,2},{1,3},{2,0},{3,1},{4,6},{5,7},{6,4},{7,5},{8,10},{9,11},{10,... | collective-permute-start | bytes 110600 | tf_op jit(solution)/shard_map/ppermute | solution.py:354
  37.1 6.2 %collective-permute-start.17 = (f32[72,128]{1,0:T(8,128)S(1)}, f32[72,128]{1,0:T(8,128)S(1)}, u32[]{:S(2)}, u32[]{:S(2)}) collective-permute-start(f32[72,128]{1,0:T(8,128)S(1)} %coeffs.1.refs_4_), channel_id=1, source_target_pairs={{0,1},{1,0},{2,3},{3,2},{4,5},{5,4},{6,7},{7,6},{8,9},{9,8},{10,11... | collective-permute-start | bytes 110600 | tf_op jit(solution)/shard_map/ppermute | solution.py:354
  37.8 5.9 %collective-permute-start.14 = (f32[64,128]{1,0:T(8,128)S(1)}, f32[64,128]{1,0:T(8,128)S(1)}, u32[]{:S(2)}, u32[]{:S(2)}) collective-permute-start(f32[64,128]{1,0:T(8,128)S(1)} %get-tuple-element.69), channel_id=1, source_target_pairs={{0,12},{4,8},{8,4},{12,0},{1,13},{5,9},{9,5},{13,1},{2,14},{6,10},... | collective-permute-start | bytes 98312 | tf_op jit(solution)/shard_map/ppermute | solution.py:354
  39.5 5.3 %collective-permute-start.15 = (f32[64,128]{1,0:T(8,128)S(1)}, f32[64,128]{1,0:T(8,128)S(1)}, u32[]{:S(2)}, u32[]{:S(2)}) collective-permute-start(f32[64,128]{1,0:T(8,128)S(1)} %get-tuple-element.70), channel_id=1, source_target_pairs={{0,8},{4,12},{8,0},{12,4},{1,9},{5,13},{9,1},{13,5},{2,10},{6,14},... | collective-permute-start | bytes 98312 | tf_op jit(solution)/shard_map/ppermute | solution.py:354
  40.3 4.6 %collective-permute-start.16 = (f32[64,128]{1,0:T(8,128)S(1)}, f32[64,128]{1,0:T(8,128)S(1)}, u32[]{:S(2)}, u32[]{:S(2)}) collective-permute-start(f32[64,128]{1,0:T(8,128)S(1)} %get-tuple-element.71), channel_id=1, source_target_pairs={{0,4},{4,0},{8,12},{12,8},{1,5},{5,1},{9,13},{13,9},{2,6},{6,2},{1... | collective-permute-start | bytes 98312 | tf_op jit(solution)/shard_map/ppermute | solution.py:354

commit v6 on v5

--- a/solution.py
+++ b/solution.py
@@ -387,13 +387,15 @@
     forces_far = swapped(forces, "cols", top)
     last = couplings[2:3, length - PLANE :]
     before_a, before_b = neighbours(last, 1), neighbours(last, 0)
-    got_a, got_b, forces_far = lax.optimization_barrier((got_a, got_b, forces_far))
     edges = (couplings, ground, before_a, before_b)
     q, w_a, w_b, w_both, near = call(
         second_kernel,
         "second",
         (*edges, precond, d_a, d_b, got_a, got_b),
         [(2,) + field, field, field, (2,) + field, (2, 2 * rows, PLANE)],
+    )
+    w_a, w_b, w_both, near, forces_far = lax.optimization_barrier(
+        (w_a, w_b, w_both, near, forces_far)
     )
     next_a, next_b = neighbours(w_a, 1), neighbours(w_b, 0)
     far = swapped(w_both, "cols", top)

time: 45.7 us -> 44.5 us (0.974)
  waiting for transfers between devices: 14.1 us -> 13 us
    ppermute x14, waiting for transfers between devices: 3.94 us -> 2.77 us  [swapped(): lax.ppermute(block, axis, [(i, i ^ bit) for i in range(lax.axis_size(axis...]
  transfers between devices with their start and end apart: 20 -> 20, of which waited for: 8 -> 8; matrix products, arithmetic and copies ran while one was open for 0% -> 0% of each run, Pallas kernels for 14% -> 17%
where the time goes in v6:
time: 44.5 us; the launch traced here: 44.4 us
  starting transfers between devices  22.3 us (50%)
  waiting for transfers between devices  13 us (29%)
  Pallas kernels  8.28 us (19%)
  between operations  0.78 us (2%)
    ppermute x14, starting transfers between devices, swapped(): lax.ppermute(block, axis, [(i, i ^ bit) for i in range(lax.axis_size(axis...  15.6 us
    ppermute x6, waiting for transfers between devices, neighbours(): return lax.ppermute(block, ('nodes', 'cols'), route)  10.2 us
    pallas_call x10, Pallas kernels, call(): pl.pallas_call(kernel, out_shape=shapes, in_specs=[pl.BlockSpec(memory_sp...  8.28 us
    ppermute x6, starting transfers between devices, neighbours(): return lax.ppermute(block, ('nodes', 'cols'), route)  6.75 us
    ppermute x14, waiting for transfers between devices, swapped(): lax.ppermute(block, axis, [(i, i ^ bit) for i in range(lax.axis_size(axis...  2.77 us
  transfers between devices with their start and end apart: 20, of which 8 were waited for; matrix products, arithmetic and copies ran while one was open for 0% of the time, Pallas kernels for 17%

profile of v6, /device:TPU:0, one launch (start us, length us, event | category | flops | bytes accessed | tf_op | source)
XLA Modules:
  0.0 44.4 jit_solution(10337839916698874511)
XLA Ops:
  0.6 3.0 %collective-permute-start.4 = (f32[64,2048]{1,0:T(8,128)}, f32[64,2048]{1,0:T(8,128)S(1)}, u32[]{:S(2)}, u32[]{:S(2)}) collective-permute-start(f32[64,2048]{1,0:T(8,128)} %forces.3), channel_id=1, source_target_pairs={{0,2},{1,3},{2,0},{3,1},{4,6},{5,7},{6,4},{7,5},{8,10},{9,11},{10,... | collective-permute-start | bytes 1572872 | tf_op jit(solution)/shard_map/ppermute | solution.py:354
  3.7 1.8 %first.1 = (f32[64,1024]{1,0:T(8,128)S(1)}, f32[64,1024]{1,0:T(8,128)S(1)}) custom-call(f32[64,2048]{1,0:T(8,128)} %forces.3, f32[16,128,128]{2,1,0:T(8,128)} %precond.5), custom_call_target="tpu_custom_call" | custom-call | tf_op jit(solution)/shard_map/first/pallas_call | solution.py:328
  5.5 0.1 collective-permute-start.2
  5.6 3.1 %collective-permute-start.3 = (f32[64,1024]{1,0:T(8,128)S(1)}, f32[64,1024]{1,0:T(8,128)S(1)}, u32[]{:S(2)}, u32[]{:S(2)}) collective-permute-start(f32[64,1024]{1,0:T(8,128)S(1)} %get-tuple-element.40.d_b), channel_id=1, source_target_pairs={{0,4},{1,5},{2,6},{3,7},{4,0},{5,1},{6,2},{7,3},{8,12},{9,13},{10,... | collective-permute-start | bytes 786440 | tf_op jit(solution)/shard_map/ppermute | solution.py:350
  8.8 0.1 collective-permute-start.1
  8.8 0.1 collective-permute-start
  8.9 5.7 %collective-permute-done.1.before_b = f32[1,1024]{1,0:T(1,128)S(1)} collective-permute-done((f32[1,1024]{1,0:T(1,128)S(1)}, f32[1,1024]{1,0:T(1,128)S(1)}, u32[]{:S(2)}, u32[]{:S(2)}) %collective-permute-start.1) | collective-permute-done | bytes 4128 | tf_op jit(solution)/shard_map/ppermute | solution.py:350
  14.6 1.0 %second.1 = (f32[2,64,1024]{2,1,0:T(8,128)S(1)}, f32[64,1024]{1,0:T(8,128)S(1)}, f32[64,1024]{1,0:T(8,128)S(1)}, f32[2,64,1024]{2,1,0:T(8,128)S(1)}, f32[2,128,1024]{2,1,0:T(8,128)S(1)}) custom-call(f32[3,2048]{1,0:T(4,128)S(1)} %copy-done.2, f32[1,2048]{1,0:T(1,128)S(1)} %bitcast.1, f32[1,1024]{1,0:T(1,128)S(1)} %collective-permute-done.before_a, ...), custom_call_target="tpu_custom_call" | custom-call | tf_op jit(solution)/shard_map/second/pallas_call | solution.py:328
  15.6 0.2 collective-permute-done.4.forces_far
  15.8 0.5 %collective-permute-start.5 = (f32[64,1024]{1,0:T(8,128)S(1)}, f32[64,1024]{1,0:T(8,128)S(1)}, u32[]{:S(2)}, u32[]{:S(2)}) collective-permute-start(f32[64,1024]{1,0:T(8,128)S(1)} %get-tuple-element.45.w_a), channel_id=1, source_target_pairs={{0,1},{1,0},{2,3},{3,2},{4,8},{5,9},{6,10},{7,11},{8,4},{9,5},{10,... | collective-permute-start | bytes 786440 | tf_op jit(solution)/shard_map/ppermute | solution.py:350
  16.3 2.9 %collective-permute-start.6 = (f32[64,1024]{1,0:T(8,128)S(1)}, f32[64,1024]{1,0:T(8,128)S(1)}, u32[]{:S(2)}, u32[]{:S(2)}) collective-permute-start(f32[64,1024]{1,0:T(8,128)S(1)} %get-tuple-element.46.w_b), channel_id=1, source_target_pairs={{0,4},{1,5},{2,6},{3,7},{4,0},{5,1},{6,2},{7,3},{8,12},{9,13},{10,... | collective-permute-start | bytes 786440 | tf_op jit(solution)/shard_map/ppermute | solution.py:350
  19.2 1.5 %collective-permute-start.9 = (f32[2,64,1024]{2,1,0:T(8,128)S(1)}, f32[2,64,1024]{2,1,0:T(8,128)S(1)}, u32[]{:S(2)}, u32[]{:S(2)}) collective-permute-start(f32[2,64,1024]{2,1,0:T(8,128)S(1)} %get-tuple-element.52), channel_id=1, source_target_pairs={{0,2},{1,3},{2,0},{3,1},{4,6},{5,7},{6,4},{7,5},{8,10},{9,11},{10,... | collective-permute-start | bytes 1572872 | tf_op jit(solution)/shard_map/ppermute | solution.py:354
  20.7 0.6 %other.1 = (f32[2,64,1024]{2,1,0:T(8,128)S(1)}, f32[64,128]{1,0:T(8,128)S(1)}) custom-call(f32[64,2048]{1,0:T(8,128)S(1)} %collective-permute-done.4.forces_far, f32[16,128,128]{2,1,0:T(8,128)S(1)} %copy-done, f32[64,2048]{1,0:T(8,128)S(1)} %copy-done.1, f32[2,64,1024]{2,1,0:T(8,128)S(1)} %get-tuple-element.48.q, ...), custom_call_target="tpu_custom_call" | custom-call | tf_op jit(solution)/shard_map/other/pallas_call | solution.py:328
  21.3 4.6 %collective-permute-done.6.next_b = f32[64,1024]{1,0:T(8,128)S(1)} collective-permute-done((f32[64,1024]{1,0:T(8,128)S(1)}, f32[64,1024]{1,0:T(8,128)S(1)}, u32[]{:S(2)}, u32[]{:S(2)}) %collective-permute-start.6) | collective-permute-done | bytes 262176 | tf_op jit(solution)/shard_map/ppermute | solution.py:350
  25.9 0.8 %third.1 = (f32[2,64,1024]{2,1,0:T(8,128)S(1)}, f32[8,128]{1,0:T(8,128)S(1)}) custom-call(f32[3,2048]{1,0:T(4,128)S(1)} %copy-done.2, f32[1,2048]{1,0:T(1,128)S(1)} %bitcast.2, f32[1,1024]{1,0:T(1,128)S(1)} %collective-permute-done.before_a, f32[1,1024]{1,0:T(1,128)S(1)} %collective-permute-done.1.before_b, f32[64,1024]{1,0:T(8,128)S(1)} %get-tuple-element.45.w_a, ...), custom_call_target="tpu_custom_call" | custom-call | tf_op jit(solution)/shard_map/third/pallas_call | solution.py:328
  26.7 2.5 %collective-permute-start.12 = (f32[8,128]{1,0:T(8,128)S(1)}, f32[8,128]{1,0:T(8,128)S(1)}, u32[]{:S(2)}, u32[]{:S(2)}) collective-permute-start(f32[8,128]{1,0:T(8,128)S(1)} %get-tuple-element.65.refs_0_), channel_id=1, source_target_pairs={{0,12},{4,8},{8,4},{12,0},{1,13},{5,9},{9,5},{13,1},{2,14},{6,10},... | collective-permute-start | bytes 12296 | tf_op jit(solution)/shard_map/ppermute | solution.py:354
  29.2 0.7 %collective-permute-start.11 = (f32[8,128]{1,0:T(8,128)S(1)}, f32[8,128]{1,0:T(8,128)S(1)}, u32[]{:S(2)}, u32[]{:S(2)}) collective-permute-start(f32[8,128]{1,0:T(8,128)S(1)} %get-tuple-element.65.refs_0_), channel_id=1, source_target_pairs={{0,8},{4,12},{8,0},{12,4},{1,9},{5,13},{9,1},{13,5},{2,10},{6,14},... | collective-permute-start | bytes 12296 | tf_op jit(solution)/shard_map/ppermute | solution.py:354
  29.9 1.2 %collective-permute-start.10 = (f32[8,128]{1,0:T(8,128)S(1)}, f32[8,128]{1,0:T(8,128)S(1)}, u32[]{:S(2)}, u32[]{:S(2)}) collective-permute-start(f32[8,128]{1,0:T(8,128)S(1)} %get-tuple-element.65.refs_0_), channel_id=1, source_target_pairs={{0,4},{4,0},{8,12},{12,8},{1,5},{5,1},{9,13},{13,9},{2,6},{6,2},{1... | collective-permute-start | bytes 12296 | tf_op jit(solution)/shard_map/ppermute | solution.py:354
  31.1 1.0 %early.1 = (bf16[2,128,1024]{2,1,0:T(8,128)(2,1)S(1)}, bf16[2,128,1024]{2,1,0:T(8,128)(2,1)S(1)}, f32[2,128,128]{2,1,0:T(8,128)S(1)}) custom-call(f32[2,64,1024]{2,1,0:T(8,128)S(1)} %get-tuple-element.48.q, f32[2,64,1024]{2,1,0:T(8,128)S(1)} %get-tuple-element.57.v, f32[2,128,1024]{2,1,0:T(8,128)S(1)} %get-tuple-element.58.near.refs_0_, ...), custom_call_target="tpu_custom_call" | custom-call | tf_op jit(solution)/shard_map/early/pallas_call | solution.py:328
  32.1 0.9 %collective-permute-done.9.refs_0_ = f32[2,64,1024]{2,1,0:T(8,128)S(1)} collective-permute-done((f32[2,64,1024]{2,1,0:T(8,128)S(1)}, f32[2,64,1024]{2,1,0:T(8,128)S(1)}, u32[]{:S(2)}, u32[]{:S(2)}) %collective-permute-start.9) | collective-permute-done | bytes 524320 | tf_op jit(solution)/shard_map/ppermute | solution.py:354
  33.0 0.6 %far.1.far_gram = f32[128,128]{1,0:T(8,128)S(1)} custom-call(bf16[2,128,1024]{2,1,0:T(8,128)(2,1)S(1)} %get-tuple-element.60.qv_high, bf16[2,128,1024]{2,1,0:T(8,128)(2,1)S(1)} %get-tuple-element.61.qv_low, f32[2,64,1024]{2,1,0:T(8,128)S(1)} %get-tuple-element.62.refs_0_, f32[2,64,1024]{2,1,0:T(8,128)S(1)} %collective-permute-done.8.refs_1_), custom_call_target="tpu_custom_call" | custom-call | tf_op jit(solution)/shard_map/far/pallas_call | solution.py:328
  33.6 0.1 collective-permute-done.11.refs_2_
  33.7 1.7 %collective-permute-start.19 = (f32[72,128]{1,0:T(8,128)S(1)}, f32[72,128]{1,0:T(8,128)S(1)}, u32[]{:S(2)}, u32[]{:S(2)}) collective-permute-start(f32[72,128]{1,0:T(8,128)S(1)} %coeffs.1.refs_4_), channel_id=1, source_target_pairs={{0,3},{1,2},{2,1},{3,0},{4,7},{5,6},{6,5},{7,4},{8,11},{9,10},{10,... | collective-permute-start | bytes 110600 | tf_op jit(solution)/shard_map/ppermute | solution.py:354
  35.4 0.5 %collective-permute-start.18 = (f32[72,128]{1,0:T(8,128)S(1)}, f32[72,128]{1,0:T(8,128)S(1)}, u32[]{:S(2)}, u32[]{:S(2)}) collective-permute-start(f32[72,128]{1,0:T(8,128)S(1)} %coeffs.1.refs_4_), channel_id=1, source_target_pairs={{0,2},{1,3},{2,0},{3,1},{4,6},{5,7},{6,4},{7,5},{8,10},{9,11},{10,... | collective-permute-start | bytes 110600 | tf_op jit(solution)/shard_map/ppermute | solution.py:354
  35.9 0.7 %late.1 = (f32[64,128]{1,0:T(8,128)S(1)}, f32[64,128]{1,0:T(8,128)S(1)}, f32[64,128]{1,0:T(8,128)S(1)}, f32[64,128]{1,0:T(8,128)S(1)}) custom-call(f32[72,128]{1,0:T(8,128)S(1)} %coeffs.1.refs_4_, bf16[2,128,1024]{2,1,0:T(8,128)(2,1)S(1)} %get-tuple-element.60.qv_high, bf16[2,128,1024]{2,1,0:T(8,128)(2,1)S(1)} %get-tuple-element.61.qv_low, ...), custom_call_target="tpu_custom_call" | custom-call | tf_op jit(solution)/shard_map/late/pallas_call | solution.py:328
  36.6 1.7 %collective-permute-start.14 = (f32[64,128]{1,0:T(8,128)S(1)}, f32[64,128]{1,0:T(8,128)S(1)}, u32[]{:S(2)}, u32[]{:S(2)}) collective-permute-start(f32[64,128]{1,0:T(8,128)S(1)} %get-tuple-element.73), channel_id=1, source_target_pairs={{0,12},{4,8},{8,4},{12,0},{1,13},{5,9},{9,5},{13,1},{2,14},{6,10},... | collective-permute-start | bytes 98312 | tf_op jit(solution)/shard_map/ppermute | solution.py:354
  38.3 0.9 %collective-permute-start.15 = (f32[64,128]{1,0:T(8,128)S(1)}, f32[64,128]{1,0:T(8,128)S(1)}, u32[]{:S(2)}, u32[]{:S(2)}) collective-permute-start(f32[64,128]{1,0:T(8,128)S(1)} %get-tuple-element.74), channel_id=1, source_target_pairs={{0,8},{4,12},{8,0},{12,4},{1,9},{5,13},{9,1},{13,5},{2,10},{6,14},... | collective-permute-start | bytes 98312 | tf_op jit(solution)/shard_map/ppermute | solution.py:354
  39.2 1.9 %collective-permute-start.16 = (f32[64,128]{1,0:T(8,128)S(1)}, f32[64,128]{1,0:T(8,128)S(1)}, u32[]{:S(2)}, u32[]{:S(2)}) collective-permute-start(f32[64,128]{1,0:T(8,128)S(1)} %get-tuple-element.75), channel_id=1, source_target_pairs={{0,4},{4,0},{8,12},{12,8},{1,5},{5,1},{9,13},{13,9},{2,6},{6,2},{1... | collective-permute-start | bytes 98312 | tf_op jit(solution)/shard_map/ppermute | solution.py:354
  41.1 1.0 %modes.1 = f32[64,2048]{1,0:T(8,128)} custom-call(f32[72,128]{1,0:T(8,128)S(1)} %coeffs.1.refs_4_, f32[2,128,1024]{2,1,0:T(8,128)S(1)} %get-tuple-element.58.near.refs_0_), custom_call_target="tpu_custom_call" | custom-call | tf_op jit(solution)/shard_map/modes/pallas_call | solution.py:328
  42.1 0.5 %collective-permute-done.14.refs_1_ = f32[64,128]{1,0:T(8,128)S(1)} collective-permute-done((f32[64,128]{1,0:T(8,128)S(1)}, f32[64,128]{1,0:T(8,128)S(1)}, u32[]{:S(2)}, u32[]{:S(2)}) %collective-permute-start.14) | collective-permute-done | bytes 32800 | tf_op jit(solution)/shard_map/ppermute | solution.py:354
  42.6 1.1 %collective-permute-done.15.refs_2_ = f32[64,128]{1,0:T(8,128)S(1)} collective-permute-done((f32[64,128]{1,0:T(8,128)S(1)}, f32[64,128]{1,0:T(8,128)S(1)}, u32[]{:S(2)}, u32[]{:S(2)}) %collective-permute-start.15) | collective-permute-done | bytes 32800 | tf_op jit(solution)/shard_map/ppermute | solution.py:354
  43.7 0.7 %fifth.1 = f32[64,64]{1,0:T(8,128)} custom-call(f32[64,128]{1,0:T(8,128)S(1)} %get-tuple-element.72.refs_0_, f32[64,128]{1,0:T(8,128)S(1)} %collective-permute-done.14.refs_1_, f32[64,128]{1,0:T(8,128)S(1)} %collective-permute-done.15.refs_2_, f32[64,128]{1,0:T(8,128)S(1)} %collective-permute-done.16.refs_3_, f32[72,128]{1,0:T(8,128)S(1)} %coeffs.1.refs_4_, ...), custom_call_target="tpu_custom_call" | custom-call | tf_op jit(solution)/shard_map/fifth/pallas_call | solution.py:328
  (27 shorter events, 0.2 us)
Async XLA Ops:
  0.6 14.0 %copy-start = (f32[16,128,128]{2,1,0:T(8,128)S(1)}, f32[16,128,128]{2,1,0:T(8,128)}, u32[]{:S(2)}) copy-start(f32[16,128,128]{2,1,0:T(8,128)} %precond.5) | copy-start | bytes 3145732
  0.6 8.1 %copy-start.2 = (f32[3,2048]{1,0:T(4,128)S(1)}, f32[3,2048]{1,0:T(4,128)}, u32[]{:S(2)}) copy-start(f32[3,2048]{1,0:T(4,128)} %couplings.3) | copy-start | bytes 73732
  0.6 15.1 %collective-permute-start.4 = (f32[64,2048]{1,0:T(8,128)}, f32[64,2048]{1,0:T(8,128)S(1)}, u32[]{:S(2)}, u32[]{:S(2)}) collective-permute-start(f32[64,2048]{1,0:T(8,128)} %forces.3), channel_id=1, source_target_pairs={{0,2},{1,3},{2,0},{3,1},{4,6},{5,7},{6,4},{7,5},{8,10},{9,11},{10,... | collective-permute-start | bytes 1572872 | tf_op jit(solution)/shard_map/ppermute | solution.py:354
  5.5 9.1 %copy-start.3 = (f32[2048]{0:T(1024)S(1)}, f32[2048]{0:T(1024)}, u32[]{:S(2)}) copy-start(f32[2048]{0:T(1024)} %param.6) | copy-start | bytes 24580
  5.5 9.1 %collective-permute-start.2 = (f32[64,1024]{1,0:T(8,128)S(1)}, f32[64,1024]{1,0:T(8,128)S(1)}, u32[]{:S(2)}, u32[]{:S(2)}) collective-permute-start(f32[64,1024]{1,0:T(8,128)S(1)} %get-tuple-element.39.d_a), channel_id=1, source_target_pairs={{0,1},{1,0},{2,3},{3,2},{4,8},{5,9},{6,10},{7,11},{8,4},{9,5},{10,... | collective-permute-start | bytes 786440 | tf_op jit(solution)/shard_map/ppermute | solution.py:350
  5.6 9.0 %collective-permute-start.3 = (f32[64,1024]{1,0:T(8,128)S(1)}, f32[64,1024]{1,0:T(8,128)S(1)}, u32[]{:S(2)}, u32[]{:S(2)}) collective-permute-start(f32[64,1024]{1,0:T(8,128)S(1)} %get-tuple-element.40.d_b), channel_id=1, source_target_pairs={{0,4},{1,5},{2,6},{3,7},{4,0},{5,1},{6,2},{7,3},{8,12},{9,13},{10,... | collective-permute-start | bytes 786440 | tf_op jit(solution)/shard_map/ppermute | solution.py:350
  8.8 5.8 %collective-permute-start.1 = (f32[1,1024]{1,0:T(1,128)S(1)}, f32[1,1024]{1,0:T(1,128)S(1)}, u32[]{:S(2)}, u32[]{:S(2)}) collective-permute-start(f32[1,1024]{1,0:T(1,128)S(1)} %slice.3), channel_id=1, source_target_pairs={{0,4},{1,5},{2,6},{3,7},{4,0},{5,1},{6,2},{7,3},{8,12},{9,13},{10,... | collective-permute-start | bytes 12296 | tf_op jit(solution)/shard_map/ppermute | solution.py:350
  8.8 5.7 %collective-permute-start = (f32[1,1024]{1,0:T(1,128)S(1)}, f32[1,1024]{1,0:T(1,128)S(1)}, u32[]{:S(2)}, u32[]{:S(2)}) collective-permute-start(f32[1,1024]{1,0:T(1,128)S(1)} %slice.3), channel_id=1, source_target_pairs={{0,1},{1,0},{2,3},{3,2},{4,8},{5,9},{6,10},{7,11},{8,4},{9,5},{10,... | collective-permute-start | bytes 12296 | tf_op jit(solution)/shard_map/ppermute | solution.py:350
  14.6 6.1 %copy-start.1 = (f32[64,2048]{1,0:T(8,128)S(1)}, f32[64,2048]{1,0:T(8,128)}, u32[]{:S(2)}) copy-start(f32[64,2048]{1,0:T(8,128)} %forces.3) | copy-start | bytes 1572868
  15.8 10.1 %collective-permute-start.7 = (f32[2,128,1024]{2,1,0:T(8,128)S(1)}, f32[2,128,1024]{2,1,0:T(8,128)S(1)}, u32[]{:S(2)}, u32[]{:S(2)}) collective-permute-start(f32[2,128,1024]{2,1,0:T(8,128)S(1)} %get-tuple-element.58.near.refs_0_), channel_id=1, source_target_pairs={{0,1},{1,0},{2,3},{3,2},{4,5},{5,4},{6,7},{7,6},{8,9},{9,8},{10,11... | collective-permute-start | bytes 3145736 | tf_op jit(solution)/shard_map/ppermute | solution.py:354
  15.8 5.5 %collective-permute-start.5 = (f32[64,1024]{1,0:T(8,128)S(1)}, f32[64,1024]{1,0:T(8,128)S(1)}, u32[]{:S(2)}, u32[]{:S(2)}) collective-permute-start(f32[64,1024]{1,0:T(8,128)S(1)} %get-tuple-element.45.w_a), channel_id=1, source_target_pairs={{0,1},{1,0},{2,3},{3,2},{4,8},{5,9},{6,10},{7,11},{8,4},{9,5},{10,... | collective-permute-start | bytes 786440 | tf_op jit(solution)/shard_map/ppermute | solution.py:350
  16.3 9.6 %collective-permute-start.6 = (f32[64,1024]{1,0:T(8,128)S(1)}, f32[64,1024]{1,0:T(8,128)S(1)}, u32[]{:S(2)}, u32[]{:S(2)}) collective-permute-start(f32[64,1024]{1,0:T(8,128)S(1)} %get-tuple-element.46.w_b), channel_id=1, source_target_pairs={{0,4},{1,5},{2,6},{3,7},{4,0},{5,1},{6,2},{7,3},{8,12},{9,13},{10,... | collective-permute-start | bytes 786440 | tf_op jit(solution)/shard_map/ppermute | solution.py:350
  19.2 13.8 %collective-permute-start.9 = (f32[2,64,1024]{2,1,0:T(8,128)S(1)}, f32[2,64,1024]{2,1,0:T(8,128)S(1)}, u32[]{:S(2)}, u32[]{:S(2)}) collective-permute-start(f32[2,64,1024]{2,1,0:T(8,128)S(1)} %get-tuple-element.52), channel_id=1, source_target_pairs={{0,2},{1,3},{2,0},{3,1},{4,6},{5,7},{6,4},{7,5},{8,10},{9,11},{10,... | collective-permute-start | bytes 1572872 | tf_op jit(solution)/shard_map/ppermute | solution.py:354
  25.9 7.1 %collective-permute-start.8 = (f32[2,64,1024]{2,1,0:T(8,128)S(1)}, f32[2,64,1024]{2,1,0:T(8,128)S(1)}, u32[]{:S(2)}, u32[]{:S(2)}) collective-permute-start(f32[2,64,1024]{2,1,0:T(8,128)S(1)} %get-tuple-element.62.refs_0_), channel_id=1, source_target_pairs={{0,1},{1,0},{2,3},{3,2},{4,5},{5,4},{6,7},{7,6},{8,9},{9,8},{10,11... | collective-permute-start | bytes 1572872 | tf_op jit(solution)/shard_map/ppermute | solution.py:354
  26.7 6.9 %collective-permute-start.12 = (f32[8,128]{1,0:T(8,128)S(1)}, f32[8,128]{1,0:T(8,128)S(1)}, u32[]{:S(2)}, u32[]{:S(2)}) collective-permute-start(f32[8,128]{1,0:T(8,128)S(1)} %get-tuple-element.65.refs_0_), channel_id=1, source_target_pairs={{0,12},{4,8},{8,4},{12,0},{1,13},{5,9},{9,5},{13,1},{2,14},{6,10},... | collective-permute-start | bytes 12296 | tf_op jit(solution)/shard_map/ppermute | solution.py:354
  29.2 4.5 %collective-permute-start.11 = (f32[8,128]{1,0:T(8,128)S(1)}, f32[8,128]{1,0:T(8,128)S(1)}, u32[]{:S(2)}, u32[]{:S(2)}) collective-permute-start(f32[8,128]{1,0:T(8,128)S(1)} %get-tuple-element.65.refs_0_), channel_id=1, source_target_pairs={{0,8},{4,12},{8,0},{12,4},{1,9},{5,13},{9,1},{13,5},{2,10},{6,14},... | collective-permute-start | bytes 12296 | tf_op jit(solution)/shard_map/ppermute | solution.py:354
  29.9 3.8 %collective-permute-start.10 = (f32[8,128]{1,0:T(8,128)S(1)}, f32[8,128]{1,0:T(8,128)S(1)}, u32[]{:S(2)}, u32[]{:S(2)}) collective-permute-start(f32[8,128]{1,0:T(8,128)S(1)} %get-tuple-element.65.refs_0_), channel_id=1, source_target_pairs={{0,4},{4,0},{8,12},{12,8},{1,5},{5,1},{9,13},{13,9},{2,6},{6,2},{1... | collective-permute-start | bytes 12296 | tf_op jit(solution)/shard_map/ppermute | solution.py:354
  33.7 2.2 %collective-permute-start.13 = (f32[2,64,1024]{2,1,0:T(8,128)S(1)}, f32[2,64,1024]{2,1,0:T(8,128)S(1)}, u32[]{:S(2)}, u32[]{:S(2)}) collective-permute-start(f32[2,64,1024]{2,1,0:T(8,128)S(1)} %collective-permute-done.9.refs_0_), channel_id=1, source_target_pairs={{0,1},{1,0},{2,3},{3,2},{4,5},{5,4},{6,7},{7,6},{8,9},{9,8},{10,11... | collective-permute-start | bytes 1572872 | tf_op jit(solution)/shard_map/ppermute | solution.py:354
  33.7 5.4 %collective-permute-start.19 = (f32[72,128]{1,0:T(8,128)S(1)}, f32[72,128]{1,0:T(8,128)S(1)}, u32[]{:S(2)}, u32[]{:S(2)}) collective-permute-start(f32[72,128]{1,0:T(8,128)S(1)} %coeffs.1.refs_4_), channel_id=1, source_target_pairs={{0,3},{1,2},{2,1},{3,0},{4,7},{5,6},{6,5},{7,4},{8,11},{9,10},{10,... | collective-permute-start | bytes 110600 | tf_op jit(solution)/shard_map/ppermute | solution.py:354
  35.4 6.7 %collective-permute-start.18 = (f32[72,128]{1,0:T(8,128)S(1)}, f32[72,128]{1,0:T(8,128)S(1)}, u32[]{:S(2)}, u32[]{:S(2)}) collective-permute-start(f32[72,128]{1,0:T(8,128)S(1)} %coeffs.1.refs_4_), channel_id=1, source_target_pairs={{0,2},{1,3},{2,0},{3,1},{4,6},{5,7},{6,4},{7,5},{8,10},{9,11},{10,... | collective-permute-start | bytes 110600 | tf_op jit(solution)/shard_map/ppermute | solution.py:354
  35.9 6.2 %collective-permute-start.17 = (f32[72,128]{1,0:T(8,128)S(1)}, f32[72,128]{1,0:T(8,128)S(1)}, u32[]{:S(2)}, u32[]{:S(2)}) collective-permute-start(f32[72,128]{1,0:T(8,128)S(1)} %coeffs.1.refs_4_), channel_id=1, source_target_pairs={{0,1},{1,0},{2,3},{3,2},{4,5},{5,4},{6,7},{7,6},{8,9},{9,8},{10,11... | collective-permute-start | bytes 110600 | tf_op jit(solution)/shard_map/ppermute | solution.py:354
  36.6 5.9 %collective-permute-start.14 = (f32[64,128]{1,0:T(8,128)S(1)}, f32[64,128]{1,0:T(8,128)S(1)}, u32[]{:S(2)}, u32[]{:S(2)}) collective-permute-start(f32[64,128]{1,0:T(8,128)S(1)} %get-tuple-element.73), channel_id=1, source_target_pairs={{0,12},{4,8},{8,4},{12,0},{1,13},{5,9},{9,5},{13,1},{2,14},{6,10},... | collective-permute-start | bytes 98312 | tf_op jit(solution)/shard_map/ppermute | solution.py:354
  38.3 5.4 %collective-permute-start.15 = (f32[64,128]{1,0:T(8,128)S(1)}, f32[64,128]{1,0:T(8,128)S(1)}, u32[]{:S(2)}, u32[]{:S(2)}) collective-permute-start(f32[64,128]{1,0:T(8,128)S(1)} %get-tuple-element.74), channel_id=1, source_target_pairs={{0,8},{4,12},{8,0},{12,4},{1,9},{5,13},{9,1},{13,5},{2,10},{6,14},... | collective-permute-start | bytes 98312 | tf_op jit(solution)/shard_map/ppermute | solution.py:354
  39.2 4.5 %collective-permute-start.16 = (f32[64,128]{1,0:T(8,128)S(1)}, f32[64,128]{1,0:T(8,128)S(1)}, u32[]{:S(2)}, u32[]{:S(2)}) collective-permute-start(f32[64,128]{1,0:T(8,128)S(1)} %get-tuple-element.75), channel_id=1, source_target_pairs={{0,4},{4,0},{8,12},{12,8},{1,5},{5,1},{9,13},{13,9},{2,6},{6,2},{1... | collective-permute-start | bytes 98312 | tf_op jit(solution)/shard_map/ppermute | solution.py:354

commit v7 on v6

--- a/solution.py
+++ b/solution.py
@@ -443,7 +443,11 @@
     scale = 1.0 / (length * nodes)
     (modes,) = call(modes_kernel, "modes", (coeffs, near[0]), [(rows, length)])
     if exchange:
-        theirs = [coeffs] + [swapped(coeffs, "cols", i) for i in range(1, cols)]
+        held = {0: coeffs}
+        for bit in reversed(bits):
+            for key in list(held):
+                held[key ^ bit] = swapped(held[key] if key == 0 else held[key][0:8], "cols", bit)
+        theirs = [held[key] for key in range(cols)]
         sums = [grams[0]] + [swapped(grams[i], "nodes", i) for i in reversed(range(1, nodes))]
         (tile,) = call(
             functools.partial(fifth_kernel, scale, nodes),

time: 44.5 us -> 43.9 us (0.987)
  transfers between devices with their start and end apart: 20 -> 20, of which waited for: 8 -> 10; matrix products, arithmetic and copies ran while one was open for 0% -> 0% of each run, Pallas kernels for 17% -> 17%
where the time goes in v7:
time: 43.9 us; the launch traced here: 43.8 us
  starting transfers between devices  21.9 us (50%)
  waiting for transfers between devices  12.8 us (29%)
  Pallas kernels  8.28 us (19%)
  between operations  0.78 us (2%)
    ppermute x14, starting transfers between devices, swapped(): lax.ppermute(block, axis, [(i, i ^ bit) for i in range(lax.axis_size(axis...  15.1 us
    ppermute x6, waiting for transfers between devices, neighbours(): return lax.ppermute(block, ('nodes', 'cols'), route)  10.2 us
    pallas_call x10, Pallas kernels, call(): pl.pallas_call(kernel, out_shape=shapes, in_specs=[pl.BlockSpec(memory_sp...  8.28 us
    ppermute x6, starting transfers between devices, neighbours(): return lax.ppermute(block, ('nodes', 'cols'), route)  6.75 us
    ppermute x14, waiting for transfers between devices, swapped(): lax.ppermute(block, axis, [(i, i ^ bit) for i in range(lax.axis_size(axis...  2.58 us
  transfers between devices with their start and end apart: 20, of which 10 were waited for; matrix products, arithmetic and copies ran while one was open for 0% of the time, Pallas kernels for 17%

profile of v7, /device:TPU:0, one launch (start us, length us, event | category | flops | bytes accessed | tf_op | source)
XLA Modules:
  0.0 43.8 jit_solution(17871893873951188859)
XLA Ops:
  0.6 3.0 %collective-permute-start.4 = (f32[64,2048]{1,0:T(8,128)}, f32[64,2048]{1,0:T(8,128)S(1)}, u32[]{:S(2)}, u32[]{:S(2)}) collective-permute-start(f32[64,2048]{1,0:T(8,128)} %forces.3), channel_id=1, source_target_pairs={{0,2},{1,3},{2,0},{3,1},{4,6},{5,7},{6,4},{7,5},{8,10},{9,11},{10,... | collective-permute-start | bytes 1572872 | tf_op jit(solution)/shard_map/ppermute | solution.py:354
  3.7 1.8 %first.1 = (f32[64,1024]{1,0:T(8,128)S(1)}, f32[64,1024]{1,0:T(8,128)S(1)}) custom-call(f32[64,2048]{1,0:T(8,128)} %forces.3, f32[16,128,128]{2,1,0:T(8,128)} %precond.5), custom_call_target="tpu_custom_call" | custom-call | tf_op jit(solution)/shard_map/first/pallas_call | solution.py:328
  5.6 3.1 %collective-permute-start.3 = (f32[64,1024]{1,0:T(8,128)S(1)}, f32[64,1024]{1,0:T(8,128)S(1)}, u32[]{:S(2)}, u32[]{:S(2)}) collective-permute-start(f32[64,1024]{1,0:T(8,128)S(1)} %get-tuple-element.40.d_b), channel_id=1, source_target_pairs={{0,4},{1,5},{2,6},{3,7},{4,0},{5,1},{6,2},{7,3},{8,12},{9,13},{10,... | collective-permute-start | bytes 786440 | tf_op jit(solution)/shard_map/ppermute | solution.py:350
  8.9 5.7 %collective-permute-done.1.before_b = f32[1,1024]{1,0:T(1,128)S(1)} collective-permute-done((f32[1,1024]{1,0:T(1,128)S(1)}, f32[1,1024]{1,0:T(1,128)S(1)}, u32[]{:S(2)}, u32[]{:S(2)}) %collective-permute-start.1) | collective-permute-done | bytes 4128 | tf_op jit(solution)/shard_map/ppermute | solution.py:350
  14.6 1.0 %second.1 = (f32[2,64,1024]{2,1,0:T(8,128)S(1)}, f32[64,1024]{1,0:T(8,128)S(1)}, f32[64,1024]{1,0:T(8,128)S(1)}, f32[2,64,1024]{2,1,0:T(8,128)S(1)}, f32[2,128,1024]{2,1,0:T(8,128)S(1)}) custom-call(f32[3,2048]{1,0:T(4,128)S(1)} %copy-done.2, f32[1,2048]{1,0:T(1,128)S(1)} %bitcast.1, f32[1,1024]{1,0:T(1,128)S(1)} %collective-permute-done.before_a, ...), custom_call_target="tpu_custom_call" | custom-call | tf_op jit(solution)/shard_map/second/pallas_call | solution.py:328
  15.6 0.2 collective-permute-done.4.forces_far
  15.8 0.5 %collective-permute-start.5 = (f32[64,1024]{1,0:T(8,128)S(1)}, f32[64,1024]{1,0:T(8,128)S(1)}, u32[]{:S(2)}, u32[]{:S(2)}) collective-permute-start(f32[64,1024]{1,0:T(8,128)S(1)} %get-tuple-element.45.w_a), channel_id=1, source_target_pairs={{0,1},{1,0},{2,3},{3,2},{4,8},{5,9},{6,10},{7,11},{8,4},{9,5},{10,... | collective-permute-start | bytes 786440 | tf_op jit(solution)/shard_map/ppermute | solution.py:350
  16.3 2.9 %collective-permute-start.6 = (f32[64,1024]{1,0:T(8,128)S(1)}, f32[64,1024]{1,0:T(8,128)S(1)}, u32[]{:S(2)}, u32[]{:S(2)}) collective-permute-start(f32[64,1024]{1,0:T(8,128)S(1)} %get-tuple-element.46.w_b), channel_id=1, source_target_pairs={{0,4},{1,5},{2,6},{3,7},{4,0},{5,1},{6,2},{7,3},{8,12},{9,13},{10,... | collective-permute-start | bytes 786440 | tf_op jit(solution)/shard_map/ppermute | solution.py:350
  19.2 1.5 %collective-permute-start.9 = (f32[2,64,1024]{2,1,0:T(8,128)S(1)}, f32[2,64,1024]{2,1,0:T(8,128)S(1)}, u32[]{:S(2)}, u32[]{:S(2)}) collective-permute-start(f32[2,64,1024]{2,1,0:T(8,128)S(1)} %get-tuple-element.52), channel_id=1, source_target_pairs={{0,2},{1,3},{2,0},{3,1},{4,6},{5,7},{6,4},{7,5},{8,10},{9,11},{10,... | collective-permute-start | bytes 1572872 | tf_op jit(solution)/shard_map/ppermute | solution.py:354
  20.7 0.6 %other.1 = (f32[2,64,1024]{2,1,0:T(8,128)S(1)}, f32[64,128]{1,0:T(8,128)S(1)}) custom-call(f32[64,2048]{1,0:T(8,128)S(1)} %collective-permute-done.4.forces_far, f32[16,128,128]{2,1,0:T(8,128)S(1)} %copy-done, f32[64,2048]{1,0:T(8,128)S(1)} %copy-done.1, f32[2,64,1024]{2,1,0:T(8,128)S(1)} %get-tuple-element.48.q, ...), custom_call_target="tpu_custom_call" | custom-call | tf_op jit(solution)/shard_map/other/pallas_call | solution.py:328
  21.3 4.6 %collective-permute-done.6.next_b = f32[64,1024]{1,0:T(8,128)S(1)} collective-permute-done((f32[64,1024]{1,0:T(8,128)S(1)}, f32[64,1024]{1,0:T(8,128)S(1)}, u32[]{:S(2)}, u32[]{:S(2)}) %collective-permute-start.6) | collective-permute-done | bytes 262176 | tf_op jit(solution)/shard_map/ppermute | solution.py:350
  25.9 0.8 %third.1 = (f32[2,64,1024]{2,1,0:T(8,128)S(1)}, f32[8,128]{1,0:T(8,128)S(1)}) custom-call(f32[3,2048]{1,0:T(4,128)S(1)} %copy-done.2, f32[1,2048]{1,0:T(1,128)S(1)} %bitcast.2, f32[1,1024]{1,0:T(1,128)S(1)} %collective-permute-done.before_a, f32[1,1024]{1,0:T(1,128)S(1)} %collective-permute-done.1.before_b, f32[64,1024]{1,0:T(8,128)S(1)} %get-tuple-element.45.w_a, ...), custom_call_target="tpu_custom_call" | custom-call | tf_op jit(solution)/shard_map/third/pallas_call | solution.py:328
  26.7 2.5 %collective-permute-start.12 = (f32[8,128]{1,0:T(8,128)S(1)}, f32[8,128]{1,0:T(8,128)S(1)}, u32[]{:S(2)}, u32[]{:S(2)}) collective-permute-start(f32[8,128]{1,0:T(8,128)S(1)} %get-tuple-element.65.refs_0_), channel_id=1, source_target_pairs={{0,12},{4,8},{8,4},{12,0},{1,13},{5,9},{9,5},{13,1},{2,14},{6,10},... | collective-permute-start | bytes 12296 | tf_op jit(solution)/shard_map/ppermute | solution.py:354
  29.2 0.7 %collective-permute-start.11 = (f32[8,128]{1,0:T(8,128)S(1)}, f32[8,128]{1,0:T(8,128)S(1)}, u32[]{:S(2)}, u32[]{:S(2)}) collective-permute-start(f32[8,128]{1,0:T(8,128)S(1)} %get-tuple-element.65.refs_0_), channel_id=1, source_target_pairs={{0,8},{4,12},{8,0},{12,4},{1,9},{5,13},{9,1},{13,5},{2,10},{6,14},... | collective-permute-start | bytes 12296 | tf_op jit(solution)/shard_map/ppermute | solution.py:354
  29.9 1.2 %collective-permute-start.10 = (f32[8,128]{1,0:T(8,128)S(1)}, f32[8,128]{1,0:T(8,128)S(1)}, u32[]{:S(2)}, u32[]{:S(2)}) collective-permute-start(f32[8,128]{1,0:T(8,128)S(1)} %get-tuple-element.65.refs_0_), channel_id=1, source_target_pairs={{0,4},{4,0},{8,12},{12,8},{1,5},{5,1},{9,13},{13,9},{2,6},{6,2},{1... | collective-permute-start | bytes 12296 | tf_op jit(solution)/shard_map/ppermute | solution.py:354
  31.1 1.0 %early.1 = (bf16[2,128,1024]{2,1,0:T(8,128)(2,1)S(1)}, bf16[2,128,1024]{2,1,0:T(8,128)(2,1)S(1)}, f32[2,128,128]{2,1,0:T(8,128)S(1)}) custom-call(f32[2,64,1024]{2,1,0:T(8,128)S(1)} %get-tuple-element.48.q, f32[2,64,1024]{2,1,0:T(8,128)S(1)} %get-tuple-element.57.v, f32[2,128,1024]{2,1,0:T(8,128)S(1)} %get-tuple-element.58.near.refs_0_, ...), custom_call_target="tpu_custom_call" | custom-call | tf_op jit(solution)/shard_map/early/pallas_call | solution.py:328
  32.1 0.9 %collective-permute-done.9.refs_0_ = f32[2,64,1024]{2,1,0:T(8,128)S(1)} collective-permute-done((f32[2,64,1024]{2,1,0:T(8,128)S(1)}, f32[2,64,1024]{2,1,0:T(8,128)S(1)}, u32[]{:S(2)}, u32[]{:S(2)}) %collective-permute-start.9) | collective-permute-done | bytes 524320 | tf_op jit(solution)/shard_map/ppermute | solution.py:354
  33.0 0.6 %far.1.far_gram = f32[128,128]{1,0:T(8,128)S(1)} custom-call(bf16[2,128,1024]{2,1,0:T(8,128)(2,1)S(1)} %get-tuple-element.60.qv_high, bf16[2,128,1024]{2,1,0:T(8,128)(2,1)S(1)} %get-tuple-element.61.qv_low, f32[2,64,1024]{2,1,0:T(8,128)S(1)} %get-tuple-element.62.refs_0_, f32[2,64,1024]{2,1,0:T(8,128)S(1)} %collective-permute-done.8.refs_1_), custom_call_target="tpu_custom_call" | custom-call | tf_op jit(solution)/shard_map/far/pallas_call | solution.py:328
  33.6 0.1 collective-permute-done.11.refs_2_
  33.7 1.6 %collective-permute-start.18 = (f32[72,128]{1,0:T(8,128)S(1)}, f32[72,128]{1,0:T(8,128)S(1)}, u32[]{:S(2)}, u32[]{:S(2)}) collective-permute-start(f32[72,128]{1,0:T(8,128)S(1)} %coeffs.1.refs_4_), channel_id=1, source_target_pairs={{0,2},{1,3},{2,0},{3,1},{4,6},{5,7},{6,4},{7,5},{8,10},{9,11},{10,... | collective-permute-start | bytes 110600 | tf_op jit(solution)/shard_map/ppermute | solution.py:354
  35.3 0.2 collective-permute-start.17
  35.5 0.1 collective-permute-done.13.refs_1_
  35.6 0.7 %late.1 = (f32[64,128]{1,0:T(8,128)S(1)}, f32[64,128]{1,0:T(8,128)S(1)}, f32[64,128]{1,0:T(8,128)S(1)}, f32[64,128]{1,0:T(8,128)S(1)}) custom-call(f32[72,128]{1,0:T(8,128)S(1)} %coeffs.1.refs_4_, bf16[2,128,1024]{2,1,0:T(8,128)(2,1)S(1)} %get-tuple-element.60.qv_high, bf16[2,128,1024]{2,1,0:T(8,128)(2,1)S(1)} %get-tuple-element.61.qv_low, ...), custom_call_target="tpu_custom_call" | custom-call | tf_op jit(solution)/shard_map/late/pallas_call | solution.py:328
  36.3 1.6 %collective-permute-start.14 = (f32[64,128]{1,0:T(8,128)S(1)}, f32[64,128]{1,0:T(8,128)S(1)}, u32[]{:S(2)}, u32[]{:S(2)}) collective-permute-start(f32[64,128]{1,0:T(8,128)S(1)} %get-tuple-element.73), channel_id=1, source_target_pairs={{0,12},{4,8},{8,4},{12,0},{1,13},{5,9},{9,5},{13,1},{2,14},{6,10},... | collective-permute-start | bytes 98312 | tf_op jit(solution)/shard_map/ppermute | solution.py:354
  37.9 0.9 %collective-permute-start.15 = (f32[64,128]{1,0:T(8,128)S(1)}, f32[64,128]{1,0:T(8,128)S(1)}, u32[]{:S(2)}, u32[]{:S(2)}) collective-permute-start(f32[64,128]{1,0:T(8,128)S(1)} %get-tuple-element.74), channel_id=1, source_target_pairs={{0,8},{4,12},{8,0},{12,4},{1,9},{5,13},{9,1},{13,5},{2,10},{6,14},... | collective-permute-start | bytes 98312 | tf_op jit(solution)/shard_map/ppermute | solution.py:354
  38.8 1.9 %collective-permute-start.16 = (f32[64,128]{1,0:T(8,128)S(1)}, f32[64,128]{1,0:T(8,128)S(1)}, u32[]{:S(2)}, u32[]{:S(2)}) collective-permute-start(f32[64,128]{1,0:T(8,128)S(1)} %get-tuple-element.75), channel_id=1, source_target_pairs={{0,4},{4,0},{8,12},{12,8},{1,5},{5,1},{9,13},{13,9},{2,6},{6,2},{1... | collective-permute-start | bytes 98312 | tf_op jit(solution)/shard_map/ppermute | solution.py:354
  40.7 1.0 %modes.1 = f32[64,2048]{1,0:T(8,128)} custom-call(f32[72,128]{1,0:T(8,128)S(1)} %coeffs.1.refs_4_, f32[2,128,1024]{2,1,0:T(8,128)S(1)} %get-tuple-element.58.near.refs_0_), custom_call_target="tpu_custom_call" | custom-call | tf_op jit(solution)/shard_map/modes/pallas_call | solution.py:328
  41.8 0.1 collective-permute-done.19.refs_7_
  41.9 0.4 collective-permute-done.14.refs_1_
  42.3 0.5 %collective-permute-done.15.refs_2_ = f32[64,128]{1,0:T(8,128)S(1)} collective-permute-done((f32[64,128]{1,0:T(8,128)S(1)}, f32[64,128]{1,0:T(8,128)S(1)}, u32[]{:S(2)}, u32[]{:S(2)}) %collective-permute-start.15) | collective-permute-done | bytes 32800 | tf_op jit(solution)/shard_map/ppermute | solution.py:354
  42.8 0.3 collective-permute-done.16.refs_3_
  43.1 0.7 %fifth.1 = f32[64,64]{1,0:T(8,128)} custom-call(f32[64,128]{1,0:T(8,128)S(1)} %get-tuple-element.72.refs_0_, f32[64,128]{1,0:T(8,128)S(1)} %collective-permute-done.14.refs_1_, f32[64,128]{1,0:T(8,128)S(1)} %collective-permute-done.15.refs_2_, f32[64,128]{1,0:T(8,128)S(1)} %collective-permute-done.16.refs_3_, f32[72,128]{1,0:T(8,128)S(1)} %coeffs.1.refs_4_, ...), custom_call_target="tpu_custom_call" | custom-call | tf_op jit(solution)/shard_map/fifth/pallas_call | solution.py:328
  (28 shorter events, 0.3 us)
Async XLA Ops:
  0.6 14.0 %copy-start = (f32[16,128,128]{2,1,0:T(8,128)S(1)}, f32[16,128,128]{2,1,0:T(8,128)}, u32[]{:S(2)}) copy-start(f32[16,128,128]{2,1,0:T(8,128)} %precond.5) | copy-start | bytes 3145732
  0.6 8.1 %copy-start.2 = (f32[3,2048]{1,0:T(4,128)S(1)}, f32[3,2048]{1,0:T(4,128)}, u32[]{:S(2)}) copy-start(f32[3,2048]{1,0:T(4,128)} %couplings.3) | copy-start | bytes 73732
  0.6 15.1 %collective-permute-start.4 = (f32[64,2048]{1,0:T(8,128)}, f32[64,2048]{1,0:T(8,128)S(1)}, u32[]{:S(2)}, u32[]{:S(2)}) collective-permute-start(f32[64,2048]{1,0:T(8,128)} %forces.3), channel_id=1, source_target_pairs={{0,2},{1,3},{2,0},{3,1},{4,6},{5,7},{6,4},{7,5},{8,10},{9,11},{10,... | collective-permute-start | bytes 1572872 | tf_op jit(solution)/shard_map/ppermute | solution.py:354
  5.5 9.1 %copy-start.3 = (f32[2048]{0:T(1024)S(1)}, f32[2048]{0:T(1024)}, u32[]{:S(2)}) copy-start(f32[2048]{0:T(1024)} %param.6) | copy-start | bytes 24580
  5.5 9.1 %collective-permute-start.2 = (f32[64,1024]{1,0:T(8,128)S(1)}, f32[64,1024]{1,0:T(8,128)S(1)}, u32[]{:S(2)}, u32[]{:S(2)}) collective-permute-start(f32[64,1024]{1,0:T(8,128)S(1)} %get-tuple-element.39.d_a), channel_id=1, source_target_pairs={{0,1},{1,0},{2,3},{3,2},{4,8},{5,9},{6,10},{7,11},{8,4},{9,5},{10,... | collective-permute-start | bytes 786440 | tf_op jit(solution)/shard_map/ppermute | solution.py:350
  5.6 9.0 %collective-permute-start.3 = (f32[64,1024]{1,0:T(8,128)S(1)}, f32[64,1024]{1,0:T(8,128)S(1)}, u32[]{:S(2)}, u32[]{:S(2)}) collective-permute-start(f32[64,1024]{1,0:T(8,128)S(1)} %get-tuple-element.40.d_b), channel_id=1, source_target_pairs={{0,4},{1,5},{2,6},{3,7},{4,0},{5,1},{6,2},{7,3},{8,12},{9,13},{10,... | collective-permute-start | bytes 786440 | tf_op jit(solution)/shard_map/ppermute | solution.py:350
  8.8 5.8 %collective-permute-start.1 = (f32[1,1024]{1,0:T(1,128)S(1)}, f32[1,1024]{1,0:T(1,128)S(1)}, u32[]{:S(2)}, u32[]{:S(2)}) collective-permute-start(f32[1,1024]{1,0:T(1,128)S(1)} %slice.6), channel_id=1, source_target_pairs={{0,4},{1,5},{2,6},{3,7},{4,0},{5,1},{6,2},{7,3},{8,12},{9,13},{10,... | collective-permute-start | bytes 12296 | tf_op jit(solution)/shard_map/ppermute | solution.py:350
  8.8 5.7 %collective-permute-start = (f32[1,1024]{1,0:T(1,128)S(1)}, f32[1,1024]{1,0:T(1,128)S(1)}, u32[]{:S(2)}, u32[]{:S(2)}) collective-permute-start(f32[1,1024]{1,0:T(1,128)S(1)} %slice.6), channel_id=1, source_target_pairs={{0,1},{1,0},{2,3},{3,2},{4,8},{5,9},{6,10},{7,11},{8,4},{9,5},{10,... | collective-permute-start | bytes 12296 | tf_op jit(solution)/shard_map/ppermute | solution.py:350
  14.6 6.1 %copy-start.1 = (f32[64,2048]{1,0:T(8,128)S(1)}, f32[64,2048]{1,0:T(8,128)}, u32[]{:S(2)}) copy-start(f32[64,2048]{1,0:T(8,128)} %forces.3) | copy-start | bytes 1572868
  15.8 10.1 %collective-permute-start.7 = (f32[2,128,1024]{2,1,0:T(8,128)S(1)}, f32[2,128,1024]{2,1,0:T(8,128)S(1)}, u32[]{:S(2)}, u32[]{:S(2)}) collective-permute-start(f32[2,128,1024]{2,1,0:T(8,128)S(1)} %get-tuple-element.58.near.refs_0_), channel_id=1, source_target_pairs={{0,1},{1,0},{2,3},{3,2},{4,5},{5,4},{6,7},{7,6},{8,9},{9,8},{10,11... | collective-permute-start | bytes 3145736 | tf_op jit(solution)/shard_map/ppermute | solution.py:354
  15.8 5.5 %collective-permute-start.5 = (f32[64,1024]{1,0:T(8,128)S(1)}, f32[64,1024]{1,0:T(8,128)S(1)}, u32[]{:S(2)}, u32[]{:S(2)}) collective-permute-start(f32[64,1024]{1,0:T(8,128)S(1)} %get-tuple-element.45.w_a), channel_id=1, source_target_pairs={{0,1},{1,0},{2,3},{3,2},{4,8},{5,9},{6,10},{7,11},{8,4},{9,5},{10,... | collective-permute-start | bytes 786440 | tf_op jit(solution)/shard_map/ppermute | solution.py:350
  16.3 9.6 %collective-permute-start.6 = (f32[64,1024]{1,0:T(8,128)S(1)}, f32[64,1024]{1,0:T(8,128)S(1)}, u32[]{:S(2)}, u32[]{:S(2)}) collective-permute-start(f32[64,1024]{1,0:T(8,128)S(1)} %get-tuple-element.46.w_b), channel_id=1, source_target_pairs={{0,4},{1,5},{2,6},{3,7},{4,0},{5,1},{6,2},{7,3},{8,12},{9,13},{10,... | collective-permute-start | bytes 786440 | tf_op jit(solution)/shard_map/ppermute | solution.py:350
  19.2 13.8 %collective-permute-start.9 = (f32[2,64,1024]{2,1,0:T(8,128)S(1)}, f32[2,64,1024]{2,1,0:T(8,128)S(1)}, u32[]{:S(2)}, u32[]{:S(2)}) collective-permute-start(f32[2,64,1024]{2,1,0:T(8,128)S(1)} %get-tuple-element.52), channel_id=1, source_target_pairs={{0,2},{1,3},{2,0},{3,1},{4,6},{5,7},{6,4},{7,5},{8,10},{9,11},{10,... | collective-permute-start | bytes 1572872 | tf_op jit(solution)/shard_map/ppermute | solution.py:354
  25.9 7.1 %collective-permute-start.8 = (f32[2,64,1024]{2,1,0:T(8,128)S(1)}, f32[2,64,1024]{2,1,0:T(8,128)S(1)}, u32[]{:S(2)}, u32[]{:S(2)}) collective-permute-start(f32[2,64,1024]{2,1,0:T(8,128)S(1)} %get-tuple-element.62.refs_0_), channel_id=1, source_target_pairs={{0,1},{1,0},{2,3},{3,2},{4,5},{5,4},{6,7},{7,6},{8,9},{9,8},{10,11... | collective-permute-start | bytes 1572872 | tf_op jit(solution)/shard_map/ppermute | solution.py:354
  26.7 6.9 %collective-permute-start.12 = (f32[8,128]{1,0:T(8,128)S(1)}, f32[8,128]{1,0:T(8,128)S(1)}, u32[]{:S(2)}, u32[]{:S(2)}) collective-permute-start(f32[8,128]{1,0:T(8,128)S(1)} %get-tuple-element.65.refs_0_), channel_id=1, source_target_pairs={{0,12},{4,8},{8,4},{12,0},{1,13},{5,9},{9,5},{13,1},{2,14},{6,10},... | collective-permute-start | bytes 12296 | tf_op jit(solution)/shard_map/ppermute | solution.py:354
  29.2 4.5 %collective-permute-start.11 = (f32[8,128]{1,0:T(8,128)S(1)}, f32[8,128]{1,0:T(8,128)S(1)}, u32[]{:S(2)}, u32[]{:S(2)}) collective-permute-start(f32[8,128]{1,0:T(8,128)S(1)} %get-tuple-element.65.refs_0_), channel_id=1, source_target_pairs={{0,8},{4,12},{8,0},{12,4},{1,9},{5,13},{9,1},{13,5},{2,10},{6,14},... | collective-permute-start | bytes 12296 | tf_op jit(solution)/shard_map/ppermute | solution.py:354
  29.9 3.8 %collective-permute-start.10 = (f32[8,128]{1,0:T(8,128)S(1)}, f32[8,128]{1,0:T(8,128)S(1)}, u32[]{:S(2)}, u32[]{:S(2)}) collective-permute-start(f32[8,128]{1,0:T(8,128)S(1)} %get-tuple-element.65.refs_0_), channel_id=1, source_target_pairs={{0,4},{4,0},{8,12},{12,8},{1,5},{5,1},{9,13},{13,9},{2,6},{6,2},{1... | collective-permute-start | bytes 12296 | tf_op jit(solution)/shard_map/ppermute | solution.py:354
  33.7 1.9 %collective-permute-start.13 = (f32[2,64,1024]{2,1,0:T(8,128)S(1)}, f32[2,64,1024]{2,1,0:T(8,128)S(1)}, u32[]{:S(2)}, u32[]{:S(2)}) collective-permute-start(f32[2,64,1024]{2,1,0:T(8,128)S(1)} %collective-permute-done.9.refs_0_), channel_id=1, source_target_pairs={{0,1},{1,0},{2,3},{3,2},{4,5},{5,4},{6,7},{7,6},{8,9},{9,8},{10,11... | collective-permute-start | bytes 1572872 | tf_op jit(solution)/shard_map/ppermute | solution.py:354
  33.7 7.0 %collective-permute-start.18 = (f32[72,128]{1,0:T(8,128)S(1)}, f32[72,128]{1,0:T(8,128)S(1)}, u32[]{:S(2)}, u32[]{:S(2)}) collective-permute-start(f32[72,128]{1,0:T(8,128)S(1)} %coeffs.1.refs_4_), channel_id=1, source_target_pairs={{0,2},{1,3},{2,0},{3,1},{4,6},{5,7},{6,4},{7,5},{8,10},{9,11},{10,... | collective-permute-start | bytes 110600 | tf_op jit(solution)/shard_map/ppermute | solution.py:354
  35.3 6.5 %collective-permute-start.17 = (f32[72,128]{1,0:T(8,128)S(1)}, f32[72,128]{1,0:T(8,128)S(1)}, u32[]{:S(2)}, u32[]{:S(2)}) collective-permute-start(f32[72,128]{1,0:T(8,128)S(1)} %coeffs.1.refs_4_), channel_id=1, source_target_pairs={{0,1},{1,0},{2,3},{3,2},{4,5},{5,4},{6,7},{7,6},{8,9},{9,8},{10,11... | collective-permute-start | bytes 110600 | tf_op jit(solution)/shard_map/ppermute | solution.py:354
  36.3 6.1 %collective-permute-start.14 = (f32[64,128]{1,0:T(8,128)S(1)}, f32[64,128]{1,0:T(8,128)S(1)}, u32[]{:S(2)}, u32[]{:S(2)}) collective-permute-start(f32[64,128]{1,0:T(8,128)S(1)} %get-tuple-element.73), channel_id=1, source_target_pairs={{0,12},{4,8},{8,4},{12,0},{1,13},{5,9},{9,5},{13,1},{2,14},{6,10},... | collective-permute-start | bytes 98312 | tf_op jit(solution)/shard_map/ppermute | solution.py:354
  37.9 4.9 %collective-permute-start.15 = (f32[64,128]{1,0:T(8,128)S(1)}, f32[64,128]{1,0:T(8,128)S(1)}, u32[]{:S(2)}, u32[]{:S(2)}) collective-permute-start(f32[64,128]{1,0:T(8,128)S(1)} %get-tuple-element.74), channel_id=1, source_target_pairs={{0,8},{4,12},{8,0},{12,4},{1,9},{5,13},{9,1},{13,5},{2,10},{6,14},... | collective-permute-start | bytes 98312 | tf_op jit(solution)/shard_map/ppermute | solution.py:354
  38.8 4.3 %collective-permute-start.16 = (f32[64,128]{1,0:T(8,128)S(1)}, f32[64,128]{1,0:T(8,128)S(1)}, u32[]{:S(2)}, u32[]{:S(2)}) collective-permute-start(f32[64,128]{1,0:T(8,128)S(1)} %get-tuple-element.75), channel_id=1, source_target_pairs={{0,4},{4,0},{8,12},{12,8},{1,5},{5,1},{9,13},{13,9},{2,6},{6,2},{1... | collective-permute-start | bytes 98312 | tf_op jit(solution)/shard_map/ppermute | solution.py:354
  40.7 1.2 %collective-permute-start.19 = (f32[8,128]{1,0:T(8,128)S(1)}, f32[8,128]{1,0:T(8,128)S(1)}, u32[]{:S(2)}, u32[]{:S(2)}) collective-permute-start(f32[8,128]{1,0:T(8,128)S(1)} %slice.8), channel_id=1, source_target_pairs={{0,1},{1,0},{2,3},{3,2},{4,5},{5,4},{6,7},{7,6},{8,9},{9,8},{10,11... | collective-permute-start | bytes 12296 | tf_op jit(solution)/shard_map/ppermute | solution.py:354

commit v8 on v7

--- a/solution.py
+++ b/solution.py
@@ -135,7 +135,8 @@
     result = result - up * ahead_row(here, after)
     result = result - down * behind_row(before, here)
     result = result - middle * load(other, k)
-    result = result - crossing * load(halo, k)
+    if halo is not None:
+        result = result - crossing * load(halo, k)
     return result.reshape(rows, LANES)
 
 
@@ -169,9 +170,13 @@
     return packed
 
 
-def other_kernel(forces_far, precond, forces, q, near, d_far, packed):
+def other_kernel(
+    forces_far, precond, forces, q, near, couplings, ground, before_a, before_b, w_a, w_b, d_far, local, packed
+):
     rows = forces.shape[0]
-    sums = [jnp.zeros((rows, LANES), F32) for _ in range(3)]
+    springs = all_springs(couplings, ground, (before_a, before_b))
+    fields = (w_a, w_b)
+    sums = [jnp.zeros((rows, LANES), F32) for _ in range(4)]
     for slot, plane in enumerate(slot_planes()):
         for k in range(CHUNKS):
             d_far[slot, :, chunk(k)] = block_product(
@@ -181,7 +186,11 @@
             q_here = q[slot, :, chunk(k)]
             sums[0] += forces[:, plane_chunk(plane, k)] * d_here
             sums[1] += d_here * q_here
-            sums[2] += q_here * near[slot, rows : 2 * rows, chunk(k)]
+            w_here = near[slot, rows : 2 * rows, chunk(k)]
+            sums[2] += q_here * w_here
+            image = stiff_chunk(springs[slot], k, fields[slot], fields[1 - slot], None, rows)
+            local[slot, :, chunk(k)] = image
+            sums[3] += w_here * image
     packed[...] = place_sums(jnp.zeros((rows, LANES), F32), 0, sums)
 
 
@@ -202,19 +211,17 @@
             near[slot, rows : 2 * rows, chunk(k)] = w
 
 
-def third_kernel(couplings, ground, before_a, before_b, w_a, w_b, next_a, next_b, packed, v, dots):
+def third_kernel(couplings, ground, before_a, before_b, w_a, w_b, next_a, next_b, local, packed, v, dots):
     rows = w_a.shape[0]
     springs = all_springs(couplings, ground, (before_a, before_b))
-    fields = (w_a, w_b)
-    total = jnp.zeros((rows, LANES), F32)
-    for slot in range(2):
+    total = jnp.zeros((rows // 8, 8, LANES), F32)
+    for slot, (here, halo) in enumerate(((w_a, next_a), (w_b, next_b))):
         for k in range(CHUNKS):
-            image = stiff_chunk(
-                springs[slot], k, fields[slot], fields[1 - slot], (next_a, next_b)[slot], rows
-            )
-            v[slot, :, chunk(k)] = image
-            total += fields[slot][:, chunk(k)] * image
-    values = place_sums(packed[...], 3, [total])
+            term = springs[slot][k][6] * halo[:, chunk(k)].reshape(rows // 8, 8, LANES)
+            v[slot, :, chunk(k)] = local[slot, :, chunk(k)] - term.reshape(rows, LANES)
+            total += here[:, chunk(k)].reshape(rows // 8, 8, LANES) * term
+    crossing = jnp.sum(total.reshape(rows, LANES), axis=1, keepdims=True)
+    values = packed[...] - jnp.where(lane_index(rows) == 3, crossing, 0.0)
     if rows < LANES:
         values = jnp.concatenate([values, jnp.zeros((LANES - rows, LANES), F32)], axis=0)
     dots[...] = values.T[0:8, :]
@@ -224,8 +231,9 @@
     return jnp.concatenate([field[slot] for field in fields], axis=0)
 
 
-def early_kernel(n_near, q, v, *refs):
-    near, (qv_high, qv_low, near_gram) = refs[:n_near], refs[n_near:]
+def early_kernel(n_near, q, v, d_far, *refs):
+    near, (qv_high, qv_low, near_gram, own_far) = refs[:n_near], refs[n_near:]
+    far_sum = None
     sums = [None] * n_near
     for slot in range(2):
         images = split(jnp.concatenate([q[slot], v[slot]], axis=0))
@@ -233,6 +241,9 @@
         for i in range(n_near):
             term = product(images, split(near[i][slot]), ((1,), (1,)))
             sums[i] = term if slot == 0 else sums[i] + term
+        term = product(images, split(d_far[slot]), ((1,), (1,)))
+        far_sum = term if slot == 0 else far_sum + term
+    own_far[...] = far_sum
     for i in range(n_near):
         near_gram[i] = sums[i]
 
@@ -266,7 +277,7 @@
         coeffs[8 * i : 8 * i + 8, :] = pair
 
 
-def late_kernel(n_near, n_far, exchange, coeffs, qv_high, qv_low, near_gram, far_gram, *refs):
+def late_kernel(n_near, n_far, exchange, coeffs, qv_high, qv_low, near_gram, own_far, far_gram, *refs):
     far, outs, gram = refs[:n_far], refs[n_far:-1], refs[-1]
     rows = near_gram.shape[1] // 2
     far_sum = None
@@ -279,10 +290,9 @@
         gram = outs[0]
     for i in range(n_near):
         gram[i] = p * near_gram[i, 0:rows] + s * near_gram[i, rows : 2 * rows]
-    d_part = far_gram[...]
+    d_part = [own_far[...]] + [far_gram[:, i * rows : (i + 1) * rows] for i in range(n_far - 1)]
     for i in range(n_far):
-        there = slice(i * rows, (i + 1) * rows)
-        both = jnp.concatenate([d_part[:, there], far_sum[:, there]], axis=1)
+        both = jnp.concatenate([d_part[i], far_sum[:, i * rows : (i + 1) * rows]], axis=1)
         gram[n_near + i] = p * both[0:rows] + s * both[rows : 2 * rows]
     if exchange:
         mine = lax.axis_index("nodes") ^ lax.axis_index("cols")
@@ -400,18 +410,18 @@
     next_a, next_b = neighbours(w_a, 1), neighbours(w_b, 0)
     far = swapped(w_both, "cols", top)
     near = shared(near)
-    d_far, packed = call(
+    d_far, local, packed = call(
         other_kernel,
         "other",
-        (forces_far, precond, forces, q, near[0]),
-        [(2,) + field, (rows, LANES)],
+        (forces_far, precond, forces, q, near[0], *edges, w_a, w_b),
+        [(2,) + field, (2,) + field, (rows, LANES)],
     )
     next_a, next_b, d_far, near = lax.optimization_barrier((next_a, next_b, d_far, near))
     d_far = shared(d_far)
     v, dots = call(
         third_kernel,
         "third",
-        (*edges, w_a, w_b, next_a, next_b, packed),
+        (*edges, w_a, w_b, next_a, next_b, local, packed),
         [(2,) + field, (8, LANES)],
     )
     exchange = nodes == cols
@@ -420,15 +430,15 @@
     else:
         dots = [lax.psum(dots, "nodes")]
     halves = jax.ShapeDtypeStruct((2, 2 * rows, PLANE), jnp.bfloat16)
-    qv_high, qv_low, near_gram = call(
+    qv_high, qv_low, near_gram, own_far = call(
         functools.partial(early_kernel, len(near)),
         "early",
-        (q, v, *near),
-        [halves, halves, (len(near), 2 * rows, 2 * rows)],
+        (q, v, d_far[0], *near),
+        [halves, halves, (len(near), 2 * rows, 2 * rows), (2 * rows, rows)],
     )
     d_far, far = lax.optimization_barrier((d_far, far))
     (far_gram,) = call(
-        far_kernel, "far", (qv_high, qv_low, *d_far), [(2 * rows, len(d_far) * rows)]
+        far_kernel, "far", (qv_high, qv_low, *d_far[1:]), [(2 * rows, (len(d_far) - 1) * rows)]
     )
     far, far_gram, *dots = lax.optimization_barrier((far, far_gram, *dots))
     far = shared(far)
@@ -436,7 +446,7 @@
     grams = call(
         functools.partial(late_kernel, len(near), len(d_far), exchange),
         "late",
-        (coeffs, qv_high, qv_low, near_gram, far_gram, *far),
+        (coeffs, qv_high, qv_low, near_gram, own_far, far_gram, *far),
         [(rows, LANES)] * cols if exchange else [(cols, rows, LANES)],
         [pltpu.VMEM((cols, rows, LANES), F32)],
     )

time: 43.9 us -> 43.8 us (level)
  transfers between devices with their start and end apart: 20 -> 20, of which waited for: 10 -> 8; matrix products, arithmetic and copies ran while one was open for 0% -> 0% of each run, Pallas kernels for 17% -> 18%
where the time goes in v8:
time: 43.8 us; the launch traced here: 43.7 us
  starting transfers between devices  21.9 us (50%)
  waiting for transfers between devices  12.5 us (29%)
  Pallas kernels  8.37 us (19%)
  between operations  0.81 us (2%)
    ppermute x14, starting transfers between devices, swapped(): lax.ppermute(block, axis, [(i, i ^ bit) for i in range(lax.axis_size(axis...  15.2 us
    ppermute x6, waiting for transfers between devices, neighbours(): return lax.ppermute(block, ('nodes', 'cols'), route)  9.89 us
    pallas_call x10, Pallas kernels, call(): pl.pallas_call(kernel, out_shape=shapes, in_specs=[pl.BlockSpec(memory_sp...  8.37 us
    ppermute x6, starting transfers between devices, neighbours(): return lax.ppermute(block, ('nodes', 'cols'), route)  6.75 us
    ppermute x14, waiting for transfers between devices, swapped(): lax.ppermute(block, axis, [(i, i ^ bit) for i in range(lax.axis_size(axis...  2.65 us
  transfers between devices with their start and end apart: 20, of which 8 were waited for; matrix products, arithmetic and copies ran while one was open for 0% of the time, Pallas kernels for 18%

profile of v8, /device:TPU:0, one launch (start us, length us, event | category | flops | bytes accessed | tf_op | source)
XLA Modules:
  0.0 43.7 jit_solution(14792519386443085813)
XLA Ops:
  0.6 3.0 %collective-permute-start.4 = (f32[64,2048]{1,0:T(8,128)}, f32[64,2048]{1,0:T(8,128)S(1)}, u32[]{:S(2)}, u32[]{:S(2)}) collective-permute-start(f32[64,2048]{1,0:T(8,128)} %forces.3), channel_id=1, source_target_pairs={{0,2},{1,3},{2,0},{3,1},{4,6},{5,7},{6,4},{7,5},{8,10},{9,11},{10,... | collective-permute-start | bytes 1572872 | tf_op jit(solution)/shard_map/ppermute | solution.py:364
  3.7 1.8 %first.1 = (f32[64,1024]{1,0:T(8,128)S(1)}, f32[64,1024]{1,0:T(8,128)S(1)}) custom-call(f32[64,2048]{1,0:T(8,128)} %forces.3, f32[16,128,128]{2,1,0:T(8,128)} %precond.5), custom_call_target="tpu_custom_call" | custom-call | tf_op jit(solution)/shard_map/first/pallas_call | solution.py:338
  5.6 3.1 %collective-permute-start.3 = (f32[64,1024]{1,0:T(8,128)S(1)}, f32[64,1024]{1,0:T(8,128)S(1)}, u32[]{:S(2)}, u32[]{:S(2)}) collective-permute-start(f32[64,1024]{1,0:T(8,128)S(1)} %get-tuple-element.41.d_b), channel_id=1, source_target_pairs={{0,4},{1,5},{2,6},{3,7},{4,0},{5,1},{6,2},{7,3},{8,12},{9,13},{10,... | collective-permute-start | bytes 786440 | tf_op jit(solution)/shard_map/ppermute | solution.py:360
  8.8 0.1 collective-permute-start.1
  8.8 0.1 collective-permute-start
  8.9 5.7 %collective-permute-done.1.before_b = f32[1,1024]{1,0:T(1,128)S(1)} collective-permute-done((f32[1,1024]{1,0:T(1,128)S(1)}, f32[1,1024]{1,0:T(1,128)S(1)}, u32[]{:S(2)}, u32[]{:S(2)}) %collective-permute-start.1) | collective-permute-done | bytes 4128 | tf_op jit(solution)/shard_map/ppermute | solution.py:360
  14.6 1.0 %second.1 = (f32[2,64,1024]{2,1,0:T(8,128)S(1)}, f32[64,1024]{1,0:T(8,128)S(1)}, f32[64,1024]{1,0:T(8,128)S(1)}, f32[2,64,1024]{2,1,0:T(8,128)S(1)}, f32[2,128,1024]{2,1,0:T(8,128)S(1)}) custom-call(f32[3,2048]{1,0:T(4,128)S(1)} %copy-done.2, f32[1,2048]{1,0:T(1,128)S(1)} %bitcast.1, f32[1,1024]{1,0:T(1,128)S(1)} %collective-permute-done.before_a, ...), custom_call_target="tpu_custom_call" | custom-call | tf_op jit(solution)/shard_map/second/pallas_call | solution.py:338
  15.6 0.2 collective-permute-done.4.forces_far
  15.8 0.5 %collective-permute-start.5 = (f32[64,1024]{1,0:T(8,128)S(1)}, f32[64,1024]{1,0:T(8,128)S(1)}, u32[]{:S(2)}, u32[]{:S(2)}) collective-permute-start(f32[64,1024]{1,0:T(8,128)S(1)} %get-tuple-element.46.w_a), channel_id=1, source_target_pairs={{0,1},{1,0},{2,3},{3,2},{4,8},{5,9},{6,10},{7,11},{8,4},{9,5},{10,... | collective-permute-start | bytes 786440 | tf_op jit(solution)/shard_map/ppermute | solution.py:360
  16.3 2.9 %collective-permute-start.6 = (f32[64,1024]{1,0:T(8,128)S(1)}, f32[64,1024]{1,0:T(8,128)S(1)}, u32[]{:S(2)}, u32[]{:S(2)}) collective-permute-start(f32[64,1024]{1,0:T(8,128)S(1)} %get-tuple-element.47.w_b), channel_id=1, source_target_pairs={{0,4},{1,5},{2,6},{3,7},{4,0},{5,1},{6,2},{7,3},{8,12},{9,13},{10,... | collective-permute-start | bytes 786440 | tf_op jit(solution)/shard_map/ppermute | solution.py:360
  19.2 1.5 %collective-permute-start.9 = (f32[2,64,1024]{2,1,0:T(8,128)S(1)}, f32[2,64,1024]{2,1,0:T(8,128)S(1)}, u32[]{:S(2)}, u32[]{:S(2)}) collective-permute-start(f32[2,64,1024]{2,1,0:T(8,128)S(1)} %get-tuple-element.53), channel_id=1, source_target_pairs={{0,2},{1,3},{2,0},{3,1},{4,6},{5,7},{6,4},{7,5},{8,10},{9,11},{10,... | collective-permute-start | bytes 1572872 | tf_op jit(solution)/shard_map/ppermute | solution.py:364
  20.7 1.0 %other.1 = (f32[2,64,1024]{2,1,0:T(8,128)S(1)}, f32[2,64,1024]{2,1,0:T(8,128)S(1)}, f32[64,128]{1,0:T(8,128)S(1)}) custom-call(f32[64,2048]{1,0:T(8,128)S(1)} %collective-permute-done.4.forces_far, f32[16,128,128]{2,1,0:T(8,128)S(1)} %copy-done, f32[64,2048]{1,0:T(8,128)S(1)} %copy-done.1, f32[2,64,1024]{2,1,0:T(8,128)S(1)} %get-tuple-element.49.q, ...), custom_call_target="tpu_custom_call" | custom-call | tf_op jit(solution)/shard_map/other/pallas_call | solution.py:338
  21.7 4.2 %collective-permute-done.6.next_b = f32[64,1024]{1,0:T(8,128)S(1)} collective-permute-done((f32[64,1024]{1,0:T(8,128)S(1)}, f32[64,1024]{1,0:T(8,128)S(1)}, u32[]{:S(2)}, u32[]{:S(2)}) %collective-permute-start.6) | collective-permute-done | bytes 262176 | tf_op jit(solution)/shard_map/ppermute | solution.py:360
  25.9 0.2 third.1
  26.1 2.5 %collective-permute-start.12 = (f32[8,128]{1,0:T(8,128)S(1)}, f32[8,128]{1,0:T(8,128)S(1)}, u32[]{:S(2)}, u32[]{:S(2)}) collective-permute-start(f32[8,128]{1,0:T(8,128)S(1)} %get-tuple-element.66.refs_0_), channel_id=1, source_target_pairs={{0,12},{4,8},{8,4},{12,0},{1,13},{5,9},{9,5},{13,1},{2,14},{6,10},... | collective-permute-start | bytes 12296 | tf_op jit(solution)/shard_map/ppermute | solution.py:364
  28.6 0.7 %collective-permute-start.11 = (f32[8,128]{1,0:T(8,128)S(1)}, f32[8,128]{1,0:T(8,128)S(1)}, u32[]{:S(2)}, u32[]{:S(2)}) collective-permute-start(f32[8,128]{1,0:T(8,128)S(1)} %get-tuple-element.66.refs_0_), channel_id=1, source_target_pairs={{0,8},{4,12},{8,0},{12,4},{1,9},{5,13},{9,1},{13,5},{2,10},{6,14},... | collective-permute-start | bytes 12296 | tf_op jit(solution)/shard_map/ppermute | solution.py:364
  29.3 1.2 %collective-permute-start.10 = (f32[8,128]{1,0:T(8,128)S(1)}, f32[8,128]{1,0:T(8,128)S(1)}, u32[]{:S(2)}, u32[]{:S(2)}) collective-permute-start(f32[8,128]{1,0:T(8,128)S(1)} %get-tuple-element.66.refs_0_), channel_id=1, source_target_pairs={{0,4},{4,0},{8,12},{12,8},{1,5},{5,1},{9,13},{13,9},{2,6},{6,2},{1... | collective-permute-start | bytes 12296 | tf_op jit(solution)/shard_map/ppermute | solution.py:364
  30.5 1.4 %early.1 = (bf16[2,128,1024]{2,1,0:T(8,128)(2,1)S(1)}, bf16[2,128,1024]{2,1,0:T(8,128)(2,1)S(1)}, f32[2,128,128]{2,1,0:T(8,128)S(1)}, f32[128,64]{1,0:T(8,128)S(1)}) custom-call(f32[2,64,1024]{2,1,0:T(8,128)S(1)} %get-tuple-element.49.q, f32[2,64,1024]{2,1,0:T(8,128)S(1)} %get-tuple-element.59.v, f32[2,64,1024]{2,1,0:T(8,128)S(1)} %get-tuple-element.52.d_far, ...), custom_call_target="tpu_custom_call" | custom-call | tf_op jit(solution)/shard_map/early/pallas_call | solution.py:338
  31.9 1.1 %collective-permute-done.9.refs_0_ = f32[2,64,1024]{2,1,0:T(8,128)S(1)} collective-permute-done((f32[2,64,1024]{2,1,0:T(8,128)S(1)}, f32[2,64,1024]{2,1,0:T(8,128)S(1)}, u32[]{:S(2)}, u32[]{:S(2)}) %collective-permute-start.9) | collective-permute-done | bytes 524320 | tf_op jit(solution)/shard_map/ppermute | solution.py:364
  33.0 0.6 %far.1.far_gram = f32[128,64]{1,0:T(8,128)S(1)} custom-call(bf16[2,128,1024]{2,1,0:T(8,128)(2,1)S(1)} %get-tuple-element.62.qv_high, bf16[2,128,1024]{2,1,0:T(8,128)(2,1)S(1)} %get-tuple-element.63.qv_low, f32[2,64,1024]{2,1,0:T(8,128)S(1)} %collective-permute-done.8.refs_0_), custom_call_target="tpu_custom_call" | custom-call | tf_op jit(solution)/shard_map/far/pallas_call | solution.py:338
  33.7 1.6 %collective-permute-start.18 = (f32[72,128]{1,0:T(8,128)S(1)}, f32[72,128]{1,0:T(8,128)S(1)}, u32[]{:S(2)}, u32[]{:S(2)}) collective-permute-start(f32[72,128]{1,0:T(8,128)S(1)} %coeffs.1.refs_4_), channel_id=1, source_target_pairs={{0,2},{1,3},{2,0},{3,1},{4,6},{5,7},{6,4},{7,5},{8,10},{9,11},{10,... | collective-permute-start | bytes 110600 | tf_op jit(solution)/shard_map/ppermute | solution.py:364
  35.2 0.2 collective-permute-start.17
  35.5 0.1 collective-permute-done.13.refs_1_
  35.5 0.7 %late.1 = (f32[64,128]{1,0:T(8,128)S(1)}, f32[64,128]{1,0:T(8,128)S(1)}, f32[64,128]{1,0:T(8,128)S(1)}, f32[64,128]{1,0:T(8,128)S(1)}) custom-call(f32[72,128]{1,0:T(8,128)S(1)} %coeffs.1.refs_4_, bf16[2,128,1024]{2,1,0:T(8,128)(2,1)S(1)} %get-tuple-element.62.qv_high, bf16[2,128,1024]{2,1,0:T(8,128)(2,1)S(1)} %get-tuple-element.63.qv_low, ...), custom_call_target="tpu_custom_call" | custom-call | tf_op jit(solution)/shard_map/late/pallas_call | solution.py:338
  36.2 1.5 %collective-permute-start.14 = (f32[64,128]{1,0:T(8,128)S(1)}, f32[64,128]{1,0:T(8,128)S(1)}, u32[]{:S(2)}, u32[]{:S(2)}) collective-permute-start(f32[64,128]{1,0:T(8,128)S(1)} %get-tuple-element.75), channel_id=1, source_target_pairs={{0,12},{4,8},{8,4},{12,0},{1,13},{5,9},{9,5},{13,1},{2,14},{6,10},... | collective-permute-start | bytes 98312 | tf_op jit(solution)/shard_map/ppermute | solution.py:364
  37.7 0.5 %collective-permute-start.15 = (f32[64,128]{1,0:T(8,128)S(1)}, f32[64,128]{1,0:T(8,128)S(1)}, u32[]{:S(2)}, u32[]{:S(2)}) collective-permute-start(f32[64,128]{1,0:T(8,128)S(1)} %get-tuple-element.76), channel_id=1, source_target_pairs={{0,8},{4,12},{8,0},{12,4},{1,9},{5,13},{9,1},{13,5},{2,10},{6,14},... | collective-permute-start | bytes 98312 | tf_op jit(solution)/shard_map/ppermute | solution.py:364
  38.2 2.4 %collective-permute-start.16 = (f32[64,128]{1,0:T(8,128)S(1)}, f32[64,128]{1,0:T(8,128)S(1)}, u32[]{:S(2)}, u32[]{:S(2)}) collective-permute-start(f32[64,128]{1,0:T(8,128)S(1)} %get-tuple-element.77), channel_id=1, source_target_pairs={{0,4},{4,0},{8,12},{12,8},{1,5},{5,1},{9,13},{13,9},{2,6},{6,2},{1... | collective-permute-start | bytes 98312 | tf_op jit(solution)/shard_map/ppermute | solution.py:364
  40.7 1.0 %modes.1 = f32[64,2048]{1,0:T(8,128)} custom-call(f32[72,128]{1,0:T(8,128)S(1)} %coeffs.1.refs_4_, f32[2,128,1024]{2,1,0:T(8,128)S(1)} %get-tuple-element.60.near.refs_0_), custom_call_target="tpu_custom_call" | custom-call | tf_op jit(solution)/shard_map/modes/pallas_call | solution.py:338
  41.7 0.1 collective-permute-done.19.refs_7_
  41.9 0.2 collective-permute-done.14.refs_1_
  42.0 1.0 %collective-permute-done.15.refs_2_ = f32[64,128]{1,0:T(8,128)S(1)} collective-permute-done((f32[64,128]{1,0:T(8,128)S(1)}, f32[64,128]{1,0:T(8,128)S(1)}, u32[]{:S(2)}, u32[]{:S(2)}) %collective-permute-start.15) | collective-permute-done | bytes 32800 | tf_op jit(solution)/shard_map/ppermute | solution.py:364
  43.0 0.7 %fifth.1 = f32[64,64]{1,0:T(8,128)} custom-call(f32[64,128]{1,0:T(8,128)S(1)} %get-tuple-element.74.refs_0_, f32[64,128]{1,0:T(8,128)S(1)} %collective-permute-done.14.refs_1_, f32[64,128]{1,0:T(8,128)S(1)} %collective-permute-done.15.refs_2_, f32[64,128]{1,0:T(8,128)S(1)} %collective-permute-done.16.refs_3_, f32[72,128]{1,0:T(8,128)S(1)} %coeffs.1.refs_4_, ...), custom_call_target="tpu_custom_call" | custom-call | tf_op jit(solution)/shard_map/fifth/pallas_call | solution.py:338
  (28 shorter events, 0.2 us)
Async XLA Ops:
  0.6 14.0 %copy-start = (f32[16,128,128]{2,1,0:T(8,128)S(1)}, f32[16,128,128]{2,1,0:T(8,128)}, u32[]{:S(2)}) copy-start(f32[16,128,128]{2,1,0:T(8,128)} %precond.5) | copy-start | bytes 3145732
  0.6 8.1 %copy-start.2 = (f32[3,2048]{1,0:T(4,128)S(1)}, f32[3,2048]{1,0:T(4,128)}, u32[]{:S(2)}) copy-start(f32[3,2048]{1,0:T(4,128)} %couplings.5) | copy-start | bytes 73732
  0.6 15.1 %collective-permute-start.4 = (f32[64,2048]{1,0:T(8,128)}, f32[64,2048]{1,0:T(8,128)S(1)}, u32[]{:S(2)}, u32[]{:S(2)}) collective-permute-start(f32[64,2048]{1,0:T(8,128)} %forces.3), channel_id=1, source_target_pairs={{0,2},{1,3},{2,0},{3,1},{4,6},{5,7},{6,4},{7,5},{8,10},{9,11},{10,... | collective-permute-start | bytes 1572872 | tf_op jit(solution)/shard_map/ppermute | solution.py:364
  5.5 9.1 %copy-start.3 = (f32[2048]{0:T(1024)S(1)}, f32[2048]{0:T(1024)}, u32[]{:S(2)}) copy-start(f32[2048]{0:T(1024)} %param.6) | copy-start | bytes 24580
  5.5 9.1 %collective-permute-start.2 = (f32[64,1024]{1,0:T(8,128)S(1)}, f32[64,1024]{1,0:T(8,128)S(1)}, u32[]{:S(2)}, u32[]{:S(2)}) collective-permute-start(f32[64,1024]{1,0:T(8,128)S(1)} %get-tuple-element.40.d_a), channel_id=1, source_target_pairs={{0,1},{1,0},{2,3},{3,2},{4,8},{5,9},{6,10},{7,11},{8,4},{9,5},{10,... | collective-permute-start | bytes 786440 | tf_op jit(solution)/shard_map/ppermute | solution.py:360
  5.6 9.0 %collective-permute-start.3 = (f32[64,1024]{1,0:T(8,128)S(1)}, f32[64,1024]{1,0:T(8,128)S(1)}, u32[]{:S(2)}, u32[]{:S(2)}) collective-permute-start(f32[64,1024]{1,0:T(8,128)S(1)} %get-tuple-element.41.d_b), channel_id=1, source_target_pairs={{0,4},{1,5},{2,6},{3,7},{4,0},{5,1},{6,2},{7,3},{8,12},{9,13},{10,... | collective-permute-start | bytes 786440 | tf_op jit(solution)/shard_map/ppermute | solution.py:360
  8.8 5.8 %collective-permute-start.1 = (f32[1,1024]{1,0:T(1,128)S(1)}, f32[1,1024]{1,0:T(1,128)S(1)}, u32[]{:S(2)}, u32[]{:S(2)}) collective-permute-start(f32[1,1024]{1,0:T(1,128)S(1)} %slice.6), channel_id=1, source_target_pairs={{0,4},{1,5},{2,6},{3,7},{4,0},{5,1},{6,2},{7,3},{8,12},{9,13},{10,... | collective-permute-start | bytes 12296 | tf_op jit(solution)/shard_map/ppermute | solution.py:360
  8.8 5.7 %collective-permute-start = (f32[1,1024]{1,0:T(1,128)S(1)}, f32[1,1024]{1,0:T(1,128)S(1)}, u32[]{:S(2)}, u32[]{:S(2)}) collective-permute-start(f32[1,1024]{1,0:T(1,128)S(1)} %slice.6), channel_id=1, source_target_pairs={{0,1},{1,0},{2,3},{3,2},{4,8},{5,9},{6,10},{7,11},{8,4},{9,5},{10,... | collective-permute-start | bytes 12296 | tf_op jit(solution)/shard_map/ppermute | solution.py:360
  14.6 6.1 %copy-start.1 = (f32[64,2048]{1,0:T(8,128)S(1)}, f32[64,2048]{1,0:T(8,128)}, u32[]{:S(2)}) copy-start(f32[64,2048]{1,0:T(8,128)} %forces.3) | copy-start | bytes 1572868
  15.8 10.1 %collective-permute-start.7 = (f32[2,128,1024]{2,1,0:T(8,128)S(1)}, f32[2,128,1024]{2,1,0:T(8,128)S(1)}, u32[]{:S(2)}, u32[]{:S(2)}) collective-permute-start(f32[2,128,1024]{2,1,0:T(8,128)S(1)} %get-tuple-element.60.near.refs_0_), channel_id=1, source_target_pairs={{0,1},{1,0},{2,3},{3,2},{4,5},{5,4},{6,7},{7,6},{8,9},{9,8},{10,11... | collective-permute-start | bytes 3145736 | tf_op jit(solution)/shard_map/ppermute | solution.py:364
  15.8 5.9 %collective-permute-start.5 = (f32[64,1024]{1,0:T(8,128)S(1)}, f32[64,1024]{1,0:T(8,128)S(1)}, u32[]{:S(2)}, u32[]{:S(2)}) collective-permute-start(f32[64,1024]{1,0:T(8,128)S(1)} %get-tuple-element.46.w_a), channel_id=1, source_target_pairs={{0,1},{1,0},{2,3},{3,2},{4,8},{5,9},{6,10},{7,11},{8,4},{9,5},{10,... | collective-permute-start | bytes 786440 | tf_op jit(solution)/shard_map/ppermute | solution.py:360
  16.3 9.6 %collective-permute-start.6 = (f32[64,1024]{1,0:T(8,128)S(1)}, f32[64,1024]{1,0:T(8,128)S(1)}, u32[]{:S(2)}, u32[]{:S(2)}) collective-permute-start(f32[64,1024]{1,0:T(8,128)S(1)} %get-tuple-element.47.w_b), channel_id=1, source_target_pairs={{0,4},{1,5},{2,6},{3,7},{4,0},{5,1},{6,2},{7,3},{8,12},{9,13},{10,... | collective-permute-start | bytes 786440 | tf_op jit(solution)/shard_map/ppermute | solution.py:360
  19.2 13.8 %collective-permute-start.9 = (f32[2,64,1024]{2,1,0:T(8,128)S(1)}, f32[2,64,1024]{2,1,0:T(8,128)S(1)}, u32[]{:S(2)}, u32[]{:S(2)}) collective-permute-start(f32[2,64,1024]{2,1,0:T(8,128)S(1)} %get-tuple-element.53), channel_id=1, source_target_pairs={{0,2},{1,3},{2,0},{3,1},{4,6},{5,7},{6,4},{7,5},{8,10},{9,11},{10,... | collective-permute-start | bytes 1572872 | tf_op jit(solution)/shard_map/ppermute | solution.py:364
  25.9 7.1 %collective-permute-start.8 = (f32[2,64,1024]{2,1,0:T(8,128)S(1)}, f32[2,64,1024]{2,1,0:T(8,128)S(1)}, u32[]{:S(2)}, u32[]{:S(2)}) collective-permute-start(f32[2,64,1024]{2,1,0:T(8,128)S(1)} %get-tuple-element.52.d_far), channel_id=1, source_target_pairs={{0,1},{1,0},{2,3},{3,2},{4,5},{5,4},{6,7},{7,6},{8,9},{9,8},{10,11... | collective-permute-start | bytes 1572872 | tf_op jit(solution)/shard_map/ppermute | solution.py:364
  26.1 7.4 %collective-permute-start.12 = (f32[8,128]{1,0:T(8,128)S(1)}, f32[8,128]{1,0:T(8,128)S(1)}, u32[]{:S(2)}, u32[]{:S(2)}) collective-permute-start(f32[8,128]{1,0:T(8,128)S(1)} %get-tuple-element.66.refs_0_), channel_id=1, source_target_pairs={{0,12},{4,8},{8,4},{12,0},{1,13},{5,9},{9,5},{13,1},{2,14},{6,10},... | collective-permute-start | bytes 12296 | tf_op jit(solution)/shard_map/ppermute | solution.py:364
  28.6 4.9 %collective-permute-start.11 = (f32[8,128]{1,0:T(8,128)S(1)}, f32[8,128]{1,0:T(8,128)S(1)}, u32[]{:S(2)}, u32[]{:S(2)}) collective-permute-start(f32[8,128]{1,0:T(8,128)S(1)} %get-tuple-element.66.refs_0_), channel_id=1, source_target_pairs={{0,8},{4,12},{8,0},{12,4},{1,9},{5,13},{9,1},{13,5},{2,10},{6,14},... | collective-permute-start | bytes 12296 | tf_op jit(solution)/shard_map/ppermute | solution.py:364
  29.3 4.2 %collective-permute-start.10 = (f32[8,128]{1,0:T(8,128)S(1)}, f32[8,128]{1,0:T(8,128)S(1)}, u32[]{:S(2)}, u32[]{:S(2)}) collective-permute-start(f32[8,128]{1,0:T(8,128)S(1)} %get-tuple-element.66.refs_0_), channel_id=1, source_target_pairs={{0,4},{4,0},{8,12},{12,8},{1,5},{5,1},{9,13},{13,9},{2,6},{6,2},{1... | collective-permute-start | bytes 12296 | tf_op jit(solution)/shard_map/ppermute | solution.py:364
  33.6 2.0 %collective-permute-start.13 = (f32[2,64,1024]{2,1,0:T(8,128)S(1)}, f32[2,64,1024]{2,1,0:T(8,128)S(1)}, u32[]{:S(2)}, u32[]{:S(2)}) collective-permute-start(f32[2,64,1024]{2,1,0:T(8,128)S(1)} %collective-permute-done.9.refs_0_), channel_id=1, source_target_pairs={{0,1},{1,0},{2,3},{3,2},{4,5},{5,4},{6,7},{7,6},{8,9},{9,8},{10,11... | collective-permute-start | bytes 1572872 | tf_op jit(solution)/shard_map/ppermute | solution.py:364
  33.7 7.0 %collective-permute-start.18 = (f32[72,128]{1,0:T(8,128)S(1)}, f32[72,128]{1,0:T(8,128)S(1)}, u32[]{:S(2)}, u32[]{:S(2)}) collective-permute-start(f32[72,128]{1,0:T(8,128)S(1)} %coeffs.1.refs_4_), channel_id=1, source_target_pairs={{0,2},{1,3},{2,0},{3,1},{4,6},{5,7},{6,4},{7,5},{8,10},{9,11},{10,... | collective-permute-start | bytes 110600 | tf_op jit(solution)/shard_map/ppermute | solution.py:364
  35.2 6.5 %collective-permute-start.17 = (f32[72,128]{1,0:T(8,128)S(1)}, f32[72,128]{1,0:T(8,128)S(1)}, u32[]{:S(2)}, u32[]{:S(2)}) collective-permute-start(f32[72,128]{1,0:T(8,128)S(1)} %coeffs.1.refs_4_), channel_id=1, source_target_pairs={{0,1},{1,0},{2,3},{3,2},{4,5},{5,4},{6,7},{7,6},{8,9},{9,8},{10,11... | collective-permute-start | bytes 110600 | tf_op jit(solution)/shard_map/ppermute | solution.py:364
  36.2 5.8 %collective-permute-start.14 = (f32[64,128]{1,0:T(8,128)S(1)}, f32[64,128]{1,0:T(8,128)S(1)}, u32[]{:S(2)}, u32[]{:S(2)}) collective-permute-start(f32[64,128]{1,0:T(8,128)S(1)} %get-tuple-element.75), channel_id=1, source_target_pairs={{0,12},{4,8},{8,4},{12,0},{1,13},{5,9},{9,5},{13,1},{2,14},{6,10},... | collective-permute-start | bytes 98312 | tf_op jit(solution)/shard_map/ppermute | solution.py:364
  37.7 5.3 %collective-permute-start.15 = (f32[64,128]{1,0:T(8,128)S(1)}, f32[64,128]{1,0:T(8,128)S(1)}, u32[]{:S(2)}, u32[]{:S(2)}) collective-permute-start(f32[64,128]{1,0:T(8,128)S(1)} %get-tuple-element.76), channel_id=1, source_target_pairs={{0,8},{4,12},{8,0},{12,4},{1,9},{5,13},{9,1},{13,5},{2,10},{6,14},... | collective-permute-start | bytes 98312 | tf_op jit(solution)/shard_map/ppermute | solution.py:364
  38.2 4.7 %collective-permute-start.16 = (f32[64,128]{1,0:T(8,128)S(1)}, f32[64,128]{1,0:T(8,128)S(1)}, u32[]{:S(2)}, u32[]{:S(2)}) collective-permute-start(f32[64,128]{1,0:T(8,128)S(1)} %get-tuple-element.77), channel_id=1, source_target_pairs={{0,4},{4,0},{8,12},{12,8},{1,5},{5,1},{9,13},{13,9},{2,6},{6,2},{1... | collective-permute-start | bytes 98312 | tf_op jit(solution)/shard_map/ppermute | solution.py:364
  40.7 1.2 %collective-permute-start.19 = (f32[8,128]{1,0:T(8,128)S(1)}, f32[8,128]{1,0:T(8,128)S(1)}, u32[]{:S(2)}, u32[]{:S(2)}) collective-permute-start(f32[8,128]{1,0:T(8,128)S(1)} %slice.8), channel_id=1, source_target_pairs={{0,1},{1,0},{2,3},{3,2},{4,5},{5,4},{6,7},{7,6},{8,9},{9,8},{10,11... | collective-permute-start | bytes 12296 | tf_op jit(solution)/shard_map/ppermute | solution.py:364
